TPU v7x, 32 devices: a whole 2x2x4 slice. The times are simulated.
32 devices in a mesh: dp: 4 (over x, core), expert: 8 (over z, y).
Axes of the slice: x: 2, y: 2, z: 4, core: 2. Of those that a mesh axis runs over, the one named last changes fastest.
Arguments:
- tokens: bfloat16 [512, 4096], P(('dp', 'expert')), may hold values from -6 to 6
- routes: int32 [512, 8], P(('dp', 'expert')), may hold values from 0 to 15, all different within a row; in each aligned block of 16 rows (0 to 15, 16 to 31, ...) at most 16 rows name the same one
- route_gates: float32 [512, 8], P(('dp', 'expert')), may hold values from 0.02 to 0.5
- placement: int32 [16], replicated, may hold values from 0 to 15, each once
- swap_flags: int32 [16], replicated, may hold values from 0 to 1, as said below
- gate_weight: bfloat16 [8, 4096, 1536], P('expert', None, 'dp'), may hold values from -0.09375 to 0.09375
- up_weight: bfloat16 [8, 4096, 1536], P('expert', None, 'dp'), may hold values from -0.09375 to 0.09375
- down_weight: bfloat16 [8, 1536, 4096], P('expert', 'dp'), may hold values from -0.21875 to 0.21875
Outputs:
- layer_out: bfloat16 [512, 4096], P(('dp', 'expert'))
Inputs may be any that keep to these rules, and one draw needn't show every extreme that they name: `routes`: each row names 8 different experts; among the 16 rows of one device no expert is named more than 16 times, a bound that some block reaches. `placement`: A permutation of the 16 positions. swap_flags[P] equals swap_flags[(P + 8) mod 16].
All inputs are finite; a program needn't handle non-finite values.
Results may differ from a plain program's by a relative error of at most 0.0065.
Values may be sent and summed in bfloat16 or wider, within the bound.
No kernel may reach another device: no remote copies, remote signals or barrier semaphores. Data moves between devices by JAX's collectives and lax.ppermute only.
A program may use at most 128 MiB of HBM per device.

v0:
```python
import jax
import jax.numpy as jnp
from jax import lax
from jax.sharding import PartitionSpec as P


def passed_along(value, axis, by):
    peers = lax.axis_size(axis)
    return lax.ppermute(value, axis, [(i, (i + by) % peers) for i in range(peers)])


def expert_block(received, w_gate, w_up, w_down):
    gate_act = jnp.dot(received, w_gate, preferred_element_type=jnp.float32)
    up_act = jnp.dot(received, w_up, preferred_element_type=jnp.float32)
    hidden = (jax.nn.silu(gate_act) * up_act).astype(jnp.bfloat16)
    return jnp.dot(hidden, w_down, preferred_element_type=jnp.float32).astype(jnp.bfloat16)


def on_device(
    tokens, routes, route_gates, placement, swap_flags, gate_weight, up_weight, down_weight
):
    tok_dev = tokens.shape[0]
    features = tokens.shape[1]
    route_count = routes.shape[1]
    columns = lax.axis_size("expert")
    replicas = lax.axis_size("dp")
    slot_count = replicas // 2
    experts = slot_count * columns
    capacity = 2 * tok_dev * route_count // experts
    lane_count = slot_count * columns * capacity
    expert_ids = jnp.arange(experts, dtype=jnp.int32)
    flat_routes = routes.reshape(-1)
    matches = (flat_routes[:, None] == expert_ids[None, :]).astype(jnp.int32)
    target = jnp.sum(matches * placement[None, :], axis=1)
    ranking = jnp.sum(matches * (jnp.cumsum(matches, axis=0) - 1), axis=1)
    w_gate = gate_weight[0]
    w_up = up_weight[0]
    w_down = down_weight[0]
    partner_blocks = passed_along((w_gate, w_up, w_down), "expert", columns // 2)
    own_position = lax.axis_index("expert") * slot_count + lax.axis_index("dp") // 2
    own_flag = jnp.sum(jnp.where(expert_ids == own_position, swap_flags, 0))
    unswapped = own_flag == 0
    w_gate = jnp.where(unswapped, w_gate, partner_blocks[0])
    w_up = jnp.where(unswapped, w_up, partner_blocks[1])
    w_down = jnp.where(unswapped, w_down, partner_blocks[2])
    column = target // slot_count
    slot_id = target % slot_count
    lane_index = (slot_id * columns + column) * capacity + ranking
    pair_row = jnp.arange(tok_dev * route_count, dtype=jnp.int32) // route_count
    lane_hit = (jnp.arange(lane_count, dtype=jnp.int32)[:, None] == lane_index[None, :]).astype(
        jnp.float32
    )
    row_hit = (jnp.arange(tok_dev, dtype=jnp.int32)[:, None] == pair_row[None, :]).astype(
        jnp.float32
    )
    selector = jnp.dot(lane_hit, row_hit.T, precision=lax.Precision.HIGHEST).astype(jnp.bfloat16)
    combine = jnp.dot(
        row_hit * route_gates.reshape(-1)[None, :], lane_hit.T, precision=lax.Precision.HIGHEST
    )
    outgoing = jnp.dot(selector, tokens, preferred_element_type=jnp.float32).astype(jnp.bfloat16)
    outgoing = outgoing.reshape(slot_count, columns, capacity, features)
    doubled = jnp.repeat(outgoing, 2, axis=0)
    arrived = lax.all_to_all(
        lax.all_to_all(doubled, "dp", split_axis=0, concat_axis=0, tiled=True),
        "expert",
        split_axis=1,
        concat_axis=1,
        tiled=True,
    )
    partial_value = expert_block(arrived.reshape(-1, features), w_gate, w_up, w_down)
    partial_value = partial_value.reshape(replicas, columns, capacity, features)
    returned = lax.all_to_all(
        lax.all_to_all(partial_value, "dp", split_axis=0, concat_axis=0, tiled=True),
        "expert",
        split_axis=1,
        concat_axis=1,
        tiled=True,
    )
    halves = returned.reshape(slot_count, 2, columns, capacity, features)
    summed = (halves[:, 0].astype(jnp.float32) + halves[:, 1].astype(jnp.float32)).astype(
        jnp.bfloat16
    )
    expert_rows = summed.reshape(lane_count, features)
    layer_out = jnp.dot(combine, expert_rows.astype(jnp.float32), precision=lax.Precision.HIGHEST)
    return layer_out.astype(jnp.bfloat16)


def solution(mesh):
    return jax.shard_map(
        on_device,
        mesh=mesh,
        in_specs=(
            P(("dp", "expert"), None),
            P(("dp", "expert"), None),
            P(("dp", "expert"), None),
            P(),
            P(),
            P("expert", None, "dp"),
            P("expert", None, "dp"),
            P("expert", "dp", None),
        ),
        out_specs=P(("dp", "expert"), None),
        check_vma=False,
    )
```

profile of v0, /device:TPU:0, one launch (start us, length us, event | category | flops | bytes accessed | tf_op | source)
XLA Modules:
  0.0 720.5 jit_solution(12465381971978215713)
XLA Ops:
  0.0 0.0 copy-start
  0.0 0.8 copy.29
  0.8 0.1 eq.62
  0.9 0.1 fusion.12
  1.0 0.2 reduce_window_sum.11
  1.2 0.8 select_reduce_fusion.1
  2.0 0.1 convolution_convert_fusion.3
  2.2 0.0 copy-done
  2.2 0.7 convolution_convert_fusion.1
  2.9 0.5 broadcast_in_dim.6
  3.4 52.2 %all_to_all.20 = bf16[4,8,16,4096]{3,2,1,0:T(8,128)(2,1)S(1)} all-to-all(bf16[4,8,16,4096]{3,2,1,0:T(8,128)(2,1)S(1)} %bitcast.27), channel_id=1, replica_groups=mesh['dp'=4,'expert'=8] {'dp'}, dimensions={0} | all-to-all | bytes 8388608 | tf_op jit(solution)/shard_map/all_to_all | solution.py:64
  55.6 2.2 copy.30
  57.8 0.0 copy-start.2
  57.8 0.0 copy-start.5
  57.8 6.1 all-to-all-start.1
  63.9 0.0 copy-done.2
  64.0 2.9 collective-permute-start.1
  66.9 0.1 collective-permute-start
  66.9 2.9 collective-permute-start.2
  69.8 0.0 copy-done.5
  69.8 0.6 fusion.20
  71.1 289.8 %all-to-all-done.1 = bf16[4,8,16,4096]{3,2,0,1:T(8,128)(2,1)} async-done(((bf16[4,8,16,4096]{3,2,0,1:T(8,128)(2,1)}), bf16[4,8,16,4096]{3,2,0,1:T(8,128)(2,1)}, u32[]{:S(2)}, u32[]{:S(2)}) %all-to-all-start.1) | async-done | bytes 4194336 | tf_op jit(solution)/shard_map/all_to_all | solution.py:63
  360.9 2.5 copy.31
  363.4 65.0 %collective-permute-done.1 = bf16[4096,384]{1,0:T(8,128)(2,1)} collective-permute-done((bf16[4096,384]{1,0:T(8,128)(2,1)S(1)}, bf16[4096,384]{1,0:T(8,128)(2,1)}, u32[]{:S(2)}, u32[]{:S(2)}) %collective-permute-start.1) | collective-permute-done | bytes 3145760 | tf_op jit(solution)/shard_map/ppermute | solution.py:9
  428.3 0.0 copy-start.3
  428.3 2.4 fusion.1
  430.7 0.0 copy-start.4
  430.7 65.0 %collective-permute-done = bf16[4096,384]{1,0:T(8,128)(2,1)} collective-permute-done((bf16[4096,384]{1,0:T(8,128)(2,1)}, bf16[4096,384]{1,0:T(8,128)(2,1)}, u32[]{:S(2)}, u32[]{:S(2)}) %collective-permute-start) | collective-permute-done | bytes 3145760 | tf_op jit(solution)/shard_map/ppermute | solution.py:9
  495.7 0.0 copy-done.3
  495.7 2.4 fusion.3
  498.1 63.2 %collective-permute-done.2 = bf16[384,4096]{1,0:T(8,128)(2,1)} collective-permute-done((bf16[384,4096]{1,0:T(8,128)(2,1)}, bf16[384,4096]{1,0:T(8,128)(2,1)}, u32[]{:S(2)}, u32[]{:S(2)}) %collective-permute-start.2) | collective-permute-done | bytes 3145760 | tf_op jit(solution)/shard_map/ppermute | solution.py:9
  561.3 0.0 copy-done.4
  561.3 2.4 convolution_convert_fusion
  563.7 51.9 %all_to_all.21 = bf16[4,8,16,4096]{3,2,1,0:T(8,128)(2,1)S(1)} all-to-all(bf16[4,8,16,4096]{3,2,1,0:T(8,128)(2,1)S(1)} %bitcast.33), channel_id=1, replica_groups=mesh['dp'=4,'expert'=8] {'dp'}, dimensions={0} | all-to-all | bytes 8388608 | tf_op jit(solution)/shard_map/all_to_all | solution.py:73
  615.6 2.2 copy.32
  617.9 0.0 copy-start.1
  617.9 4.7 all-to-all-start.3
  622.6 0.0 copy-done.1
  622.6 0.1 copy.28
  622.6 0.1 mul.49
  622.7 0.1 fusion.9
  622.9 92.8 %all-to-all-done.3 = bf16[4,8,16,4096]{3,2,0,1:T(8,128)(2,1)} async-done(((bf16[4,8,16,4096]{3,2,0,1:T(8,128)(2,1)}), bf16[4,8,16,4096]{3,2,0,1:T(8,128)(2,1)}, u32[]{:S(2)}, u32[]{:S(2)}) %all-to-all-start.3) | async-done | bytes 4194336 | tf_op jit(solution)/shard_map/all_to_all | solution.py:72
  715.7 2.5 copy.33
  718.1 0.8 add_convert_fusion
  718.9 1.6 convolution_convert_fusion.2
  (1 shorter events, 0.0 us)
Async XLA Ops:
  0.0 2.2 copy-start
  57.8 6.1 copy-start.2
  57.8 12.0 %copy-start.5 = (s32[16]{0:T(128)S(1)}, s32[16]{0:T(128)}, u32[]{:S(2)}) copy-start(s32[16]{0:T(128)} %param.12) | copy-start | bytes 196
  57.8 303.1 %all-to-all-start.1 = ((bf16[4,8,16,4096]{3,2,0,1:T(8,128)(2,1)}), bf16[4,8,16,4096]{3,2,0,1:T(8,128)(2,1)}, u32[]{:S(2)}, u32[]{:S(2)}) async-start(bf16[4,8,16,4096]{3,2,0,1:T(8,128)(2,1)} %copy.30), calls=%async_computation.1 | async-start | bytes 8388608 | tf_op jit(solution)/shard_map/all_to_all | solution.py:63
  64.0 364.4 %collective-permute-start.1 = (bf16[4096,384]{1,0:T(8,128)(2,1)S(1)}, bf16[4096,384]{1,0:T(8,128)(2,1)}, u32[]{:S(2)}, u32[]{:S(2)}) collective-permute-start(bf16[4096,384]{1,0:T(8,128)(2,1)S(1)} %bitcast.34), channel_id=1, source_target_pairs={{0,4},{1,5},{2,6},{3,7},{4,0},{5,1},{6,2},{7,3},{8,12},{9,13},{10,... | collective-permute-start | bytes 9437192 | tf_op jit(solution)/shard_map/ppermute | solution.py:9
  66.9 428.9 %collective-permute-start = (bf16[4096,384]{1,0:T(8,128)(2,1)}, bf16[4096,384]{1,0:T(8,128)(2,1)}, u32[]{:S(2)}, u32[]{:S(2)}) collective-permute-start(bf16[4096,384]{1,0:T(8,128)(2,1)} %bitcast.35), channel_id=1, source_target_pairs={{0,4},{1,5},{2,6},{3,7},{4,0},{5,1},{6,2},{7,3},{8,12},{9,13},{10,... | collective-permute-start | bytes 9437192 | tf_op jit(solution)/shard_map/ppermute | solution.py:9
  66.9 494.4 %collective-permute-start.2 = (bf16[384,4096]{1,0:T(8,128)(2,1)}, bf16[384,4096]{1,0:T(8,128)(2,1)}, u32[]{:S(2)}, u32[]{:S(2)}) collective-permute-start(bf16[384,4096]{1,0:T(8,128)(2,1)} %bitcast.36), channel_id=1, source_target_pairs={{0,4},{1,5},{2,6},{3,7},{4,0},{5,1},{6,2},{7,3},{8,12},{9,13},{10,... | collective-permute-start | bytes 9437192 | tf_op jit(solution)/shard_map/ppermute | solution.py:9
  428.3 67.4 %copy-start.3 = (bf16[1,4096,384]{2,1,0:T(8,128)(2,1)S(1)}, bf16[1,4096,384]{2,1,0:T(8,128)(2,1)}, u32[]{:S(2)}) copy-start(bf16[1,4096,384]{2,1,0:T(8,128)(2,1)} %param.13) | copy-start | bytes 9437188
  430.7 130.6 %copy-start.4 = (bf16[1,384,4096]{2,1,0:T(8,128)(2,1)S(1)}, bf16[1,384,4096]{2,1,0:T(8,128)(2,1)}, u32[]{:S(2)}) copy-start(bf16[1,384,4096]{2,1,0:T(8,128)(2,1)} %param.15) | copy-start | bytes 9437188
  617.9 4.7 copy-start.1
  617.9 97.8 %all-to-all-start.3 = ((bf16[4,8,16,4096]{3,2,0,1:T(8,128)(2,1)}), bf16[4,8,16,4096]{3,2,0,1:T(8,128)(2,1)}, u32[]{:S(2)}, u32[]{:S(2)}) async-start(bf16[4,8,16,4096]{3,2,0,1:T(8,128)(2,1)} %copy.32), calls=%async_computation.3 | async-start | bytes 8388608 | tf_op jit(solution)/shard_map/all_to_all | solution.py:72
where the time goes:
time: 721 us; the launch traced here: 720 us
  waiting for transfers between devices  576 us (80%)
  blocking collectives  104 us (14%)
  starting transfers between devices  16.6 us (2%)
  local copies, waits for them, and re-layouts  11 us (2%)
  matrix products  9.8 us (1%)
    all_to_all x1, waiting for transfers between devices, on_device(): lax.all_to_all(lax.all_to_all(doubled, 'dp', split_axis=0, concat_axis=0,...  290 us
    ppermute x3, waiting for transfers between devices, passed_along(): lax.ppermute(value, axis, [(i, (i + by) % peers) for i in range(peers)])  193 us
    all_to_all x1, waiting for transfers between devices, on_device(): lax.all_to_all(lax.all_to_all(partial_value, 'dp', split_axis=0, concat_a...  92.8 us
    all_to_all x1, blocking collectives, on_device(): lax.all_to_all(doubled, 'dp', split_axis=0, concat_axis=0, tiled=True)  52.2 us
    all_to_all x1, blocking collectives, on_device(): lax.all_to_all(partial_value, 'dp', split_axis=0, concat_axis=0, tiled=True)  51.9 us
  transfers between devices with their start and end apart: 5, of which 5 were waited for; matrix products, arithmetic and copies ran while one was open for 1% of the time, Pallas kernels for 0%

commit v1 on v0

v1 whole, which is shorter than its diff:
```python
import jax
import jax.numpy as jnp
from jax import lax
from jax.sharding import PartitionSpec as P

MESH_AXES = ("dp", "expert")
F32 = jnp.float32
BF16 = jnp.bfloat16


def expert_block(received, w_gate, w_up, w_down):
    gate_act = jnp.dot(received, w_gate, preferred_element_type=F32)
    up_act = jnp.dot(received, w_up, preferred_element_type=F32)
    hidden = (jax.nn.silu(gate_act) * up_act).astype(BF16)
    return jnp.dot(hidden, w_down, preferred_element_type=F32)


def holder_of(placement, swap_flags):
    experts = placement.shape[0]
    ids = jnp.arange(experts, dtype=jnp.int32)
    flag_at = jnp.sum(jnp.where(placement[:, None] == ids[None, :], swap_flags[None, :], 0), axis=1)
    return jnp.where(flag_at == 0, placement, (placement + experts // 2) % experts)


def routed_position(routes, holder):
    ids = jnp.arange(holder.shape[0], dtype=jnp.int32)
    return jnp.sum(jnp.where(routes[..., None] == ids, holder, 0), axis=-1)


NX, NC, NZ, NY = 2, 2, 4, 2


def flat(x, c, z, y):
    return (x * NC + c) * (NZ * NY) + z * NY + y


def moved(value, to):
    pairs = [
        (flat(x, c, z, y), flat(*to(x, c, z, y)))
        for x in range(NX)
        for c in range(NC)
        for z in range(NZ)
        for y in range(NY)
    ]
    return lax.ppermute(value, MESH_AXES, pairs)


def over_x(value):
    return moved(value, lambda x, c, z, y: (1 - x, c, z, y))


def over_y(value):
    return moved(value, lambda x, c, z, y: (x, c, z, 1 - y))


def over_core(value):
    return moved(value, lambda x, c, z, y: (x, 1 - c, z, y))


def along_z(value, by):
    return moved(value, lambda x, c, z, y: (x, c, (z + by) % NZ, y))


def plane_gather(block):
    half = block.shape[0] // 2
    from_x = over_x(block)
    from_y = over_y(block)
    first = over_y(from_x[:half])
    second = over_x(from_y[half:])
    return jnp.concatenate([block, from_x, from_y, first, second], axis=0)


def plane_sum(rows):
    size = rows.shape[0] // 4
    half = size // 2
    wide = rows.astype(F32)
    mine, for_x, for_y, for_diag = (wide[i * size : (i + 1) * size] for i in range(4))
    diag = rows[3 * size :]
    add_x = over_y(diag[:half]).astype(F32)
    add_y = over_x(diag[half:]).astype(F32)
    for_x = jnp.concatenate([for_x[:half] + add_x, for_x[half:]], axis=0).astype(BF16)
    for_y = jnp.concatenate([for_y[:half], for_y[half:] + add_y], axis=0).astype(BF16)
    return mine + over_x(for_x).astype(F32) + over_y(for_y).astype(F32)


def on_device_plane(
    tokens, routes, route_gates, placement, swap_flags, gate_weight, up_weight, down_weight
):
    rows = tokens.shape[0]
    w_gate, w_up, w_down = gate_weight[0], up_weight[0], down_weight[0]
    dp_at, expert_at = lax.axis_index("dp"), lax.axis_index("expert")
    x_at, c_at, z_at, y_at = dp_at // NC, dp_at % NC, expert_at // NY, expert_at % NY
    position = expert_at * NX + x_at

    all_routes = lax.all_gather(routes, MESH_AXES, axis=0)
    all_gates = lax.all_gather(route_gates, MESH_AXES, axis=0)
    target = routed_position(all_routes, holder_of(placement, swap_flags))
    row_gate = jnp.sum(jnp.where(target == position, all_gates, 0.0), axis=-1)
    row_gate = row_gate.reshape(NX, NC, NZ, NY, rows)

    def gates_from(c, shifts):
        def at(dx, dy):
            return jnp.concatenate(
                [row_gate[x_at ^ dx, c, (z_at - k) % NZ, y_at ^ dy] for k in shifts], axis=0
            )

        return jnp.concatenate([at(0, 0), at(1, 0), at(0, 1), at(1, 1)], axis=0)

    from_z = {k: along_z(tokens, k) for k in (1, 3, 2)}
    shift_sets = ((0,), (1, 3, 2))
    starts = (tokens, jnp.concatenate([from_z[k] for k in shift_sets[1]], axis=0))
    sums = []
    for shifts, start in zip(shift_sets, starts):
        own_rows = plane_gather(start)
        other_rows = over_core(own_rows)
        own = expert_block(own_rows, w_gate, w_up, w_down)
        other = expert_block(other_rows, w_gate, w_up, w_down)
        own = own * gates_from(c_at, shifts)[:, None]
        other = (other * gates_from(1 - c_at, shifts)[:, None]).astype(BF16)
        both = (own + over_core(other).astype(F32)).astype(BF16)
        sums.append(plane_sum(both))
    total = sums[0]
    for i, k in enumerate(shift_sets[1]):
        part = sums[1][i * rows : (i + 1) * rows].astype(BF16)
        total = total + along_z(part, NZ - k).astype(F32)
    return total.astype(BF16)


def on_device_lanes(
    tokens, routes, route_gates, placement, swap_flags, gate_weight, up_weight, down_weight
):
    tok_dev, features = tokens.shape
    route_count = routes.shape[1]
    columns = lax.axis_size("expert")
    replicas = lax.axis_size("dp")
    slot_count = replicas // 2
    experts = slot_count * columns
    capacity = 2 * tok_dev * route_count // experts
    lane_count = experts * capacity
    expert_ids = jnp.arange(experts, dtype=jnp.int32)
    flat_routes = routes.reshape(-1)
    matches = (flat_routes[:, None] == expert_ids[None, :]).astype(jnp.int32)
    target = routed_position(flat_routes, holder_of(placement, swap_flags))
    ranking = jnp.sum(matches * (jnp.cumsum(matches, axis=0) - 1), axis=1)
    column = target // slot_count
    slot_id = target % slot_count
    lane_index = (slot_id * columns + column) * capacity + ranking
    pair_row = jnp.arange(tok_dev * route_count, dtype=jnp.int32) // route_count
    lane_hit = (jnp.arange(lane_count, dtype=jnp.int32)[:, None] == lane_index[None, :]).astype(F32)
    row_hit = (jnp.arange(tok_dev, dtype=jnp.int32)[:, None] == pair_row[None, :]).astype(F32)
    selector = jnp.dot(lane_hit, row_hit.T, precision=lax.Precision.HIGHEST).astype(BF16)
    combine = jnp.dot(
        row_hit * route_gates.reshape(-1)[None, :], lane_hit.T, precision=lax.Precision.HIGHEST
    )
    outgoing = jnp.dot(selector, tokens, preferred_element_type=F32).astype(BF16)
    outgoing = outgoing.reshape(slot_count, columns, capacity, features)

    def exchanged(value):
        value = lax.all_to_all(value, "dp", split_axis=0, concat_axis=0, tiled=True)
        return lax.all_to_all(value, "expert", split_axis=1, concat_axis=1, tiled=True)

    arrived = exchanged(jnp.repeat(outgoing, 2, axis=0))
    partial_value = expert_block(
        arrived.reshape(-1, features), gate_weight[0], up_weight[0], down_weight[0]
    ).astype(BF16)
    returned = exchanged(partial_value.reshape(replicas, columns, capacity, features))
    halves = returned.reshape(slot_count, 2, columns, capacity, features)
    summed = (halves[:, 0].astype(F32) + halves[:, 1].astype(F32)).astype(BF16)
    expert_rows = summed.reshape(lane_count, features)
    layer_out = jnp.dot(combine, expert_rows.astype(F32), precision=lax.Precision.HIGHEST)
    return layer_out.astype(BF16)


def solution(mesh):
    planes = mesh.shape["dp"] == NX * NC and mesh.shape["expert"] == NZ * NY
    return jax.shard_map(
        on_device_plane if planes else on_device_lanes,
        mesh=mesh,
        in_specs=(
            P(MESH_AXES, None),
            P(MESH_AXES, None),
            P(MESH_AXES, None),
            P(),
            P(),
            P("expert", None, "dp"),
            P("expert", None, "dp"),
            P("expert", "dp", None),
        ),
        out_specs=P(MESH_AXES, None),
        check_vma=False,
    )
```

time: 721 us -> 246 us (0.34)
  waiting for transfers between devices: 576 us -> 26.9 us
  blocking collectives: 104 us -> 131 us
  matrix products: 9.8 us -> 31.7 us
  starting transfers between devices: 16.6 us -> 26.4 us
  other arithmetic: 2.51 us -> 11.1 us
    all_to_all x2 -> x0, waiting for transfers between devices: 383 us -> none  [the longest x1 290 us: on_device(): lax.all_to_all(lax.all_to_all(doubled, 'dp', split_axis=0, concat_axis=0,...]
    ppermute x3 -> x26, waiting for transfers between devices: 193 us -> 26.9 us  [moved(): return lax.ppermute(value, MESH_AXES, pairs)]
    all_gather x0 -> x2, blocking collectives: none -> 131 us  [the longest x1 66 us: on_device_plane(): all_gates = lax.all_gather(route_gates, MESH_AXES, axis=0)]
    all_to_all x2 -> x0, blocking collectives: 104 us -> none  [the longest x1 52.2 us: on_device(): lax.all_to_all(doubled, 'dp', split_axis=0, concat_axis=0, tiled=True)]
    dot_general x7 -> x8, matrix products: 9.8 us -> 31.7 us  [the longest x4 21.8 us: expert_block(): return jnp.dot(hidden, w_down, preferred_element_type=F32)]
    ppermute x3 -> x26, starting transfers between devices: 5.84 us -> 26.4 us  [moved(): return lax.ppermute(value, MESH_AXES, pairs)]
    all_to_all x2 -> x0, starting transfers between devices: 10.8 us -> none  [the longest x1 6.1 us: on_device(): lax.all_to_all(lax.all_to_all(doubled, 'dp', split_axis=0, concat_axis=0,...]
    all_to_all x4 -> x0, local copies, waits for them, and re-layouts: 9.4 us -> none  [the longest x1 2.46 us: on_device(): lax.all_to_all(lax.all_to_all(doubled, 'dp', split_axis=0, concat_axis=0,...]
  transfers between devices with their start and end apart: 5 -> 26, of which waited for: 5 -> 8; matrix products, arithmetic and copies ran while one was open for 1% -> 17% of each run, Pallas kernels for 0% -> 0%
where the time goes in v1:
time: 246 us; the launch traced here: 245 us
  blocking collectives  131 us (53%)
  matrix products  31.7 us (13%)
  waiting for transfers between devices  26.9 us (11%)
  starting transfers between devices  26.4 us (11%)
  local copies, waits for them, and re-layouts  18.2 us (7%)
  other arithmetic  11.1 us (5%)
    all_gather x1, blocking collectives, on_device_plane(): all_gates = lax.all_gather(route_gates, MESH_AXES, axis=0)  66 us
    all_gather x1, blocking collectives, on_device_plane(): all_routes = lax.all_gather(routes, MESH_AXES, axis=0)  64.8 us
    ppermute x26, waiting for transfers between devices, moved(): return lax.ppermute(value, MESH_AXES, pairs)  26.9 us
    ppermute x26, starting transfers between devices, moved(): return lax.ppermute(value, MESH_AXES, pairs)  26.4 us
    dot_general x4, matrix products, expert_block(): return jnp.dot(hidden, w_down, preferred_element_type=F32)  21.8 us
    dot_general x4, matrix products, expert_block(): up_act = jnp.dot(received, w_up, preferred_element_type=F32)  9.91 us
    unnamed x51, local copies, waits for them, and re-layouts  9.87 us
  transfers between devices with their start and end apart: 26, of which 8 were waited for; matrix products, arithmetic and copies ran while one was open for 17% of the time, Pallas kernels for 0%

profile of v1, /device:TPU:0, one launch (start us, length us, event | category | flops | bytes accessed | tf_op | source)
XLA Modules:
  0.0 245.5 jit_solution(11547712007401922267)
XLA Ops:
  0.0 3.0 %collective-permute-start.10 = (bf16[16,4096]{1,0:T(8,128)(2,1)}, bf16[16,4096]{1,0:T(8,128)(2,1)}, u32[]{:S(2)}, u32[]{:S(2)}) collective-permute-start(bf16[16,4096]{1,0:T(8,128)(2,1)} %param.8), channel_id=1, source_target_pairs={{0,2},{1,3},{2,4},{3,5},{4,6},{5,7},{6,0},{7,1},{8,10},{9,11},{10,... | collective-permute-start | bytes 393224 | tf_op jit(solution)/shard_map/ppermute | solution.py:45
  3.0 2.1 collective-permute-start.11
  5.1 1.0 collective-permute-start.12
  6.1 1.5 collective-permute-start
  7.6 1.5 collective-permute-start.1
  9.1 1.6 constant_dynamic-update-slice_fusion.4
  10.7 64.8 %all-gather.2 = s32[32,16,8]{1,2,0:T(8,128)S(1)} all-gather(s32[1,16,8]{1,2,0:T(8,128)} %bitcast.131), channel_id=2, replica_groups=mesh['dp'=4,'expert'=8] {'dp','expert'}, dimensions={0}, use_global_device_ids=true | all-gather | bytes 16896 | tf_op jit(solution)/shard_map/all_gather | solution.py:95
  76.2 0.9 select_reduce_fusion.2
  77.7 66.0 %all-gather.3 = f32[32,16,8]{1,2,0:T(8,128)S(1)} all-gather(f32[1,16,8]{1,2,0:T(8,128)} %bitcast.132), channel_id=3, replica_groups=mesh['dp'=4,'expert'=8] {'dp','expert'}, dimensions={0}, use_global_device_ids=true | all-gather | bytes 16896 | tf_op jit(solution)/shard_map/all_gather | solution.py:96
  144.5 1.2 select_reduce_fusion
  145.7 0.9 select_reduce_fusion.1
  148.1 1.6 constant_dynamic-update-slice_fusion.7
  149.7 1.6 constant_dynamic-update-slice_fusion.6
  151.3 1.6 constant_dynamic-update-slice_fusion.5
  153.9 1.6 collective-permute-start.2
  155.5 1.6 collective-permute-start.3
  158.4 3.5 %collective-permute-done.2 = bf16[8,4096]{1,0:T(8,128)(2,1)S(1)} collective-permute-done((bf16[8,4096]{1,0:T(8,128)(2,1)S(1)}, bf16[8,4096]{1,0:T(8,128)(2,1)S(1)}, u32[]{:S(2)}, u32[]{:S(2)}) %collective-permute-start.2) | collective-permute-done | bytes 65568 | tf_op jit(solution)/shard_map/ppermute | solution.py:45
  163.7 1.5 collective-permute-start.16
  166.8 3.7 %collective-permute-done.15 = bf16[24,4096]{1,0:T(8,128)(2,1)S(1)} collective-permute-done((bf16[24,4096]{1,0:T(8,128)(2,1)S(1)}, bf16[24,4096]{1,0:T(8,128)(2,1)S(1)}, u32[]{:S(2)}, u32[]{:S(2)}) %collective-permute-start.15) | collective-permute-done | bytes 196640 | tf_op jit(solution)/shard_map/ppermute | solution.py:45
  172.0 0.8 copy-done.2
  173.5 4.4 %fusion.1 = bf16[64,4096]{1,0:T(8,128)(2,1)} fusion(bf16[1,384,4096]{2,1,0:T(8,128)(2,1)S(1)} %copy-done, f32[64]{0:T(128)S(1)} %copy-done.20, f32[64,384]{1,0:T(8,128)S(1)} %fusion.10, bf16[64,4096]{1,0:T(8,128)(2,1)} %copy-done.2, bf16[1,4096,384]{2,1,0:T(8,128)(2,1)} %param.13), kind=kOutput, calls=%fused_computation.5 | convolution fusion | flops 403324928 | bytes 7438592 | tf_op jit(solution)/shard_map/dot_general | solution.py:15
  178.9 2.6 %fusion.12 = f32[64,384]{1,0:T(8,128)S(1)} fusion(bf16[64,4096]{1,0:T(8,128)(2,1)} %constant_dynamic-update-slice_fusion, bf16[1,4096,384]{2,1,0:T(8,128)(2,1)} %param.14), kind=kOutput, calls=%fused_computation.16 | convolution fusion | flops 201326592 | bytes 3768320 | tf_op jit(solution)/shard_map/dot_general | solution.py:13
  181.5 4.9 %fusion.100 = (f32[64,4096]{1,0:T(8,128)}, bf16[64,4096]{1,0:T(8,128)(2,1)}) fusion(bf16[64,4096]{1,0:T(8,128)(2,1)} %collective-permute-done.5, f32[64]{0:T(128)S(1)} %pad_maximum_fusion.4, bf16[1,384,4096]{2,1,0:T(8,128)(2,1)S(1)} %copy-done, f32[64,384]{1,0:T(8,128)S(1)} %fusion.12, bf16[64,4096]{1,0:T(8,128)(2,1)} %constant_dynamic-update-slice_fusion, ...), kind=kOutput, calls=%fused_computation.156 | convolution fusion | flops 404111360 | bytes 9011456 | tf_op jit(solution)/shard_map/dot_general | solution.py:15
  186.4 3.3 %fusion.6 = f32[192,384]{1,0:T(8,128)S(1)} fusion(bf16[192,4096]{1,0:T(8,128)(2,1)} %collective-permute-done.17, bf16[1,4096,384]{2,1,0:T(8,128)(2,1)} %param.14), kind=kOutput, calls=%fused_computation.10 | convolution fusion | flops 603979776 | bytes 5013504 | tf_op jit(solution)/shard_map/dot_general | solution.py:13
  189.8 5.5 %fusion = bf16[192,4096]{1,0:T(8,128)(2,1)} fusion(bf16[1,384,4096]{2,1,0:T(8,128)(2,1)S(1)} %copy-done, f32[192]{0:T(256)S(1)} %concatenate.46, f32[192,384]{1,0:T(8,128)S(1)} %fusion.6, bf16[192,4096]{1,0:T(8,128)(2,1)} %collective-permute-done.17, bf16[1,4096,384]{2,1,0:T(8,128)(2,1)} %param.13), kind=kOutput, calls=%fused_computation.2 | convolution fusion | flops 1209974784 | bytes 9732864 | tf_op jit(solution)/shard_map/dot_general | solution.py:15
  195.3 1.6 fusion.95
  196.8 1.1 collective-permute-start.6
  198.0 1.5 collective-permute-start.8
  199.5 3.3 %fusion.8 = f32[192,384]{1,0:T(8,128)S(1)} fusion(bf16[192,4096]{1,0:T(8,128)(2,1)} %constant_dynamic-update-slice_fusion.8, bf16[1,4096,384]{2,1,0:T(8,128)(2,1)} %param.14), kind=kOutput, calls=%fused_computation.12 | convolution fusion | flops 603979776 | bytes 5013504 | tf_op jit(solution)/shard_map/dot_general | solution.py:13
  202.8 1.7 fusion.46
  204.5 6.9 %fusion.97 = (f32[192,4096]{1,0:T(8,128)}, bf16[192,4096]{1,0:T(8,128)(2,1)}) fusion(bf16[192,4096]{1,0:T(8,128)(2,1)} %collective-permute-done.18, f32[192]{0:T(256)S(1)} %concatenate.45, bf16[1,384,4096]{2,1,0:T(8,128)(2,1)S(1)} %copy-done, f32[192,384]{1,0:T(8,128)S(1)} %fusion.8, bf16[192,4096]{1,0:T(8,128)(2,1)} %constant_dynamic-update-slice_fusion.8, ...), kind=kOutput, calls=%fused_computation.155 | convolution fusion | flops 1212334080 | bytes 14451456 | tf_op jit(solution)/shard_map/dot_general | solution.py:15
  211.4 1.3 fusion.94
  212.7 0.9 collective-permute-start.19
  213.7 0.9 collective-permute-start.21
  214.6 0.9 pad_maximum_fusion.2
  215.5 1.2 collective-permute-start.7
  216.7 2.9 %collective-permute-done.19 = bf16[24,4096]{1,0:T(8,128)(2,1)S(1)} collective-permute-done((bf16[24,4096]{1,0:T(8,128)(2,1)S(1)}, bf16[24,4096]{1,0:T(8,128)(2,1)S(1)}, u32[]{:S(2)}, u32[]{:S(2)}) %collective-permute-start.19) | collective-permute-done | bytes 196640 | tf_op jit(solution)/shard_map/ppermute | solution.py:45
  219.6 1.9 collective-permute-done.21
  221.5 1.2 fusion.29
  223.4 1.2 collective-permute-start.22
  224.6 0.9 collective-permute-start.9
  225.6 5.8 %collective-permute-done.20 = bf16[48,4096]{1,0:T(8,128)(2,1)S(1)} collective-permute-done((bf16[48,4096]{1,0:T(8,128)(2,1)S(1)}, bf16[48,4096]{1,0:T(8,128)(2,1)S(1)}, u32[]{:S(2)}, u32[]{:S(2)}) %collective-permute-start.20) | collective-permute-done | bytes 393248 | tf_op jit(solution)/shard_map/ppermute | solution.py:45
  231.4 1.4 collective-permute-done.22
  232.8 1.3 fusion.25
  234.1 2.0 collective-permute-start.24
  236.1 5.3 %collective-permute-done.23 = bf16[16,4096]{1,0:T(8,128)(2,1)S(1)} collective-permute-done((bf16[16,4096]{1,0:T(8,128)(2,1)S(1)}, bf16[16,4096]{1,0:T(8,128)(2,1)S(1)}, u32[]{:S(2)}, u32[]{:S(2)}) %collective-permute-start.23) | collective-permute-done | bytes 131104 | tf_op jit(solution)/shard_map/ppermute | solution.py:45
  241.4 2.4 collective-permute-done.25
  243.8 1.7 fusion.34
  (95 shorter events, 13.1 us)
Async XLA Ops:
  0.0 173.4 %copy-start = (bf16[1,384,4096]{2,1,0:T(8,128)(2,1)S(1)}, bf16[1,384,4096]{2,1,0:T(8,128)(2,1)}, u32[]{:S(2)}) copy-start(bf16[1,384,4096]{2,1,0:T(8,128)(2,1)} %param.15) | copy-start | bytes 9437188
  0.0 148.1 %collective-permute-start.10 = (bf16[16,4096]{1,0:T(8,128)(2,1)}, bf16[16,4096]{1,0:T(8,128)(2,1)}, u32[]{:S(2)}, u32[]{:S(2)}) collective-permute-start(bf16[16,4096]{1,0:T(8,128)(2,1)} %param.8), channel_id=1, source_target_pairs={{0,2},{1,3},{2,4},{3,5},{4,6},{5,7},{6,0},{7,1},{8,10},{9,11},{10,... | collective-permute-start | bytes 393224 | tf_op jit(solution)/shard_map/ppermute | solution.py:45
  3.0 146.7 %collective-permute-start.11 = (bf16[16,4096]{1,0:T(8,128)(2,1)}, bf16[16,4096]{1,0:T(8,128)(2,1)}, u32[]{:S(2)}, u32[]{:S(2)}) collective-permute-start(bf16[16,4096]{1,0:T(8,128)(2,1)} %param.8), channel_id=1, source_target_pairs={{0,6},{1,7},{2,0},{3,1},{4,2},{5,3},{6,4},{7,5},{8,14},{9,15},{10,... | collective-permute-start | bytes 393224 | tf_op jit(solution)/shard_map/ppermute | solution.py:45
  5.1 146.2 %collective-permute-start.12 = (bf16[16,4096]{1,0:T(8,128)(2,1)}, bf16[16,4096]{1,0:T(8,128)(2,1)}, u32[]{:S(2)}, u32[]{:S(2)}) collective-permute-start(bf16[16,4096]{1,0:T(8,128)(2,1)} %param.8), channel_id=1, source_target_pairs={{0,4},{1,5},{2,6},{3,7},{4,0},{5,1},{6,2},{7,3},{8,12},{9,13},{10,... | collective-permute-start | bytes 393224 | tf_op jit(solution)/shard_map/ppermute | solution.py:45
  6.1 147.8 %collective-permute-start = (bf16[16,4096]{1,0:T(8,128)(2,1)}, bf16[16,4096]{1,0:T(8,128)(2,1)S(1)}, u32[]{:S(2)}, u32[]{:S(2)}) collective-permute-start(bf16[16,4096]{1,0:T(8,128)(2,1)} %param.8), channel_id=1, source_target_pairs={{0,16},{1,17},{2,18},{3,19},{4,20},{5,21},{6,22},{7,23},{8,24},{9,... | collective-permute-start | bytes 393224 | tf_op jit(solution)/shard_map/ppermute | solution.py:45
  7.6 148.0 %collective-permute-start.1 = (bf16[16,4096]{1,0:T(8,128)(2,1)}, bf16[16,4096]{1,0:T(8,128)(2,1)S(1)}, u32[]{:S(2)}, u32[]{:S(2)}) collective-permute-start(bf16[16,4096]{1,0:T(8,128)(2,1)} %param.8), channel_id=1, source_target_pairs={{0,1},{1,0},{2,3},{3,2},{4,5},{5,4},{6,7},{7,6},{8,9},{9,8},{10,11... | collective-permute-start | bytes 393224 | tf_op jit(solution)/shard_map/ppermute | solution.py:45
  146.7 26.1 %copy-start.1 = (bf16[1,4096,384]{2,1,0:T(8,128)(2,1)S(1)}, bf16[1,4096,384]{2,1,0:T(8,128)(2,1)}, u32[]{:S(2)}) copy-start(bf16[1,4096,384]{2,1,0:T(8,128)(2,1)} %param.14) | copy-start | bytes 9437188
  152.9 10.3 %collective-permute-start.13 = (bf16[48,4096]{1,0:T(8,128)(2,1)S(1)}, bf16[48,4096]{1,0:T(8,128)(2,1)S(1)}, u32[]{:S(2)}, u32[]{:S(2)}) collective-permute-start(bf16[48,4096]{1,0:T(8,128)(2,1)S(1)} %get-tuple-element.20), channel_id=1, source_target_pairs={{0,16},{1,17},{2,18},{3,19},{4,20},{5,21},{6,22},{7,23},{8,24},{9,... | collective-permute-start | bytes 1179656 | tf_op jit(solution)/shard_map/ppermute | solution.py:45
  153.4 10.3 %collective-permute-start.14 = (bf16[48,4096]{1,0:T(8,128)(2,1)S(1)}, bf16[48,4096]{1,0:T(8,128)(2,1)S(1)}, u32[]{:S(2)}, u32[]{:S(2)}) collective-permute-start(bf16[48,4096]{1,0:T(8,128)(2,1)S(1)} %get-tuple-element.20), channel_id=1, source_target_pairs={{0,1},{1,0},{2,3},{3,2},{4,5},{5,4},{6,7},{7,6},{8,9},{9,8},{10,11... | collective-permute-start | bytes 1179656 | tf_op jit(solution)/shard_map/ppermute | solution.py:45
  153.9 8.0 %collective-permute-start.2 = (bf16[8,4096]{1,0:T(8,128)(2,1)S(1)}, bf16[8,4096]{1,0:T(8,128)(2,1)S(1)}, u32[]{:S(2)}, u32[]{:S(2)}) collective-permute-start(bf16[8,4096]{1,0:T(8,128)(2,1)S(1)} %slice.109), channel_id=1, source_target_pairs={{0,1},{1,0},{2,3},{3,2},{4,5},{5,4},{6,7},{7,6},{8,9},{9,8},{10,11... | collective-permute-start | bytes 196616 | tf_op jit(solution)/shard_map/ppermute | solution.py:45
  155.5 7.0 %collective-permute-start.3 = (bf16[8,4096]{1,0:T(8,128)(2,1)S(1)}, bf16[8,4096]{1,0:T(8,128)(2,1)S(1)}, u32[]{:S(2)}, u32[]{:S(2)}) collective-permute-start(bf16[8,4096]{1,0:T(8,128)(2,1)S(1)} %slice.110), channel_id=1, source_target_pairs={{0,16},{1,17},{2,18},{3,19},{4,20},{5,21},{6,22},{7,23},{8,24},{9,... | collective-permute-start | bytes 196616 | tf_op jit(solution)/shard_map/ppermute | solution.py:45
  163.1 8.8 %collective-permute-start.4 = (bf16[64,4096]{1,0:T(8,128)(2,1)}, bf16[64,4096]{1,0:T(8,128)(2,1)S(1)}, u32[]{:S(2)}, u32[]{:S(2)}) collective-permute-start(bf16[64,4096]{1,0:T(8,128)(2,1)} %constant_dynamic-update-slice_fusion), channel_id=1, source_target_pairs={{0,8},{1,9},{2,10},{3,11},{4,12},{5,13},{6,14},{7,15},{8,0},{9,1},... | collective-permute-start | bytes 1572872 | tf_op jit(solution)/shard_map/ppermute | solution.py:45
  163.2 7.4 %collective-permute-start.15 = (bf16[24,4096]{1,0:T(8,128)(2,1)S(1)}, bf16[24,4096]{1,0:T(8,128)(2,1)S(1)}, u32[]{:S(2)}, u32[]{:S(2)}) collective-permute-start(bf16[24,4096]{1,0:T(8,128)(2,1)S(1)} %slice.118), channel_id=1, source_target_pairs={{0,1},{1,0},{2,3},{3,2},{4,5},{5,4},{6,7},{7,6},{8,9},{9,8},{10,11... | collective-permute-start | bytes 589832 | tf_op jit(solution)/shard_map/ppermute | solution.py:45
  163.7 9.7 %copy-start.20 = (f32[64]{0:T(128)S(1)}, f32[64]{0:T(128)}, u32[]{:S(2)}) copy-start(f32[64]{0:T(128)} %pad_maximum_fusion.5) | copy-start | bytes 772
  163.7 7.5 %collective-permute-start.16 = (bf16[24,4096]{1,0:T(8,128)(2,1)S(1)}, bf16[24,4096]{1,0:T(8,128)(2,1)S(1)}, u32[]{:S(2)}, u32[]{:S(2)}) collective-permute-start(bf16[24,4096]{1,0:T(8,128)(2,1)S(1)} %slice.119), channel_id=1, source_target_pairs={{0,16},{1,17},{2,18},{3,19},{4,20},{5,21},{6,22},{7,23},{8,24},{9,... | collective-permute-start | bytes 589832 | tf_op jit(solution)/shard_map/ppermute | solution.py:45
  172.0 14.5 %collective-permute-start.17 = (bf16[192,4096]{1,0:T(8,128)(2,1)}, bf16[192,4096]{1,0:T(8,128)(2,1)}, u32[]{:S(2)}, u32[]{:S(2)}) collective-permute-start(bf16[192,4096]{1,0:T(8,128)(2,1)} %constant_dynamic-update-slice_fusion.8), channel_id=1, source_target_pairs={{0,8},{1,9},{2,10},{3,11},{4,12},{5,13},{6,14},{7,15},{8,0},{9,1},... | collective-permute-start | bytes 4718600 | tf_op jit(solution)/shard_map/ppermute | solution.py:45
  172.0 0.8 copy-start.2
  173.4 5.1 %copy-start.4 = (f32[16]{0:T(128)S(1)}, f32[16]{0:T(128)}, u32[]{:S(2)}) copy-start(f32[16]{0:T(128)} %get-tuple-element.27) | copy-start | bytes 196
  173.4 5.1 %copy-start.5 = (f32[16]{0:T(128)S(1)}, f32[16]{0:T(128)}, u32[]{:S(2)}) copy-start(f32[16]{0:T(128)} %get-tuple-element.28) | copy-start | bytes 196
  173.4 5.1 %copy-start.6 = (f32[16]{0:T(128)S(1)}, f32[16]{0:T(128)}, u32[]{:S(2)}) copy-start(f32[16]{0:T(128)} %get-tuple-element.29) | copy-start | bytes 196
  173.4 5.1 %copy-start.7 = (f32[16]{0:T(128)S(1)}, f32[16]{0:T(128)}, u32[]{:S(2)}) copy-start(f32[16]{0:T(128)} %get-tuple-element.30) | copy-start | bytes 196
  173.4 5.1 %copy-start.8 = (f32[16]{0:T(128)S(1)}, f32[16]{0:T(128)}, u32[]{:S(2)}) copy-start(f32[16]{0:T(128)} %get-tuple-element.31) | copy-start | bytes 196
  173.4 5.1 %copy-start.9 = (f32[16]{0:T(128)S(1)}, f32[16]{0:T(128)}, u32[]{:S(2)}) copy-start(f32[16]{0:T(128)} %get-tuple-element.32) | copy-start | bytes 196
  173.4 5.1 %copy-start.10 = (f32[16]{0:T(128)S(1)}, f32[16]{0:T(128)}, u32[]{:S(2)}) copy-start(f32[16]{0:T(128)} %get-tuple-element.33) | copy-start | bytes 196
  173.5 5.1 %copy-start.11 = (f32[16]{0:T(128)S(1)}, f32[16]{0:T(128)}, u32[]{:S(2)}) copy-start(f32[16]{0:T(128)} %get-tuple-element.34) | copy-start | bytes 196
  173.5 5.1 %copy-start.12 = (f32[16]{0:T(128)S(1)}, f32[16]{0:T(128)}, u32[]{:S(2)}) copy-start(f32[16]{0:T(128)} %get-tuple-element.35) | copy-start | bytes 196
  173.5 5.1 %copy-start.13 = (f32[16]{0:T(128)S(1)}, f32[16]{0:T(128)}, u32[]{:S(2)}) copy-start(f32[16]{0:T(128)} %get-tuple-element.36) | copy-start | bytes 196
  173.5 5.1 %copy-start.14 = (f32[16]{0:T(128)S(1)}, f32[16]{0:T(128)}, u32[]{:S(2)}) copy-start(f32[16]{0:T(128)} %get-tuple-element.37) | copy-start | bytes 196
  173.5 5.1 %copy-start.15 = (f32[16]{0:T(128)S(1)}, f32[16]{0:T(128)}, u32[]{:S(2)}) copy-start(f32[16]{0:T(128)} %get-tuple-element.38) | copy-start | bytes 196
  173.5 5.2 %copy-start.16 = (f32[16]{0:T(128)S(1)}, f32[16]{0:T(128)}, u32[]{:S(2)}) copy-start(f32[16]{0:T(128)} %get-tuple-element.54) | copy-start | bytes 196
  173.5 5.2 %copy-start.17 = (f32[16]{0:T(128)S(1)}, f32[16]{0:T(128)}, u32[]{:S(2)}) copy-start(f32[16]{0:T(128)} %get-tuple-element.55) | copy-start | bytes 196
  173.5 5.2 %copy-start.18 = (f32[16]{0:T(128)S(1)}, f32[16]{0:T(128)}, u32[]{:S(2)}) copy-start(f32[16]{0:T(128)} %get-tuple-element.56) | copy-start | bytes 196
  173.5 5.2 %copy-start.19 = (f32[16]{0:T(128)S(1)}, f32[16]{0:T(128)}, u32[]{:S(2)}) copy-start(f32[16]{0:T(128)} %get-tuple-element.57) | copy-start | bytes 196
  178.0 3.5 %collective-permute-start.5 = (bf16[64,4096]{1,0:T(8,128)(2,1)}, bf16[64,4096]{1,0:T(8,128)(2,1)}, u32[]{:S(2)}, u32[]{:S(2)}) collective-permute-start(bf16[64,4096]{1,0:T(8,128)(2,1)} %fusion.1), channel_id=1, source_target_pairs={{0,8},{1,9},{2,10},{3,11},{4,12},{5,13},{6,14},{7,15},{8,0},{9,1},... | collective-permute-start | bytes 1572872 | tf_op jit(solution)/shard_map/ppermute | solution.py:45
  195.2 9.2 %collective-permute-start.18 = (bf16[192,4096]{1,0:T(8,128)(2,1)}, bf16[192,4096]{1,0:T(8,128)(2,1)}, u32[]{:S(2)}, u32[]{:S(2)}) collective-permute-start(bf16[192,4096]{1,0:T(8,128)(2,1)} %fusion), channel_id=1, source_target_pairs={{0,8},{1,9},{2,10},{3,11},{4,12},{5,13},{6,14},{7,15},{8,0},{9,1},... | collective-permute-start | bytes 4718600 | tf_op jit(solution)/shard_map/ppermute | solution.py:45
  196.8 6.0 %collective-permute-start.6 = (bf16[8,4096]{1,0:T(8,128)(2,1)S(1)}, bf16[8,4096]{1,0:T(8,128)(2,1)S(1)}, u32[]{:S(2)}, u32[]{:S(2)}) collective-permute-start(bf16[8,4096]{1,0:T(8,128)(2,1)S(1)} %get-tuple-element.13), channel_id=1, source_target_pairs={{0,1},{1,0},{2,3},{3,2},{4,5},{5,4},{6,7},{7,6},{8,9},{9,8},{10,11... | collective-permute-start | bytes 196616 | tf_op jit(solution)/shard_map/ppermute | solution.py:45
  198.0 4.8 %collective-permute-start.8 = (bf16[8,4096]{1,0:T(8,128)(2,1)S(1)}, bf16[8,4096]{1,0:T(8,128)(2,1)S(1)}, u32[]{:S(2)}, u32[]{:S(2)}) collective-permute-start(bf16[8,4096]{1,0:T(8,128)(2,1)S(1)} %get-tuple-element.14), channel_id=1, source_target_pairs={{0,16},{1,17},{2,18},{3,19},{4,20},{5,21},{6,22},{7,23},{8,24},{9,... | collective-permute-start | bytes 196616 | tf_op jit(solution)/shard_map/ppermute | solution.py:45
  211.4 13.2 %copy-start.3 = (bf16[8,4096]{1,0:T(8,128)(2,1)S(1)}, bf16[8,4096]{1,0:T(8,128)(2,1)}, u32[]{:S(2)}) copy-start(bf16[8,4096]{1,0:T(8,128)(2,1)} %get-tuple-element.12) | copy-start | bytes 196612
  212.7 6.8 %collective-permute-start.19 = (bf16[24,4096]{1,0:T(8,128)(2,1)S(1)}, bf16[24,4096]{1,0:T(8,128)(2,1)S(1)}, u32[]{:S(2)}, u32[]{:S(2)}) collective-permute-start(bf16[24,4096]{1,0:T(8,128)(2,1)S(1)} %get-tuple-element.7), channel_id=1, source_target_pairs={{0,1},{1,0},{2,3},{3,2},{4,5},{5,4},{6,7},{7,6},{8,9},{9,8},{10,11... | collective-permute-start | bytes 589832 | tf_op jit(solution)/shard_map/ppermute | solution.py:45
  213.7 7.8 %collective-permute-start.21 = (bf16[24,4096]{1,0:T(8,128)(2,1)S(1)}, bf16[24,4096]{1,0:T(8,128)(2,1)S(1)}, u32[]{:S(2)}, u32[]{:S(2)}) collective-permute-start(bf16[24,4096]{1,0:T(8,128)(2,1)S(1)} %get-tuple-element.8), channel_id=1, source_target_pairs={{0,16},{1,17},{2,18},{3,19},{4,20},{5,21},{6,22},{7,23},{8,24},{9,... | collective-permute-start | bytes 589832 | tf_op jit(solution)/shard_map/ppermute | solution.py:45
  215.5 20.7 %collective-permute-start.7 = (bf16[16,4096]{1,0:T(8,128)(2,1)S(1)}, bf16[16,4096]{1,0:T(8,128)(2,1)S(1)}, u32[]{:S(2)}, u32[]{:S(2)}) collective-permute-start(bf16[16,4096]{1,0:T(8,128)(2,1)S(1)} %pad_maximum_fusion.2), channel_id=1, source_target_pairs={{0,16},{1,17},{2,18},{3,19},{4,20},{5,21},{6,22},{7,23},{8,24},{9,... | collective-permute-start | bytes 393224 | tf_op jit(solution)/shard_map/ppermute | solution.py:45
  222.7 8.7 %collective-permute-start.20 = (bf16[48,4096]{1,0:T(8,128)(2,1)S(1)}, bf16[48,4096]{1,0:T(8,128)(2,1)S(1)}, u32[]{:S(2)}, u32[]{:S(2)}) collective-permute-start(bf16[48,4096]{1,0:T(8,128)(2,1)S(1)} %pad_maximum_fusion), channel_id=1, source_target_pairs={{0,16},{1,17},{2,18},{3,19},{4,20},{5,21},{6,22},{7,23},{8,24},{9,... | collective-permute-start | bytes 1179656 | tf_op jit(solution)/shard_map/ppermute | solution.py:45
  223.4 9.3 %collective-permute-start.22 = (bf16[48,4096]{1,0:T(8,128)(2,1)S(1)}, bf16[48,4096]{1,0:T(8,128)(2,1)S(1)}, u32[]{:S(2)}, u32[]{:S(2)}) collective-permute-start(bf16[48,4096]{1,0:T(8,128)(2,1)S(1)} %pad_maximum_fusion.1), channel_id=1, source_target_pairs={{0,1},{1,0},{2,3},{3,2},{4,5},{5,4},{6,7},{7,6},{8,9},{9,8},{10,11... | collective-permute-start | bytes 1179656 | tf_op jit(solution)/shard_map/ppermute | solution.py:45
  224.6 11.5 %collective-permute-start.9 = (bf16[16,4096]{1,0:T(8,128)(2,1)S(1)}, bf16[16,4096]{1,0:T(8,128)(2,1)S(1)}, u32[]{:S(2)}, u32[]{:S(2)}) collective-permute-start(bf16[16,4096]{1,0:T(8,128)(2,1)S(1)} %pad_maximum_fusion.3), channel_id=1, source_target_pairs={{0,1},{1,0},{2,3},{3,2},{4,5},{5,4},{6,7},{7,6},{8,9},{9,8},{10,11... | collective-permute-start | bytes 393224 | tf_op jit(solution)/shard_map/ppermute | solution.py:45
  234.0 7.4 %collective-permute-start.23 = (bf16[16,4096]{1,0:T(8,128)(2,1)S(1)}, bf16[16,4096]{1,0:T(8,128)(2,1)S(1)}, u32[]{:S(2)}, u32[]{:S(2)}) collective-permute-start(bf16[16,4096]{1,0:T(8,128)(2,1)S(1)} %get-tuple-element.17), channel_id=1, source_target_pairs={{0,6},{1,7},{2,0},{3,1},{4,2},{5,3},{6,4},{7,5},{8,14},{9,15},{10,... | collective-permute-start | bytes 393224 | tf_op jit(solution)/shard_map/ppermute | solution.py:45
  234.1 7.3 %collective-permute-start.24 = (bf16[16,4096]{1,0:T(8,128)(2,1)S(1)}, bf16[16,4096]{1,0:T(8,128)(2,1)S(1)}, u32[]{:S(2)}, u32[]{:S(2)}) collective-permute-start(bf16[16,4096]{1,0:T(8,128)(2,1)S(1)} %get-tuple-element.19), channel_id=1, source_target_pairs={{0,2},{1,3},{2,4},{3,5},{4,6},{5,7},{6,0},{7,1},{8,10},{9,11},{10,... | collective-permute-start | bytes 393224 | tf_op jit(solution)/shard_map/ppermute | solution.py:45
  236.1 7.7 %collective-permute-start.25 = (bf16[16,4096]{1,0:T(8,128)(2,1)S(1)}, bf16[16,4096]{1,0:T(8,128)(2,1)S(1)}, u32[]{:S(2)}, u32[]{:S(2)}) collective-permute-start(bf16[16,4096]{1,0:T(8,128)(2,1)S(1)} %get-tuple-element.18), channel_id=1, source_target_pairs={{0,4},{1,5},{2,6},{3,7},{4,0},{5,1},{6,2},{7,3},{8,12},{9,13},{10,... | collective-permute-start | bytes 393224 | tf_op jit(solution)/shard_map/ppermute | solution.py:45

commit v2 on v1

--- a/solution.py
+++ b/solution.py
@@ -1,6 +1,10 @@
+import functools
+
 import jax
 import jax.numpy as jnp
 from jax import lax
+from jax.experimental import pallas as pl
+from jax.experimental.pallas import tpu as pltpu
 from jax.sharding import PartitionSpec as P
 
 MESH_AXES = ("dp", "expert")
@@ -28,6 +32,14 @@
 
 
 NX, NC, NZ, NY = 2, 2, 4, 2
+TAIL = 128
+PARTS = 3
+ORDER = (0, 1, 3, 2)
+COST = 20
+
+IN_VMEM = pl.BlockSpec(memory_space=pltpu.VMEM)
+IN_SMEM = pl.BlockSpec(memory_space=pltpu.SMEM)
+IN_HBM = pl.BlockSpec(memory_space=pltpu.HBM)
 
 
 def flat(x, c, z, y):
@@ -45,12 +57,12 @@
     return lax.ppermute(value, MESH_AXES, pairs)
 
 
-def over_x(value):
-    return moved(value, lambda x, c, z, y: (1 - x, c, z, y))
-
-
-def over_y(value):
-    return moved(value, lambda x, c, z, y: (x, c, z, 1 - y))
+def over_first(value):
+    return moved(value, lambda x, c, z, y: (x ^ 1 ^ c, c, z, y ^ c))
+
+
+def over_second(value):
+    return moved(value, lambda x, c, z, y: (x ^ c, c, z, y ^ 1 ^ c))
 
 
 def over_core(value):
@@ -58,72 +70,204 @@
 
 
 def along_z(value, by):
-    return moved(value, lambda x, c, z, y: (x, c, (z + by) % NZ, y))
-
-
-def plane_gather(block):
-    half = block.shape[0] // 2
-    from_x = over_x(block)
-    from_y = over_y(block)
-    first = over_y(from_x[:half])
-    second = over_x(from_y[half:])
-    return jnp.concatenate([block, from_x, from_y, first, second], axis=0)
-
-
-def plane_sum(rows):
-    size = rows.shape[0] // 4
-    half = size // 2
-    wide = rows.astype(F32)
-    mine, for_x, for_y, for_diag = (wide[i * size : (i + 1) * size] for i in range(4))
-    diag = rows[3 * size :]
-    add_x = over_y(diag[:half]).astype(F32)
-    add_y = over_x(diag[half:]).astype(F32)
-    for_x = jnp.concatenate([for_x[:half] + add_x, for_x[half:]], axis=0).astype(BF16)
-    for_y = jnp.concatenate([for_y[:half], for_y[half:] + add_y], axis=0).astype(BF16)
-    return mine + over_x(for_x).astype(F32) + over_y(for_y).astype(F32)
+    return moved(value, lambda x, c, z, y: (x, c, z ^ by, y))
+
+
+def kernel(body, name, outs, arrays, scalars=(), scratch=(), far=0, vmem=2, flops=0):
+    placed = [pltpu.with_memory_space_constraint(a, pltpu.HBM) for a in arrays[:far]]
+    placed += [pltpu.with_memory_space_constraint(a, pltpu.VMEM) for a in arrays[far:]]
+    return pl.pallas_call(
+        body,
+        name=name,
+        out_shape=[pltpu.VMEM(shape, dtype) for shape, dtype in outs],
+        in_specs=[IN_SMEM] * len(scalars) + [IN_HBM] * far + [IN_VMEM] * (len(arrays) - far),
+        out_specs=[IN_VMEM] * len(outs),
+        scratch_shapes=list(scratch),
+        compiler_params=pltpu.CompilerParams(vmem_limit_bytes=vmem * 2**20),
+        cost_estimate=pl.CostEstimate(flops=flops, bytes_accessed=0, transcendentals=0),
+    )(*scalars, *placed)
+
+
+def label_body(
+    tokens, routes, gates, placement, flags, out, token_at, route_at, gate_at, place_at, flag_at, sems
+):
+    rows, features = tokens.shape
+    experts = placement.shape[0]
+    pairs = (
+        (placement, place_at),
+        (flags, flag_at),
+        (routes, route_at),
+        (gates, gate_at),
+        (tokens, token_at),
+    )
+    copies = [pltpu.make_async_copy(a, b, sems.at[i]) for i, (a, b) in enumerate(pairs)]
+    for copy in copies:
+        copy.start()
+    for copy in copies:
+        copy.wait()
+    out[:, :features] = token_at[...]
+    named = route_at[...].T
+    row_gates = gate_at[...].T
+    target = jnp.zeros_like(named)
+    for x in range(experts):
+        held = place_at[x]
+        held = jnp.where(flag_at[held] == 0, held, (held + experts // 2) % experts)
+        target = jnp.where(named == x, held, target)
+    lane = lax.broadcasted_iota(jnp.int32, (rows, TAIL), 1)
+    weight = jnp.zeros((rows, TAIL), F32)
+    for k in range(named.shape[1]):
+        weight += jnp.where(lane % experts == target[:, k : k + 1], row_gates[:, k : k + 1], 0.0)
+    high = weight.astype(BF16)
+    rest = weight - high.astype(F32)
+    middle = rest.astype(BF16)
+    low = (rest - middle.astype(F32)).astype(BF16)
+    tail = jnp.where(lane < experts, high.astype(F32), 0.0)
+    tail = jnp.where((lane >= experts) & (lane < 2 * experts), middle.astype(F32), tail)
+    tail = jnp.where((lane >= 2 * experts) & (lane < PARTS * experts), low.astype(F32), tail)
+    out[:, features:] = tail.astype(BF16)
+
+
+def labelled(tokens, routes, route_gates, placement, swap_flags):
+    rows, features = tokens.shape
+    arrays = (tokens, routes.T, route_gates.T, placement, swap_flags)
+    outs = [((rows, features + TAIL), BF16)]
+    scratch = [pltpu.VMEM(a.shape, a.dtype) for a in arrays[:3]]
+    scratch += [pltpu.SMEM(a.shape, a.dtype) for a in arrays[3:]]
+    scratch.append(pltpu.SemaphoreType.DMA((len(arrays),)))
+    [out] = kernel(label_body, "label", outs, arrays, scratch=scratch, far=len(arrays))
+    return out
+
+
+def stage_body(*refs):
+    *pairs, sems = refs
+    count = len(pairs) // 2
+    copies = [pltpu.make_async_copy(pairs[i], pairs[count + i], sems.at[i]) for i in range(count)]
+    for copy in copies:
+        copy.start()
+    for copy in copies:
+        copy.wait()
+
+
+def staged(weights):
+    outs = [(w.shape, w.dtype) for w in weights]
+    scratch = [pltpu.SemaphoreType.DMA((len(weights),))]
+    return kernel(stage_body, "stage", outs, weights, scratch=scratch, far=len(weights))
+
+
+def pack_body(groups, *refs):
+    blocks, outs = list(refs[: sum(groups)]), refs[len(refs) - len(groups) :]
+    for out, count in zip(outs, groups):
+        at = 0
+        for _ in range(count):
+            block = blocks.pop(0)
+            out[at : at + block.shape[0], :] = block[...]
+            at += block.shape[0]
+
+
+def packed(*groups, after=()):
+    outs = [((sum(b.shape[0] for b in g), g[0].shape[1]), g[0].dtype) for g in groups]
+    body = functools.partial(pack_body, tuple(len(g) for g in groups))
+    return kernel(body, "pack", outs, [b for g in groups for b in g] + list(after))
+
+
+def expert_body(features, experts, mine, others, w_gate, w_up, w_down, *refs):
+    kept, sent, partner, joined, hidden = refs
+    count, half = mine.shape[0], kept.shape[0]
+    position = lax.axis_index("expert") * NX + lax.div(lax.axis_index("dp"), NC)
+    joined[:count, :] = mine[...]
+    joined[count:, :] = others[...]
+    x = joined[:, :features]
+    gate_act = jnp.dot(x, w_gate[...], preferred_element_type=F32)
+    up_act = jnp.dot(x, w_up[...], preferred_element_type=F32)
+    hidden[...] = (gate_act / (1.0 + jnp.exp(-gate_act)) * up_act).astype(BF16)
+    tail = joined[:, features:].astype(F32)
+    lane = lax.broadcasted_iota(jnp.int32, tail.shape, 1)
+    here = (lane % experts == position) & (lane < PARTS * experts)
+    row_gate = jnp.sum(jnp.where(here, tail, 0.0), axis=1, keepdims=True)
+    h = hidden[...]
+    step = 512
+    for c in range(0, features, step):
+        columns = slice(c, c + step)
+        value = jnp.dot(h, w_down[:, columns], preferred_element_type=F32) * row_gate
+        value = value.astype(BF16)
+        kept[:, columns] = value[:half]
+        sent[:, columns] = value[half:count]
+        partner[:, columns] = value[count:]
+
+
+def expert_rows(mine, others, weights, experts):
+    count, width = mine.shape
+    features, hidden_units = weights[0].shape
+    return kernel(
+        functools.partial(expert_body, features, experts),
+        "expert",
+        [((n, features), BF16) for n in (count // 2, count // 2, count)],
+        (mine, others, *weights),
+        scratch=[pltpu.VMEM((2 * count, width), BF16), pltpu.VMEM((2 * count, hidden_units), BF16)],
+        vmem=6,
+        flops=COST * 12 * count * features * hidden_units,
+    )
+
+
+def core_sum_body(sent, received, out):
+    rows = received[sent.shape[0] :, :].astype(F32)
+    out[...] = (sent[...].astype(F32) + rows).astype(BF16)
+
+
+def part_sum_body(kept, from_core, received, mine, passed):
+    rows = mine.shape[0]
+
+    def total(at):
+        return (kept[at, :].astype(F32) + from_core[at, :].astype(F32)) + received[at, :].astype(F32)
+
+    mine[...] = total(slice(0, rows))
+    passed[...] = total(slice(rows, 2 * rows)).astype(BF16)
+
+
+def plane_sum_body(mine, received, out):
+    out[...] = (mine[...] + received[...].astype(F32)).astype(out.dtype)
+
+
+def final_sum_body(*refs):
+    *parts, out = refs
+    total = parts[0][...].astype(F32)
+    for part in parts[1:]:
+        total += part[...].astype(F32)
+    out[...] = total.astype(BF16)
 
 
 def on_device_plane(
     tokens, routes, route_gates, placement, swap_flags, gate_weight, up_weight, down_weight
 ):
-    rows = tokens.shape[0]
-    w_gate, w_up, w_down = gate_weight[0], up_weight[0], down_weight[0]
-    dp_at, expert_at = lax.axis_index("dp"), lax.axis_index("expert")
-    x_at, c_at, z_at, y_at = dp_at // NC, dp_at % NC, expert_at // NY, expert_at % NY
-    position = expert_at * NX + x_at
-
-    all_routes = lax.all_gather(routes, MESH_AXES, axis=0)
-    all_gates = lax.all_gather(route_gates, MESH_AXES, axis=0)
-    target = routed_position(all_routes, holder_of(placement, swap_flags))
-    row_gate = jnp.sum(jnp.where(target == position, all_gates, 0.0), axis=-1)
-    row_gate = row_gate.reshape(NX, NC, NZ, NY, rows)
-
-    def gates_from(c, shifts):
-        def at(dx, dy):
-            return jnp.concatenate(
-                [row_gate[x_at ^ dx, c, (z_at - k) % NZ, y_at ^ dy] for k in shifts], axis=0
-            )
-
-        return jnp.concatenate([at(0, 0), at(1, 0), at(0, 1), at(1, 1)], axis=0)
-
-    from_z = {k: along_z(tokens, k) for k in (1, 3, 2)}
-    shift_sets = ((0,), (1, 3, 2))
-    starts = (tokens, jnp.concatenate([from_z[k] for k in shift_sets[1]], axis=0))
-    sums = []
-    for shifts, start in zip(shift_sets, starts):
-        own_rows = plane_gather(start)
-        other_rows = over_core(own_rows)
-        own = expert_block(own_rows, w_gate, w_up, w_down)
-        other = expert_block(other_rows, w_gate, w_up, w_down)
-        own = own * gates_from(c_at, shifts)[:, None]
-        other = (other * gates_from(1 - c_at, shifts)[:, None]).astype(BF16)
-        both = (own + over_core(other).astype(F32)).astype(BF16)
-        sums.append(plane_sum(both))
-    total = sums[0]
-    for i, k in enumerate(shift_sets[1]):
-        part = sums[1][i * rows : (i + 1) * rows].astype(BF16)
-        total = total + along_z(part, NZ - k).astype(F32)
-    return total.astype(BF16)
+    rows, features = tokens.shape
+    experts = placement.shape[0]
+    weights = gate_weight[0], up_weight[0], down_weight[0]
+    own = labelled(tokens, routes, route_gates, placement, swap_flags)
+    weights = staged(weights)
+    from_z = {k: along_z(own, k) for k in (3, 1, 2)}
+    near = {0: over_first(own)}
+    pair0, block1, block3 = packed([own, near[0]], [from_z[1]], [from_z[3]], after=weights[:1])
+    blocks = {1: block1, 3: block3, 2: from_z[2]}
+    pairs = {0: pair0}
+    mine, others = {}, {}
+    for step in ORDER:
+        if step:
+            [pairs[step]] = packed([blocks[step], over_first(blocks[step])])
+        [mine[step]] = packed([pairs[step], over_second(pairs[step])])
+        others[step] = over_core(mine[step])
+    parts = []
+    for step in ORDER:
+        kept, sent, partner = expert_rows(mine[step], others[step], weights, experts)
+        from_core = over_core(partner)
+        [sent] = kernel(core_sum_body, "core_sum", [(sent.shape, BF16)], (sent, from_core))
+        outs = [((rows, features), F32), ((rows, features), BF16)]
+        arrays = (kept, from_core, over_second(sent))
+        kept, sent = kernel(part_sum_body, "part_sum", outs, arrays)
+        outs = [((rows, features), BF16 if step else F32)]
+        [total] = kernel(plane_sum_body, "plane_sum", outs, (kept, over_first(sent)))
+        parts.append(along_z(total, step) if step else total)
+    [out] = kernel(final_sum_body, "final_sum", [((rows, features), BF16)], parts)
+    return out
 
 
 def on_device_lanes(

time: 246 us -> 85.1 us (0.35)
  blocking collectives: 131 us -> 0 us
  matrix products: 31.7 us -> 0 us
  local copies, waits for them, and re-layouts: 18.2 us -> 0.66 us
  Pallas kernels: 0 us -> 13.6 us
  other arithmetic: 11.1 us -> 0 us
  waiting for transfers between devices: 26.9 us -> 37.2 us
  starting transfers between devices: 26.4 us -> 33.3 us
    all_gather x2 -> x0, blocking collectives: 131 us -> none  [the longest x1 66 us: on_device_plane(): all_gates = lax.all_gather(route_gates, MESH_AXES, axis=0)]
    dot_general x8 -> x0, matrix products: 31.7 us -> none  [the longest x4 21.8 us: expert_block(): return jnp.dot(hidden, w_down, preferred_element_type=F32)]
    pallas_call x0 -> x27, Pallas kernels: none -> 13.6 us  [kernel(): pl.pallas_call(body, name=name, out_shape=[pltpu.VMEM(shape, dtype) for s...]
    ppermute x26 -> x30, waiting for transfers between devices: 26.9 us -> 37.2 us  [moved(): return lax.ppermute(value, MESH_AXES, pairs)]
    unnamed x51 -> x1, local copies, waits for them, and re-layouts: 9.87 us -> 0.66 us
    ppermute x26 -> x30, starting transfers between devices: 26.4 us -> 33.3 us  [moved(): return lax.ppermute(value, MESH_AXES, pairs)]
    another operation x3 -> x0, other arithmetic: 4.09 us -> none
    concatenate x5 -> x0, local copies, waits for them, and re-layouts: 3.08 us -> none  [the longest x1 1.58 us: on_device_plane(): jnp.concatenate([from_z[k] for k in shift_sets[1]], axis=0)]
  transfers between devices with their start and end apart: 26 -> 30, of which waited for: 8 -> 14; matrix products, arithmetic and copies ran while one was open for 17% -> 0% of each run, Pallas kernels for 0% -> 14%
where the time goes in v2:
time: 85.1 us; the launch traced here: 84.9 us
  waiting for transfers between devices  37.2 us (44%)
  starting transfers between devices  33.3 us (39%)
  Pallas kernels  13.6 us (16%)
    ppermute x30, waiting for transfers between devices, moved(): return lax.ppermute(value, MESH_AXES, pairs)  37.2 us
    ppermute x30, starting transfers between devices, moved(): return lax.ppermute(value, MESH_AXES, pairs)  33.3 us
    pallas_call x27, Pallas kernels, kernel(): pl.pallas_call(body, name=name, out_shape=[pltpu.VMEM(shape, dtype) for s...  13.6 us
  transfers between devices with their start and end apart: 30, of which 14 were waited for; matrix products, arithmetic and copies ran while one was open for 0% of the time, Pallas kernels for 14%

profile of v2, /device:TPU:0, one launch (start us, length us, event | category | flops | bytes accessed | tf_op | source)
XLA Modules:
  0.0 84.9 jit_solution(2485157025044245667)
XLA Ops:
  0.0 1.2 %label.1.refs_0_ = bf16[16,4224]{1,0:T(8,128)(2,1)S(1)} custom-call(bf16[16,4096]{1,0:T(8,128)(2,1)} %tokens.1, s32[8,16]{1,0:T(8,128)} %bitcast.8, f32[8,16]{1,0:T(8,128)} %bitcast.9, s32[16]{0:T(128)} %placement.1, s32[16]{0:T(128)} %flags.1), custom_call_target="tpu_custom_call" | custom-call | tf_op jit(solution)/shard_map/label/pallas_call | solution.py:79
  1.2 3.0 %collective-permute-start = (bf16[16,4224]{1,0:T(8,128)(2,1)S(1)}, bf16[16,4224]{1,0:T(8,128)(2,1)S(1)}, u32[]{:S(2)}, u32[]{:S(2)}) collective-permute-start(bf16[16,4224]{1,0:T(8,128)(2,1)S(1)} %label.1.refs_0_), channel_id=1, source_target_pairs={{0,16},{1,17},{2,18},{3,19},{4,20},{5,21},{6,22},{7,23},{8,9},{9,8... | collective-permute-start | bytes 405512 | tf_op jit(solution)/shard_map/ppermute | solution.py:57
  4.2 1.6 %collective-permute-start.1 = (bf16[16,4224]{1,0:T(8,128)(2,1)S(1)}, bf16[16,4224]{1,0:T(8,128)(2,1)S(1)}, u32[]{:S(2)}, u32[]{:S(2)}) collective-permute-start(bf16[16,4224]{1,0:T(8,128)(2,1)S(1)} %label.1.refs_0_), channel_id=1, source_target_pairs={{0,2},{1,3},{2,0},{3,1},{4,6},{5,7},{6,4},{7,5},{8,10},{9,11},{10,... | collective-permute-start | bytes 405512 | tf_op jit(solution)/shard_map/ppermute | solution.py:57
  5.8 2.5 %collective-permute-start.2 = (bf16[16,4224]{1,0:T(8,128)(2,1)S(1)}, bf16[16,4224]{1,0:T(8,128)(2,1)S(1)}, u32[]{:S(2)}, u32[]{:S(2)}) collective-permute-start(bf16[16,4224]{1,0:T(8,128)(2,1)S(1)} %label.1.refs_0_), channel_id=1, source_target_pairs={{0,6},{1,7},{2,4},{3,5},{4,2},{5,3},{6,0},{7,1},{8,14},{9,15},{10,... | collective-permute-start | bytes 405512 | tf_op jit(solution)/shard_map/ppermute | solution.py:57
  8.3 3.8 %stage.1 = (bf16[4096,384]{1,0:T(8,128)(2,1)S(1)}, bf16[4096,384]{1,0:T(8,128)(2,1)S(1)}, bf16[384,4096]{1,0:T(8,128)(2,1)S(1)}) custom-call(bf16[4096,384]{1,0:T(8,128)(2,1)} %bitcast.5, bf16[4096,384]{1,0:T(8,128)(2,1)} %bitcast.6, bf16[384,4096]{1,0:T(8,128)(2,1)} %bitcast.7), custom_call_target="tpu_custom_call" | custom-call | tf_op jit(solution)/shard_map/stage/pallas_call | solution.py:79
  12.1 2.2 %collective-permute-done.2.refs_3_ = bf16[16,4224]{1,0:T(8,128)(2,1)S(1)} collective-permute-done((bf16[16,4224]{1,0:T(8,128)(2,1)S(1)}, bf16[16,4224]{1,0:T(8,128)(2,1)S(1)}, u32[]{:S(2)}, u32[]{:S(2)}) %collective-permute-start.2) | collective-permute-done | bytes 135200 | tf_op jit(solution)/shard_map/ppermute | solution.py:57
  14.4 1.6 %collective-permute-start.8 = (bf16[16,4224]{1,0:T(8,128)(2,1)S(1)}, bf16[16,4224]{1,0:T(8,128)(2,1)S(1)}, u32[]{:S(2)}, u32[]{:S(2)}) collective-permute-start(bf16[16,4224]{1,0:T(8,128)(2,1)S(1)} %get-tuple-element.40.refs_0_), channel_id=1, source_target_pairs={{0,16},{1,17},{2,18},{3,19},{4,20},{5,21},{6,22},{7,23},{8,9},{9,8... | collective-permute-start | bytes 405512 | tf_op jit(solution)/shard_map/ppermute | solution.py:57
  15.9 3.5 %collective-permute-done.8.refs_1_ = bf16[16,4224]{1,0:T(8,128)(2,1)S(1)} collective-permute-done((bf16[16,4224]{1,0:T(8,128)(2,1)S(1)}, bf16[16,4224]{1,0:T(8,128)(2,1)S(1)}, u32[]{:S(2)}, u32[]{:S(2)}) %collective-permute-start.8) | collective-permute-done | bytes 135200 | tf_op jit(solution)/shard_map/ppermute | solution.py:57
  19.5 0.6 collective-permute-start.9
  20.0 1.9 %collective-permute-start.22 = (bf16[16,4224]{1,0:T(8,128)(2,1)S(1)}, bf16[16,4224]{1,0:T(8,128)(2,1)S(1)}, u32[]{:S(2)}, u32[]{:S(2)}) collective-permute-start(bf16[16,4224]{1,0:T(8,128)(2,1)S(1)} %label.1.refs_0_), channel_id=1, source_target_pairs={{0,4},{1,5},{2,6},{3,7},{4,0},{5,1},{6,2},{7,3},{8,12},{9,13},{10,... | collective-permute-start | bytes 405512 | tf_op jit(solution)/shard_map/ppermute | solution.py:57
  22.0 4.0 %collective-permute-done.9.refs_1_ = bf16[32,4224]{1,0:T(8,128)(2,1)S(1)} collective-permute-done((bf16[32,4224]{1,0:T(8,128)(2,1)S(1)}, bf16[32,4224]{1,0:T(8,128)(2,1)S(1)}, u32[]{:S(2)}, u32[]{:S(2)}) %collective-permute-start.9) | collective-permute-done | bytes 270368 | tf_op jit(solution)/shard_map/ppermute | solution.py:57
  26.1 1.6 %collective-permute-start.15 = (bf16[16,4224]{1,0:T(8,128)(2,1)S(1)}, bf16[16,4224]{1,0:T(8,128)(2,1)S(1)}, u32[]{:S(2)}, u32[]{:S(2)}) collective-permute-start(bf16[16,4224]{1,0:T(8,128)(2,1)S(1)} %get-tuple-element.46.refs_0_), channel_id=1, source_target_pairs={{0,16},{1,17},{2,18},{3,19},{4,20},{5,21},{6,22},{7,23},{8,9},{9,8... | collective-permute-start | bytes 405512 | tf_op jit(solution)/shard_map/ppermute | solution.py:57
  27.7 1.2 %collective-permute-start.23 = (bf16[16,4224]{1,0:T(8,128)(2,1)S(1)}, bf16[16,4224]{1,0:T(8,128)(2,1)S(1)}, u32[]{:S(2)}, u32[]{:S(2)}) collective-permute-start(bf16[16,4224]{1,0:T(8,128)(2,1)S(1)} %collective-permute-done.22.refs_0_), channel_id=1, source_target_pairs={{0,16},{1,17},{2,18},{3,19},{4,20},{5,21},{6,22},{7,23},{8,9},{9,8... | collective-permute-start | bytes 405512 | tf_op jit(solution)/shard_map/ppermute | solution.py:57
  28.8 1.6 %collective-permute-start.3 = (bf16[32,4224]{1,0:T(8,128)(2,1)S(1)}, bf16[32,4224]{1,0:T(8,128)(2,1)S(1)}, u32[]{:S(2)}, u32[]{:S(2)}) collective-permute-start(bf16[32,4224]{1,0:T(8,128)(2,1)S(1)} %get-tuple-element.32.refs_0_), channel_id=1, source_target_pairs={{0,1},{1,0},{2,3},{3,2},{4,5},{5,4},{6,7},{7,6},{8,24},{9,25},{10,... | collective-permute-start | bytes 811016 | tf_op jit(solution)/shard_map/ppermute | solution.py:57
  30.4 1.3 %collective-permute-done.15.refs_1_ = bf16[16,4224]{1,0:T(8,128)(2,1)S(1)} collective-permute-done((bf16[16,4224]{1,0:T(8,128)(2,1)S(1)}, bf16[16,4224]{1,0:T(8,128)(2,1)S(1)}, u32[]{:S(2)}, u32[]{:S(2)}) %collective-permute-start.15) | collective-permute-done | bytes 135200 | tf_op jit(solution)/shard_map/ppermute | solution.py:57
  31.7 0.6 collective-permute-start.16
  32.3 2.3 %collective-permute-done.23.refs_1_ = bf16[16,4224]{1,0:T(8,128)(2,1)S(1)} collective-permute-done((bf16[16,4224]{1,0:T(8,128)(2,1)S(1)}, bf16[16,4224]{1,0:T(8,128)(2,1)S(1)}, u32[]{:S(2)}, u32[]{:S(2)}) %collective-permute-start.23) | collective-permute-done | bytes 135200 | tf_op jit(solution)/shard_map/ppermute | solution.py:57
  34.6 0.9 %collective-permute-start.24 = (bf16[32,4224]{1,0:T(8,128)(2,1)S(1)}, bf16[32,4224]{1,0:T(8,128)(2,1)S(1)}, u32[]{:S(2)}, u32[]{:S(2)}) collective-permute-start(bf16[32,4224]{1,0:T(8,128)(2,1)S(1)} %pack.14.refs_0_), channel_id=1, source_target_pairs={{0,1},{1,0},{2,3},{3,2},{4,5},{5,4},{6,7},{7,6},{8,24},{9,25},{10,... | collective-permute-start | bytes 811016 | tf_op jit(solution)/shard_map/ppermute | solution.py:57
  35.5 0.2 collective-permute-start.4
  35.7 2.5 %collective-permute-done.16.refs_1_ = bf16[32,4224]{1,0:T(8,128)(2,1)S(1)} collective-permute-done((bf16[32,4224]{1,0:T(8,128)(2,1)S(1)}, bf16[32,4224]{1,0:T(8,128)(2,1)S(1)}, u32[]{:S(2)}, u32[]{:S(2)}) %collective-permute-start.16) | collective-permute-done | bytes 270368 | tf_op jit(solution)/shard_map/ppermute | solution.py:57
  38.3 0.4 collective-permute-start.17
  38.6 2.5 %collective-permute-done.24.refs_1_ = bf16[32,4224]{1,0:T(8,128)(2,1)S(1)} collective-permute-done((bf16[32,4224]{1,0:T(8,128)(2,1)S(1)}, bf16[32,4224]{1,0:T(8,128)(2,1)S(1)}, u32[]{:S(2)}, u32[]{:S(2)}) %collective-permute-start.24) | collective-permute-done | bytes 270368 | tf_op jit(solution)/shard_map/ppermute | solution.py:57
  41.4 1.9 %expert.5 = (bf16[32,4096]{1,0:T(8,128)(2,1)S(1)}, bf16[32,4096]{1,0:T(8,128)(2,1)S(1)}, bf16[64,4096]{1,0:T(8,128)(2,1)S(1)}) custom-call(bf16[64,4224]{1,0:T(8,128)(2,1)S(1)} %pack.11.mine, bf16[64,4224]{1,0:T(8,128)(2,1)S(1)} %collective-permute-done.10.others, bf16[4096,384]{1,0:T(8,128)(2,1)S(1)} %get-tuple-element.31.refs_4_.w_gate, ...), custom_call_target="tpu_custom_call" | custom-call | flops 24159191040 | tf_op jit(solution)/shard_map/expert/pallas_call | solution.py:79
  43.3 0.5 collective-permute-start.11
  43.7 1.9 %expert.6 = (bf16[32,4096]{1,0:T(8,128)(2,1)S(1)}, bf16[32,4096]{1,0:T(8,128)(2,1)S(1)}, bf16[64,4096]{1,0:T(8,128)(2,1)S(1)}) custom-call(bf16[64,4224]{1,0:T(8,128)(2,1)S(1)} %pack.13.mine, bf16[64,4224]{1,0:T(8,128)(2,1)S(1)} %collective-permute-done.17.others, bf16[4096,384]{1,0:T(8,128)(2,1)S(1)} %get-tuple-element.31.refs_4_.w_gate, ...), custom_call_target="tpu_custom_call" | custom-call | flops 24159191040 | tf_op jit(solution)/shard_map/expert/pallas_call | solution.py:79
  45.8 1.9 %expert.7 = (bf16[32,4096]{1,0:T(8,128)(2,1)S(1)}, bf16[32,4096]{1,0:T(8,128)(2,1)S(1)}, bf16[64,4096]{1,0:T(8,128)(2,1)S(1)}) custom-call(bf16[64,4224]{1,0:T(8,128)(2,1)S(1)} %pack.15.mine, bf16[64,4224]{1,0:T(8,128)(2,1)S(1)} %collective-permute-done.25.others, bf16[4096,384]{1,0:T(8,128)(2,1)S(1)} %get-tuple-element.31.refs_4_.w_gate, ...), custom_call_target="tpu_custom_call" | custom-call | flops 24159191040 | tf_op jit(solution)/shard_map/expert/pallas_call | solution.py:79
  47.7 0.5 collective-permute-start.26
  48.2 1.9 %expert.4 = (bf16[32,4096]{1,0:T(8,128)(2,1)S(1)}, bf16[32,4096]{1,0:T(8,128)(2,1)S(1)}, bf16[64,4096]{1,0:T(8,128)(2,1)S(1)}) custom-call(bf16[64,4224]{1,0:T(8,128)(2,1)S(1)} %pack.9.mine, bf16[64,4224]{1,0:T(8,128)(2,1)S(1)} %collective-permute-done.4.others, bf16[4096,384]{1,0:T(8,128)(2,1)S(1)} %get-tuple-element.31.refs_4_.w_gate, ...), custom_call_target="tpu_custom_call" | custom-call | flops 24159191040 | tf_op jit(solution)/shard_map/expert/pallas_call | solution.py:79
  50.1 0.2 collective-permute-start.5
  50.4 1.5 %collective-permute-start.12 = (bf16[32,4096]{1,0:T(8,128)(2,1)S(1)}, bf16[32,4096]{1,0:T(8,128)(2,1)S(1)}, u32[]{:S(2)}, u32[]{:S(2)}) collective-permute-start(bf16[32,4096]{1,0:T(8,128)(2,1)S(1)} %core_sum.5), channel_id=1, source_target_pairs={{0,1},{1,0},{2,3},{3,2},{4,5},{5,4},{6,7},{7,6},{8,24},{9,25},{10,... | collective-permute-start | bytes 786440 | tf_op jit(solution)/shard_map/ppermute | solution.py:57
  52.0 0.6 collective-permute-start.19
  52.7 1.5 %collective-permute-start.27 = (bf16[32,4096]{1,0:T(8,128)(2,1)S(1)}, bf16[32,4096]{1,0:T(8,128)(2,1)S(1)}, u32[]{:S(2)}, u32[]{:S(2)}) collective-permute-start(bf16[32,4096]{1,0:T(8,128)(2,1)S(1)} %core_sum.7), channel_id=1, source_target_pairs={{0,1},{1,0},{2,3},{3,2},{4,5},{5,4},{6,7},{7,6},{8,24},{9,25},{10,... | collective-permute-start | bytes 786440 | tf_op jit(solution)/shard_map/ppermute | solution.py:57
  54.3 0.6 collective-permute-start.6
  54.9 1.9 %collective-permute-done.12.received = bf16[32,4096]{1,0:T(8,128)(2,1)S(1)} collective-permute-done((bf16[32,4096]{1,0:T(8,128)(2,1)S(1)}, bf16[32,4096]{1,0:T(8,128)(2,1)S(1)}, u32[]{:S(2)}, u32[]{:S(2)}) %collective-permute-start.12) | collective-permute-done | bytes 262176 | tf_op jit(solution)/shard_map/ppermute | solution.py:57
  56.9 1.6 %collective-permute-start.13 = (bf16[16,4096]{1,0:T(8,128)(2,1)S(1)}, bf16[16,4096]{1,0:T(8,128)(2,1)S(1)}, u32[]{:S(2)}, u32[]{:S(2)}) collective-permute-start(bf16[16,4096]{1,0:T(8,128)(2,1)S(1)} %get-tuple-element.45), channel_id=1, source_target_pairs={{0,16},{1,17},{2,18},{3,19},{4,20},{5,21},{6,22},{7,23},{8,9},{9,8... | collective-permute-start | bytes 393224 | tf_op jit(solution)/shard_map/ppermute | solution.py:57
  58.5 1.6 %collective-permute-done.19.received = bf16[32,4096]{1,0:T(8,128)(2,1)S(1)} collective-permute-done((bf16[32,4096]{1,0:T(8,128)(2,1)S(1)}, bf16[32,4096]{1,0:T(8,128)(2,1)S(1)}, u32[]{:S(2)}, u32[]{:S(2)}) %collective-permute-start.19) | collective-permute-done | bytes 262176 | tf_op jit(solution)/shard_map/ppermute | solution.py:57
  60.2 1.6 %collective-permute-start.20 = (bf16[16,4096]{1,0:T(8,128)(2,1)S(1)}, bf16[16,4096]{1,0:T(8,128)(2,1)S(1)}, u32[]{:S(2)}, u32[]{:S(2)}) collective-permute-start(bf16[16,4096]{1,0:T(8,128)(2,1)S(1)} %get-tuple-element.51), channel_id=1, source_target_pairs={{0,16},{1,17},{2,18},{3,19},{4,20},{5,21},{6,22},{7,23},{8,9},{9,8... | collective-permute-start | bytes 393224 | tf_op jit(solution)/shard_map/ppermute | solution.py:57
  61.7 3.5 %collective-permute-done.27.received = bf16[32,4096]{1,0:T(8,128)(2,1)S(1)} collective-permute-done((bf16[32,4096]{1,0:T(8,128)(2,1)S(1)}, bf16[32,4096]{1,0:T(8,128)(2,1)S(1)}, u32[]{:S(2)}, u32[]{:S(2)}) %collective-permute-start.27) | collective-permute-done | bytes 262176 | tf_op jit(solution)/shard_map/ppermute | solution.py:57
  65.3 1.6 %collective-permute-start.28 = (bf16[16,4096]{1,0:T(8,128)(2,1)S(1)}, bf16[16,4096]{1,0:T(8,128)(2,1)S(1)}, u32[]{:S(2)}, u32[]{:S(2)}) collective-permute-start(bf16[16,4096]{1,0:T(8,128)(2,1)S(1)} %get-tuple-element.56), channel_id=1, source_target_pairs={{0,16},{1,17},{2,18},{3,19},{4,20},{5,21},{6,22},{7,23},{8,9},{9,8... | collective-permute-start | bytes 393224 | tf_op jit(solution)/shard_map/ppermute | solution.py:57
  66.9 2.5 %collective-permute-done.6.received = bf16[32,4096]{1,0:T(8,128)(2,1)S(1)} collective-permute-done((bf16[32,4096]{1,0:T(8,128)(2,1)S(1)}, bf16[32,4096]{1,0:T(8,128)(2,1)S(1)}, u32[]{:S(2)}, u32[]{:S(2)}) %collective-permute-start.6) | collective-permute-done | bytes 262176 | tf_op jit(solution)/shard_map/ppermute | solution.py:57
  69.5 1.6 %collective-permute-start.7 = (bf16[16,4096]{1,0:T(8,128)(2,1)S(1)}, bf16[16,4096]{1,0:T(8,128)(2,1)S(1)}, u32[]{:S(2)}, u32[]{:S(2)}) collective-permute-start(bf16[16,4096]{1,0:T(8,128)(2,1)S(1)} %get-tuple-element.39), channel_id=1, source_target_pairs={{0,16},{1,17},{2,18},{3,19},{4,20},{5,21},{6,22},{7,23},{8,9},{9,8... | collective-permute-start | bytes 393224 | tf_op jit(solution)/shard_map/ppermute | solution.py:57
  71.1 0.6 collective-permute-start.14
  71.8 2.7 %collective-permute-start.21 = (bf16[16,4096]{1,0:T(8,128)(2,1)S(1)}, bf16[16,4096]{1,0:T(8,128)(2,1)S(1)}, u32[]{:S(2)}, u32[]{:S(2)}) collective-permute-start(bf16[16,4096]{1,0:T(8,128)(2,1)S(1)} %plane_sum.6), channel_id=1, source_target_pairs={{0,6},{1,7},{2,4},{3,5},{4,2},{5,3},{6,0},{7,1},{8,14},{9,15},{10,... | collective-permute-start | bytes 393224 | tf_op jit(solution)/shard_map/ppermute | solution.py:57
  74.6 0.3 collective-permute-start.29
  74.9 1.6 %collective-permute-done.14.refs_1_ = bf16[16,4096]{1,0:T(8,128)(2,1)S(1)} collective-permute-done((bf16[16,4096]{1,0:T(8,128)(2,1)S(1)}, bf16[16,4096]{1,0:T(8,128)(2,1)S(1)}, u32[]{:S(2)}, u32[]{:S(2)}) %collective-permute-start.14) | collective-permute-done | bytes 131104 | tf_op jit(solution)/shard_map/ppermute | solution.py:57
  76.5 2.9 %collective-permute-done.21.refs_2_ = bf16[16,4096]{1,0:T(8,128)(2,1)S(1)} collective-permute-done((bf16[16,4096]{1,0:T(8,128)(2,1)S(1)}, bf16[16,4096]{1,0:T(8,128)(2,1)S(1)}, u32[]{:S(2)}, u32[]{:S(2)}) %collective-permute-start.21) | collective-permute-done | bytes 131104 | tf_op jit(solution)/shard_map/ppermute | solution.py:57
  79.4 4.8 %collective-permute-done.29.refs_3_ = bf16[16,4096]{1,0:T(8,128)(2,1)S(1)} collective-permute-done((bf16[16,4096]{1,0:T(8,128)(2,1)S(1)}, bf16[16,4096]{1,0:T(8,128)(2,1)S(1)}, u32[]{:S(2)}, u32[]{:S(2)}) %collective-permute-start.29) | collective-permute-done | bytes 131104 | tf_op jit(solution)/shard_map/ppermute | solution.py:57
  84.3 0.7 copy.9
  (40 shorter events, 1.5 us)
Async XLA Ops:
  1.2 10.8 %collective-permute-start = (bf16[16,4224]{1,0:T(8,128)(2,1)S(1)}, bf16[16,4224]{1,0:T(8,128)(2,1)S(1)}, u32[]{:S(2)}, u32[]{:S(2)}) collective-permute-start(bf16[16,4224]{1,0:T(8,128)(2,1)S(1)} %label.1.refs_0_), channel_id=1, source_target_pairs={{0,16},{1,17},{2,18},{3,19},{4,20},{5,21},{6,22},{7,23},{8,9},{9,8... | collective-permute-start | bytes 405512 | tf_op jit(solution)/shard_map/ppermute | solution.py:57
  4.2 7.9 %collective-permute-start.1 = (bf16[16,4224]{1,0:T(8,128)(2,1)S(1)}, bf16[16,4224]{1,0:T(8,128)(2,1)S(1)}, u32[]{:S(2)}, u32[]{:S(2)}) collective-permute-start(bf16[16,4224]{1,0:T(8,128)(2,1)S(1)} %label.1.refs_0_), channel_id=1, source_target_pairs={{0,2},{1,3},{2,0},{3,1},{4,6},{5,7},{6,4},{7,5},{8,10},{9,11},{10,... | collective-permute-start | bytes 405512 | tf_op jit(solution)/shard_map/ppermute | solution.py:57
  5.8 8.5 %collective-permute-start.2 = (bf16[16,4224]{1,0:T(8,128)(2,1)S(1)}, bf16[16,4224]{1,0:T(8,128)(2,1)S(1)}, u32[]{:S(2)}, u32[]{:S(2)}) collective-permute-start(bf16[16,4224]{1,0:T(8,128)(2,1)S(1)} %label.1.refs_0_), channel_id=1, source_target_pairs={{0,6},{1,7},{2,4},{3,5},{4,2},{5,3},{6,0},{7,1},{8,14},{9,15},{10,... | collective-permute-start | bytes 405512 | tf_op jit(solution)/shard_map/ppermute | solution.py:57
  14.4 5.1 %collective-permute-start.8 = (bf16[16,4224]{1,0:T(8,128)(2,1)S(1)}, bf16[16,4224]{1,0:T(8,128)(2,1)S(1)}, u32[]{:S(2)}, u32[]{:S(2)}) collective-permute-start(bf16[16,4224]{1,0:T(8,128)(2,1)S(1)} %get-tuple-element.40.refs_0_), channel_id=1, source_target_pairs={{0,16},{1,17},{2,18},{3,19},{4,20},{5,21},{6,22},{7,23},{8,9},{9,8... | collective-permute-start | bytes 405512 | tf_op jit(solution)/shard_map/ppermute | solution.py:57
  19.5 6.5 %collective-permute-start.9 = (bf16[32,4224]{1,0:T(8,128)(2,1)S(1)}, bf16[32,4224]{1,0:T(8,128)(2,1)S(1)}, u32[]{:S(2)}, u32[]{:S(2)}) collective-permute-start(bf16[32,4224]{1,0:T(8,128)(2,1)S(1)} %pack.10.refs_0_), channel_id=1, source_target_pairs={{0,1},{1,0},{2,3},{3,2},{4,5},{5,4},{6,7},{7,6},{8,24},{9,25},{10,... | collective-permute-start | bytes 811016 | tf_op jit(solution)/shard_map/ppermute | solution.py:57
  20.0 7.6 %collective-permute-start.22 = (bf16[16,4224]{1,0:T(8,128)(2,1)S(1)}, bf16[16,4224]{1,0:T(8,128)(2,1)S(1)}, u32[]{:S(2)}, u32[]{:S(2)}) collective-permute-start(bf16[16,4224]{1,0:T(8,128)(2,1)S(1)} %label.1.refs_0_), channel_id=1, source_target_pairs={{0,4},{1,5},{2,6},{3,7},{4,0},{5,1},{6,2},{7,3},{8,12},{9,13},{10,... | collective-permute-start | bytes 405512 | tf_op jit(solution)/shard_map/ppermute | solution.py:57
  26.0 15.3 %collective-permute-start.10 = (bf16[64,4224]{1,0:T(8,128)(2,1)S(1)}, bf16[64,4224]{1,0:T(8,128)(2,1)S(1)}, u32[]{:S(2)}, u32[]{:S(2)}) collective-permute-start(bf16[64,4224]{1,0:T(8,128)(2,1)S(1)} %pack.11.mine), channel_id=1, source_target_pairs={{0,8},{1,9},{2,10},{3,11},{4,12},{5,13},{6,14},{7,15},{8,0},{9,1},... | collective-permute-start | bytes 1622024 | tf_op jit(solution)/shard_map/ppermute | solution.py:57
  26.1 5.6 %collective-permute-start.15 = (bf16[16,4224]{1,0:T(8,128)(2,1)S(1)}, bf16[16,4224]{1,0:T(8,128)(2,1)S(1)}, u32[]{:S(2)}, u32[]{:S(2)}) collective-permute-start(bf16[16,4224]{1,0:T(8,128)(2,1)S(1)} %get-tuple-element.46.refs_0_), channel_id=1, source_target_pairs={{0,16},{1,17},{2,18},{3,19},{4,20},{5,21},{6,22},{7,23},{8,9},{9,8... | collective-permute-start | bytes 405512 | tf_op jit(solution)/shard_map/ppermute | solution.py:57
  27.7 6.9 %collective-permute-start.23 = (bf16[16,4224]{1,0:T(8,128)(2,1)S(1)}, bf16[16,4224]{1,0:T(8,128)(2,1)S(1)}, u32[]{:S(2)}, u32[]{:S(2)}) collective-permute-start(bf16[16,4224]{1,0:T(8,128)(2,1)S(1)} %collective-permute-done.22.refs_0_), channel_id=1, source_target_pairs={{0,16},{1,17},{2,18},{3,19},{4,20},{5,21},{6,22},{7,23},{8,9},{9,8... | collective-permute-start | bytes 405512 | tf_op jit(solution)/shard_map/ppermute | solution.py:57
  28.8 6.7 %collective-permute-start.3 = (bf16[32,4224]{1,0:T(8,128)(2,1)S(1)}, bf16[32,4224]{1,0:T(8,128)(2,1)S(1)}, u32[]{:S(2)}, u32[]{:S(2)}) collective-permute-start(bf16[32,4224]{1,0:T(8,128)(2,1)S(1)} %get-tuple-element.32.refs_0_), channel_id=1, source_target_pairs={{0,1},{1,0},{2,3},{3,2},{4,5},{5,4},{6,7},{7,6},{8,24},{9,25},{10,... | collective-permute-start | bytes 811016 | tf_op jit(solution)/shard_map/ppermute | solution.py:57
  31.7 6.5 %collective-permute-start.16 = (bf16[32,4224]{1,0:T(8,128)(2,1)S(1)}, bf16[32,4224]{1,0:T(8,128)(2,1)S(1)}, u32[]{:S(2)}, u32[]{:S(2)}) collective-permute-start(bf16[32,4224]{1,0:T(8,128)(2,1)S(1)} %pack.12.refs_0_), channel_id=1, source_target_pairs={{0,1},{1,0},{2,3},{3,2},{4,5},{5,4},{6,7},{7,6},{8,24},{9,25},{10,... | collective-permute-start | bytes 811016 | tf_op jit(solution)/shard_map/ppermute | solution.py:57
  34.6 6.5 %collective-permute-start.24 = (bf16[32,4224]{1,0:T(8,128)(2,1)S(1)}, bf16[32,4224]{1,0:T(8,128)(2,1)S(1)}, u32[]{:S(2)}, u32[]{:S(2)}) collective-permute-start(bf16[32,4224]{1,0:T(8,128)(2,1)S(1)} %pack.14.refs_0_), channel_id=1, source_target_pairs={{0,1},{1,0},{2,3},{3,2},{4,5},{5,4},{6,7},{7,6},{8,24},{9,25},{10,... | collective-permute-start | bytes 811016 | tf_op jit(solution)/shard_map/ppermute | solution.py:57
  35.5 12.7 %collective-permute-start.4 = (bf16[64,4224]{1,0:T(8,128)(2,1)S(1)}, bf16[64,4224]{1,0:T(8,128)(2,1)S(1)}, u32[]{:S(2)}, u32[]{:S(2)}) collective-permute-start(bf16[64,4224]{1,0:T(8,128)(2,1)S(1)} %pack.9.mine), channel_id=1, source_target_pairs={{0,8},{1,9},{2,10},{3,11},{4,12},{5,13},{6,14},{7,15},{8,0},{9,1},... | collective-permute-start | bytes 1622024 | tf_op jit(solution)/shard_map/ppermute | solution.py:57
  38.3 5.5 %collective-permute-start.17 = (bf16[64,4224]{1,0:T(8,128)(2,1)S(1)}, bf16[64,4224]{1,0:T(8,128)(2,1)S(1)}, u32[]{:S(2)}, u32[]{:S(2)}) collective-permute-start(bf16[64,4224]{1,0:T(8,128)(2,1)S(1)} %pack.13.mine), channel_id=1, source_target_pairs={{0,8},{1,9},{2,10},{3,11},{4,12},{5,13},{6,14},{7,15},{8,0},{9,1},... | collective-permute-start | bytes 1622024 | tf_op jit(solution)/shard_map/ppermute | solution.py:57
  41.2 4.7 %collective-permute-start.25 = (bf16[64,4224]{1,0:T(8,128)(2,1)S(1)}, bf16[64,4224]{1,0:T(8,128)(2,1)S(1)}, u32[]{:S(2)}, u32[]{:S(2)}) collective-permute-start(bf16[64,4224]{1,0:T(8,128)(2,1)S(1)} %pack.15.mine), channel_id=1, source_target_pairs={{0,8},{1,9},{2,10},{3,11},{4,12},{5,13},{6,14},{7,15},{8,0},{9,1},... | collective-permute-start | bytes 1622024 | tf_op jit(solution)/shard_map/ppermute | solution.py:57
  43.3 7.0 %collective-permute-start.11 = (bf16[64,4096]{1,0:T(8,128)(2,1)S(1)}, bf16[64,4096]{1,0:T(8,128)(2,1)S(1)}, u32[]{:S(2)}, u32[]{:S(2)}) collective-permute-start(bf16[64,4096]{1,0:T(8,128)(2,1)S(1)} %get-tuple-element.42), channel_id=1, source_target_pairs={{0,8},{1,9},{2,10},{3,11},{4,12},{5,13},{6,14},{7,15},{8,0},{9,1},... | collective-permute-start | bytes 1572872 | tf_op jit(solution)/shard_map/ppermute | solution.py:57
  45.6 6.2 %collective-permute-start.18 = (bf16[64,4096]{1,0:T(8,128)(2,1)S(1)}, bf16[64,4096]{1,0:T(8,128)(2,1)S(1)}, u32[]{:S(2)}, u32[]{:S(2)}) collective-permute-start(bf16[64,4096]{1,0:T(8,128)(2,1)S(1)} %get-tuple-element.48), channel_id=1, source_target_pairs={{0,8},{1,9},{2,10},{3,11},{4,12},{5,13},{6,14},{7,15},{8,0},{9,1},... | collective-permute-start | bytes 1572872 | tf_op jit(solution)/shard_map/ppermute | solution.py:57
  47.7 4.9 %collective-permute-start.26 = (bf16[64,4096]{1,0:T(8,128)(2,1)S(1)}, bf16[64,4096]{1,0:T(8,128)(2,1)S(1)}, u32[]{:S(2)}, u32[]{:S(2)}) collective-permute-start(bf16[64,4096]{1,0:T(8,128)(2,1)S(1)} %get-tuple-element.53), channel_id=1, source_target_pairs={{0,8},{1,9},{2,10},{3,11},{4,12},{5,13},{6,14},{7,15},{8,0},{9,1},... | collective-permute-start | bytes 1572872 | tf_op jit(solution)/shard_map/ppermute | solution.py:57
  50.1 4.1 %collective-permute-start.5 = (bf16[64,4096]{1,0:T(8,128)(2,1)S(1)}, bf16[64,4096]{1,0:T(8,128)(2,1)S(1)}, u32[]{:S(2)}, u32[]{:S(2)}) collective-permute-start(bf16[64,4096]{1,0:T(8,128)(2,1)S(1)} %get-tuple-element.36), channel_id=1, source_target_pairs={{0,8},{1,9},{2,10},{3,11},{4,12},{5,13},{6,14},{7,15},{8,0},{9,1},... | collective-permute-start | bytes 1572872 | tf_op jit(solution)/shard_map/ppermute | solution.py:57
  50.4 6.4 %collective-permute-start.12 = (bf16[32,4096]{1,0:T(8,128)(2,1)S(1)}, bf16[32,4096]{1,0:T(8,128)(2,1)S(1)}, u32[]{:S(2)}, u32[]{:S(2)}) collective-permute-start(bf16[32,4096]{1,0:T(8,128)(2,1)S(1)} %core_sum.5), channel_id=1, source_target_pairs={{0,1},{1,0},{2,3},{3,2},{4,5},{5,4},{6,7},{7,6},{8,24},{9,25},{10,... | collective-permute-start | bytes 786440 | tf_op jit(solution)/shard_map/ppermute | solution.py:57
  52.0 8.1 %collective-permute-start.19 = (bf16[32,4096]{1,0:T(8,128)(2,1)S(1)}, bf16[32,4096]{1,0:T(8,128)(2,1)S(1)}, u32[]{:S(2)}, u32[]{:S(2)}) collective-permute-start(bf16[32,4096]{1,0:T(8,128)(2,1)S(1)} %core_sum.6), channel_id=1, source_target_pairs={{0,1},{1,0},{2,3},{3,2},{4,5},{5,4},{6,7},{7,6},{8,24},{9,25},{10,... | collective-permute-start | bytes 786440 | tf_op jit(solution)/shard_map/ppermute | solution.py:57
  52.7 12.6 %collective-permute-start.27 = (bf16[32,4096]{1,0:T(8,128)(2,1)S(1)}, bf16[32,4096]{1,0:T(8,128)(2,1)S(1)}, u32[]{:S(2)}, u32[]{:S(2)}) collective-permute-start(bf16[32,4096]{1,0:T(8,128)(2,1)S(1)} %core_sum.7), channel_id=1, source_target_pairs={{0,1},{1,0},{2,3},{3,2},{4,5},{5,4},{6,7},{7,6},{8,24},{9,25},{10,... | collective-permute-start | bytes 786440 | tf_op jit(solution)/shard_map/ppermute | solution.py:57
  54.3 15.2 %collective-permute-start.6 = (bf16[32,4096]{1,0:T(8,128)(2,1)S(1)}, bf16[32,4096]{1,0:T(8,128)(2,1)S(1)}, u32[]{:S(2)}, u32[]{:S(2)}) collective-permute-start(bf16[32,4096]{1,0:T(8,128)(2,1)S(1)} %core_sum.4), channel_id=1, source_target_pairs={{0,1},{1,0},{2,3},{3,2},{4,5},{5,4},{6,7},{7,6},{8,24},{9,25},{10,... | collective-permute-start | bytes 786440 | tf_op jit(solution)/shard_map/ppermute | solution.py:57
  56.9 14.2 %collective-permute-start.13 = (bf16[16,4096]{1,0:T(8,128)(2,1)S(1)}, bf16[16,4096]{1,0:T(8,128)(2,1)S(1)}, u32[]{:S(2)}, u32[]{:S(2)}) collective-permute-start(bf16[16,4096]{1,0:T(8,128)(2,1)S(1)} %get-tuple-element.45), channel_id=1, source_target_pairs={{0,16},{1,17},{2,18},{3,19},{4,20},{5,21},{6,22},{7,23},{8,9},{9,8... | collective-permute-start | bytes 393224 | tf_op jit(solution)/shard_map/ppermute | solution.py:57
  60.2 11.6 %collective-permute-start.20 = (bf16[16,4096]{1,0:T(8,128)(2,1)S(1)}, bf16[16,4096]{1,0:T(8,128)(2,1)S(1)}, u32[]{:S(2)}, u32[]{:S(2)}) collective-permute-start(bf16[16,4096]{1,0:T(8,128)(2,1)S(1)} %get-tuple-element.51), channel_id=1, source_target_pairs={{0,16},{1,17},{2,18},{3,19},{4,20},{5,21},{6,22},{7,23},{8,9},{9,8... | collective-permute-start | bytes 393224 | tf_op jit(solution)/shard_map/ppermute | solution.py:57
  65.3 9.2 %collective-permute-start.28 = (bf16[16,4096]{1,0:T(8,128)(2,1)S(1)}, bf16[16,4096]{1,0:T(8,128)(2,1)S(1)}, u32[]{:S(2)}, u32[]{:S(2)}) collective-permute-start(bf16[16,4096]{1,0:T(8,128)(2,1)S(1)} %get-tuple-element.56), channel_id=1, source_target_pairs={{0,16},{1,17},{2,18},{3,19},{4,20},{5,21},{6,22},{7,23},{8,9},{9,8... | collective-permute-start | bytes 393224 | tf_op jit(solution)/shard_map/ppermute | solution.py:57
  69.5 5.4 %collective-permute-start.7 = (bf16[16,4096]{1,0:T(8,128)(2,1)S(1)}, bf16[16,4096]{1,0:T(8,128)(2,1)S(1)}, u32[]{:S(2)}, u32[]{:S(2)}) collective-permute-start(bf16[16,4096]{1,0:T(8,128)(2,1)S(1)} %get-tuple-element.39), channel_id=1, source_target_pairs={{0,16},{1,17},{2,18},{3,19},{4,20},{5,21},{6,22},{7,23},{8,9},{9,8... | collective-permute-start | bytes 393224 | tf_op jit(solution)/shard_map/ppermute | solution.py:57
  71.1 5.4 %collective-permute-start.14 = (bf16[16,4096]{1,0:T(8,128)(2,1)S(1)}, bf16[16,4096]{1,0:T(8,128)(2,1)S(1)}, u32[]{:S(2)}, u32[]{:S(2)}) collective-permute-start(bf16[16,4096]{1,0:T(8,128)(2,1)S(1)} %plane_sum.5), channel_id=1, source_target_pairs={{0,2},{1,3},{2,0},{3,1},{4,6},{5,7},{6,4},{7,5},{8,10},{9,11},{10,... | collective-permute-start | bytes 393224 | tf_op jit(solution)/shard_map/ppermute | solution.py:57
  71.8 7.5 %collective-permute-start.21 = (bf16[16,4096]{1,0:T(8,128)(2,1)S(1)}, bf16[16,4096]{1,0:T(8,128)(2,1)S(1)}, u32[]{:S(2)}, u32[]{:S(2)}) collective-permute-start(bf16[16,4096]{1,0:T(8,128)(2,1)S(1)} %plane_sum.6), channel_id=1, source_target_pairs={{0,6},{1,7},{2,4},{3,5},{4,2},{5,3},{6,0},{7,1},{8,14},{9,15},{10,... | collective-permute-start | bytes 393224 | tf_op jit(solution)/shard_map/ppermute | solution.py:57
  74.6 9.6 %collective-permute-start.29 = (bf16[16,4096]{1,0:T(8,128)(2,1)S(1)}, bf16[16,4096]{1,0:T(8,128)(2,1)S(1)}, u32[]{:S(2)}, u32[]{:S(2)}) collective-permute-start(bf16[16,4096]{1,0:T(8,128)(2,1)S(1)} %plane_sum.7), channel_id=1, source_target_pairs={{0,4},{1,5},{2,6},{3,7},{4,0},{5,1},{6,2},{7,3},{8,12},{9,13},{10,... | collective-permute-start | bytes 393224 | tf_op jit(solution)/shard_map/ppermute | solution.py:57

commit v3 on v2

--- a/solution.py
+++ b/solution.py
@@ -34,11 +34,36 @@
 NX, NC, NZ, NY = 2, 2, 4, 2
 TAIL = 128
 PARTS = 3
-ORDER = (0, 1, 3, 2)
-COST = 20
+PIECES = 4
+SEQUENCE = (
+    "pair0",
+    "block3 block1",
+    "stage2",
+    "block2",
+    "pair3 mine0 pair1",
+    "stage1",
+    "stage0",
+    "pair2",
+    "mine3",
+    "mine1",
+    "expert0",
+    "expert3",
+    "expert1",
+    "core0 core3 mine2",
+    "expert2",
+    "core1 far3",
+    "far0",
+    "core2",
+    "near3 far2 far1",
+    "near0",
+    "near2 near1",
+    "fold3",
+    "fold2",
+    "fold1",
+)
+WEIGHT = 3
 
 IN_VMEM = pl.BlockSpec(memory_space=pltpu.VMEM)
-IN_SMEM = pl.BlockSpec(memory_space=pltpu.SMEM)
 IN_HBM = pl.BlockSpec(memory_space=pltpu.HBM)
 
 
@@ -73,19 +98,53 @@
     return moved(value, lambda x, c, z, y: (x, c, z ^ by, y))
 
 
-def kernel(body, name, outs, arrays, scalars=(), scratch=(), far=0, vmem=2, flops=0):
-    placed = [pltpu.with_memory_space_constraint(a, pltpu.HBM) for a in arrays[:far]]
-    placed += [pltpu.with_memory_space_constraint(a, pltpu.VMEM) for a in arrays[far:]]
-    return pl.pallas_call(
-        body,
-        name=name,
-        out_shape=[pltpu.VMEM(shape, dtype) for shape, dtype in outs],
-        in_specs=[IN_SMEM] * len(scalars) + [IN_HBM] * far + [IN_VMEM] * (len(arrays) - far),
-        out_specs=[IN_VMEM] * len(outs),
-        scratch_shapes=list(scratch),
-        compiler_params=pltpu.CompilerParams(vmem_limit_bytes=vmem * 2**20),
-        cost_estimate=pl.CostEstimate(flops=flops, bytes_accessed=0, transcendentals=0),
-    )(*scalars, *placed)
+class Order:
+    def __init__(self):
+        self.mark = ()
+
+    def __call__(self, body, name, outs, arrays, scratch=(), far=0, vmem=2, flops=0, last=False):
+        near = [pltpu.with_memory_space_constraint(a, pltpu.VMEM) for a in (*arrays[far:], *self.mark)]
+        placed = [pltpu.with_memory_space_constraint(a, pltpu.HBM) for a in arrays[:far]]
+        given, skipped, made = len(arrays), len(self.mark), len(outs)
+        marks = [] if last else [((8, 128), F32)]
+
+        def marked(*refs):
+            rest = refs[given + skipped :]
+            for mark in rest[made : made + len(marks)]:
+                mark[...] = jnp.zeros((8, 128), F32)
+            body(*refs[:given], *rest[:made], *rest[made + len(marks) :])
+
+        results = pl.pallas_call(
+            marked,
+            name=name,
+            out_shape=[pltpu.VMEM(shape, dtype) for shape, dtype in (*outs, *marks)],
+            in_specs=[IN_HBM] * far + [IN_VMEM] * len(near),
+            out_specs=[IN_VMEM] * (made + len(marks)),
+            scratch_shapes=list(scratch),
+            compiler_params=pltpu.CompilerParams(vmem_limit_bytes=vmem * 2**20),
+            cost_estimate=pl.CostEstimate(flops=flops, bytes_accessed=0, transcendentals=0),
+        )(*placed, *near)
+        self.mark = results[made:]
+        return results[:made]
+
+
+def together(order, parts, last):
+    def body(*refs):
+        taken = 0
+        made = sum(len(arrays) for _, _, arrays in parts)
+        for part, outs, arrays in parts:
+            part(*refs[taken : taken + len(arrays)], *refs[made : made + len(outs)])
+            taken += len(arrays)
+            made += len(outs)
+
+    all_outs = [out for _, outs, _ in parts for out in outs]
+    all_arrays = [a for _, _, arrays in parts for a in arrays]
+    results = order(body, "sums", all_outs, all_arrays, last=last)
+    split = []
+    for _, outs, _ in parts:
+        split.append(results[: len(outs)])
+        results = results[len(outs) :]
+    return split
 
 
 def label_body(
@@ -127,51 +186,49 @@
     out[:, features:] = tail.astype(BF16)
 
 
-def labelled(tokens, routes, route_gates, placement, swap_flags):
+def labelled(order, tokens, routes, route_gates, placement, swap_flags):
     rows, features = tokens.shape
     arrays = (tokens, routes.T, route_gates.T, placement, swap_flags)
     outs = [((rows, features + TAIL), BF16)]
     scratch = [pltpu.VMEM(a.shape, a.dtype) for a in arrays[:3]]
     scratch += [pltpu.SMEM(a.shape, a.dtype) for a in arrays[3:]]
     scratch.append(pltpu.SemaphoreType.DMA((len(arrays),)))
-    [out] = kernel(label_body, "label", outs, arrays, scratch=scratch, far=len(arrays))
+    [out] = order(label_body, "label", outs, arrays, scratch=scratch, far=len(arrays))
     return out
 
 
-def stage_body(*refs):
-    *pairs, sems = refs
-    count = len(pairs) // 2
-    copies = [pltpu.make_async_copy(pairs[i], pairs[count + i], sems.at[i]) for i in range(count)]
+def stage_body(source, out, sems):
+    size = source.shape[0] // PIECES
+    pieces = [pl.ds(i * size, size) for i in range(PIECES)]
+    copies = [
+        pltpu.make_async_copy(source.at[piece], out.at[piece], sems.at[i])
+        for i, piece in enumerate(pieces)
+    ]
     for copy in copies:
         copy.start()
     for copy in copies:
         copy.wait()
 
 
-def staged(weights):
-    outs = [(w.shape, w.dtype) for w in weights]
-    scratch = [pltpu.SemaphoreType.DMA((len(weights),))]
-    return kernel(stage_body, "stage", outs, weights, scratch=scratch, far=len(weights))
-
-
-def pack_body(groups, *refs):
-    blocks, outs = list(refs[: sum(groups)]), refs[len(refs) - len(groups) :]
-    for out, count in zip(outs, groups):
-        at = 0
-        for _ in range(count):
-            block = blocks.pop(0)
-            out[at : at + block.shape[0], :] = block[...]
-            at += block.shape[0]
-
-
-def packed(*groups, after=()):
-    outs = [((sum(b.shape[0] for b in g), g[0].shape[1]), g[0].dtype) for g in groups]
-    body = functools.partial(pack_body, tuple(len(g) for g in groups))
-    return kernel(body, "pack", outs, [b for g in groups for b in g] + list(after))
+def staged(order, weight):
+    outs = [(weight.shape, weight.dtype)]
+    scratch = [pltpu.SemaphoreType.DMA((PIECES,))]
+    [result] = order(stage_body, "stage", outs, (weight,), scratch, far=1)
+    return result
+
+
+def pack_body(block, received, out):
+    count = block.shape[0]
+    out[:count, :] = block[...]
+    out[count:, :] = received[...]
+
+
+def block_body(received, out):
+    out[...] = received[...]
 
 
 def expert_body(features, experts, mine, others, w_gate, w_up, w_down, *refs):
-    kept, sent, partner, joined, hidden = refs
+    kept, sent, partner_kept, partner_sent, joined, hidden = refs
     count, half = mine.shape[0], kept.shape[0]
     position = lax.axis_index("expert") * NX + lax.div(lax.axis_index("dp"), NC)
     joined[:count, :] = mine[...]
@@ -192,26 +249,26 @@
         value = value.astype(BF16)
         kept[:, columns] = value[:half]
         sent[:, columns] = value[half:count]
-        partner[:, columns] = value[count:]
-
-
-def expert_rows(mine, others, weights, experts):
+        partner_kept[:, columns] = value[count : count + half]
+        partner_sent[:, columns] = value[count + half :]
+
+
+def expert_rows(order, mine, others, weights, experts):
     count, width = mine.shape
     features, hidden_units = weights[0].shape
-    return kernel(
+    return order(
         functools.partial(expert_body, features, experts),
         "expert",
-        [((n, features), BF16) for n in (count // 2, count // 2, count)],
+        [((n, features), BF16) for n in (count // 2,) * 4],
         (mine, others, *weights),
         scratch=[pltpu.VMEM((2 * count, width), BF16), pltpu.VMEM((2 * count, hidden_units), BF16)],
         vmem=6,
-        flops=COST * 12 * count * features * hidden_units,
+        flops=WEIGHT * 12 * count * features * hidden_units,
     )
 
 
 def core_sum_body(sent, received, out):
-    rows = received[sent.shape[0] :, :].astype(F32)
-    out[...] = (sent[...].astype(F32) + rows).astype(BF16)
+    out[...] = (sent[...].astype(F32) + received[...].astype(F32)).astype(BF16)
 
 
 def part_sum_body(kept, from_core, received, mine, passed):
@@ -226,14 +283,6 @@
 
 def plane_sum_body(mine, received, out):
     out[...] = (mine[...] + received[...].astype(F32)).astype(out.dtype)
-
-
-def final_sum_body(*refs):
-    *parts, out = refs
-    total = parts[0][...].astype(F32)
-    for part in parts[1:]:
-        total += part[...].astype(F32)
-    out[...] = total.astype(BF16)
 
 
 def on_device_plane(
@@ -241,33 +290,70 @@
 ):
     rows, features = tokens.shape
     experts = placement.shape[0]
-    weights = gate_weight[0], up_weight[0], down_weight[0]
-    own = labelled(tokens, routes, route_gates, placement, swap_flags)
-    weights = staged(weights)
-    from_z = {k: along_z(own, k) for k in (3, 1, 2)}
-    near = {0: over_first(own)}
-    pair0, block1, block3 = packed([own, near[0]], [from_z[1]], [from_z[3]], after=weights[:1])
-    blocks = {1: block1, 3: block3, 2: from_z[2]}
-    pairs = {0: pair0}
-    mine, others = {}, {}
-    for step in ORDER:
-        if step:
-            [pairs[step]] = packed([blocks[step], over_first(blocks[step])])
-        [mine[step]] = packed([pairs[step], over_second(pairs[step])])
-        others[step] = over_core(mine[step])
-    parts = []
-    for step in ORDER:
-        kept, sent, partner = expert_rows(mine[step], others[step], weights, experts)
-        from_core = over_core(partner)
-        [sent] = kernel(core_sum_body, "core_sum", [(sent.shape, BF16)], (sent, from_core))
-        outs = [((rows, features), F32), ((rows, features), BF16)]
-        arrays = (kept, from_core, over_second(sent))
-        kept, sent = kernel(part_sum_body, "part_sum", outs, arrays)
-        outs = [((rows, features), BF16 if step else F32)]
-        [total] = kernel(plane_sum_body, "plane_sum", outs, (kept, over_first(sent)))
-        parts.append(along_z(total, step) if step else total)
-    [out] = kernel(final_sum_body, "final_sum", [((rows, features), BF16)], parts)
-    return out
+    weights = [gate_weight[0], up_weight[0], down_weight[0]]
+    order = Order()
+    own = labelled(order, tokens, routes, route_gates, placement, swap_flags)
+    block, pair, mine, others = {0: own}, {}, {}, {}
+    kept, sent, more_kept, more_sent, total = {}, {}, {}, {}, {}
+    steps = range(1, NZ)
+    from_z = {step: along_z(own, step) for step in steps}
+    from_first = {0: over_first(own)}
+    from_second = {}
+
+    def inputs(kind, step):
+        wide = features + TAIL
+        if kind == "block":
+            return block_body, [((rows, wide), BF16)], [from_z[step]]
+        if kind == "pair":
+            return pack_body, [((2 * rows, wide), BF16)], [block[step], from_first[step]]
+        if kind == "mine":
+            return pack_body, [((4 * rows, wide), BF16)], [pair[step], from_second[step]]
+        if kind == "core":
+            return core_sum_body, [((2 * rows, features), BF16)], [sent[step], more_sent[step]]
+        if kind == "far":
+            outs = [((rows, features), F32), ((rows, features), BF16)]
+            return part_sum_body, outs, [kept[step], more_kept[step], sent[step]]
+        if kind == "near":
+            outs = [((rows, features), BF16 if step else F32)]
+            return plane_sum_body, outs, [kept[step], sent[step]]
+        outs = [((rows, features), BF16 if step == folds[-1] else F32)]
+        return plane_sum_body, outs, [total[0], total[step]]
+
+    def passed_on(kind, step, results):
+        if kind == "block":
+            [block[step]] = results
+            from_first[step] = over_first(block[step])
+        elif kind == "pair":
+            [pair[step]] = results
+            from_second[step] = over_second(pair[step])
+        elif kind == "mine":
+            [mine[step]] = results
+            others[step] = over_core(mine[step])
+        elif kind == "core":
+            sent[step] = over_second(results[0])
+        elif kind == "far":
+            kept[step], sent[step] = results[0], over_first(results[1])
+        elif kind == "near":
+            total[step] = along_z(results[0], step) if step else results[0]
+        else:
+            [total[0]] = results
+
+    folds = [int(name[-1]) for group in SEQUENCE for name in group.split() if name[:-1] == "fold"]
+    for group in SEQUENCE:
+        names = [(name[:-1], int(name[-1])) for name in group.split()]
+        kind, step = names[0]
+        if kind == "stage":
+            weights[step] = staged(order, weights[step])
+        elif kind == "expert":
+            results = expert_rows(order, mine[step], others[step], weights, experts)
+            kept[step], sent[step], more_kept[step], more_sent[step] = results
+            more_sent[step] = over_core(more_sent[step])
+            more_kept[step] = over_core(more_kept[step])
+        else:
+            results = together(order, [inputs(*name) for name in names], group is SEQUENCE[-1])
+            for name, result in zip(names, results):
+                passed_on(*name, result)
+    return total[0]
 
 
 def on_device_lanes(

time: 85.1 us -> 74.9 us (0.88)
  waiting for transfers between devices: 37.2 us -> 27.1 us
  starting transfers between devices: 33.3 us -> 31.1 us
  Pallas kernels: 13.6 us -> 15.6 us
    ppermute x30 -> x34, waiting for transfers between devices: 37.2 us -> 27.1 us  [moved(): return lax.ppermute(value, MESH_AXES, pairs)]
    ppermute x30 -> x34, starting transfers between devices: 33.3 us -> 31.1 us  [moved(): return lax.ppermute(value, MESH_AXES, pairs)]
    pallas_call x27 -> x25, Pallas kernels: 13.6 us -> 15.6 us  [__call__(): pl.pallas_call(marked, name=name, out_shape=[pltpu.VMEM(shape, dtype) for...]
  transfers between devices with their start and end apart: 30 -> 34, of which waited for: 14 -> 15; matrix products, arithmetic and copies ran while one was open for 0% -> 0% of each run, Pallas kernels for 14% -> 19%
where the time goes in v3:
time: 74.9 us; the launch traced here: 74.8 us
  starting transfers between devices  31.1 us (42%)
  waiting for transfers between devices  27.1 us (36%)
  Pallas kernels  15.6 us (21%)
    ppermute x34, starting transfers between devices, moved(): return lax.ppermute(value, MESH_AXES, pairs)  31.1 us
    ppermute x34, waiting for transfers between devices, moved(): return lax.ppermute(value, MESH_AXES, pairs)  27.1 us
    pallas_call x25, Pallas kernels, __call__(): pl.pallas_call(marked, name=name, out_shape=[pltpu.VMEM(shape, dtype) for...  15.6 us
  transfers between devices with their start and end apart: 34, of which 15 were waited for; matrix products, arithmetic and copies ran while one was open for 0% of the time, Pallas kernels for 19%

profile of v3, /device:TPU:0, one launch (start us, length us, event | category | flops | bytes accessed | tf_op | source)
XLA Modules:
  0.0 74.8 jit_solution(4969801961847584540)
XLA Ops:
  0.0 1.2 %label.1 = (bf16[16,4224]{1,0:T(8,128)(2,1)S(1)}, f32[8,128]{1,0:T(8,128)S(1)}) custom-call(bf16[16,4096]{1,0:T(8,128)(2,1)} %refs_0_.1, s32[8,16]{1,0:T(8,128)} %bitcast.8, f32[8,16]{1,0:T(8,128)} %bitcast.9, s32[16]{0:T(128)} %refs_3_.1, s32[16]{0:T(128)} %refs_4_.1), custom_call_target="tpu_custom_call" | custom-call | tf_op jit(solution)/shard_map/label/pallas_call | solution.py:117
  1.2 3.0 %collective-permute-start.2 = (bf16[16,4224]{1,0:T(8,128)(2,1)S(1)}, bf16[16,4224]{1,0:T(8,128)(2,1)S(1)}, u32[]{:S(2)}, u32[]{:S(2)}) collective-permute-start(bf16[16,4224]{1,0:T(8,128)(2,1)S(1)} %get-tuple-element.78.refs_0_), channel_id=1, source_target_pairs={{0,16},{1,17},{2,18},{3,19},{4,20},{5,21},{6,22},{7,23},{8,9},{9,8... | collective-permute-start | bytes 405512 | tf_op jit(solution)/shard_map/ppermute | solution.py:82
  4.2 3.6 %collective-permute-start = (bf16[16,4224]{1,0:T(8,128)(2,1)S(1)}, bf16[16,4224]{1,0:T(8,128)(2,1)S(1)}, u32[]{:S(2)}, u32[]{:S(2)}) collective-permute-start(bf16[16,4224]{1,0:T(8,128)(2,1)S(1)} %get-tuple-element.78.refs_0_), channel_id=1, source_target_pairs={{0,6},{1,7},{2,4},{3,5},{4,2},{5,3},{6,0},{7,1},{8,14},{9,15},{10,... | collective-permute-start | bytes 405512 | tf_op jit(solution)/shard_map/ppermute | solution.py:82
  7.8 1.6 %collective-permute-start.4 = (bf16[32,4224]{1,0:T(8,128)(2,1)S(1)}, bf16[32,4224]{1,0:T(8,128)(2,1)S(1)}, u32[]{:S(2)}, u32[]{:S(2)}) collective-permute-start(bf16[32,4224]{1,0:T(8,128)(2,1)S(1)} %get-tuple-element.82.refs_2_), channel_id=1, source_target_pairs={{0,1},{1,0},{2,3},{3,2},{4,5},{5,4},{6,7},{7,6},{8,24},{9,25},{10,... | collective-permute-start | bytes 811016 | tf_op jit(solution)/shard_map/ppermute | solution.py:82
  9.4 2.5 %collective-permute-start.6 = (bf16[16,4224]{1,0:T(8,128)(2,1)S(1)}, bf16[16,4224]{1,0:T(8,128)(2,1)S(1)}, u32[]{:S(2)}, u32[]{:S(2)}) collective-permute-start(bf16[16,4224]{1,0:T(8,128)(2,1)S(1)} %get-tuple-element.78.refs_0_), channel_id=1, source_target_pairs={{0,4},{1,5},{2,6},{3,7},{4,0},{5,1},{6,2},{7,3},{8,12},{9,13},{10,... | collective-permute-start | bytes 405512 | tf_op jit(solution)/shard_map/ppermute | solution.py:82
  11.9 0.6 collective-permute-done.refs_0_
  12.5 2.6 %collective-permute-done.1.refs_1_ = bf16[16,4224]{1,0:T(8,128)(2,1)S(1)} collective-permute-done((bf16[16,4224]{1,0:T(8,128)(2,1)S(1)}, bf16[16,4224]{1,0:T(8,128)(2,1)S(1)}, u32[]{:S(2)}, u32[]{:S(2)}) %collective-permute-start.1) | collective-permute-done | bytes 135200 | tf_op jit(solution)/shard_map/ppermute | solution.py:82
  15.2 1.6 %collective-permute-start.3 = (bf16[16,4224]{1,0:T(8,128)(2,1)S(1)}, bf16[16,4224]{1,0:T(8,128)(2,1)S(1)}, u32[]{:S(2)}, u32[]{:S(2)}) collective-permute-start(bf16[16,4224]{1,0:T(8,128)(2,1)S(1)} %get-tuple-element.81.refs_0_), channel_id=1, source_target_pairs={{0,16},{1,17},{2,18},{3,19},{4,20},{5,21},{6,22},{7,23},{8,9},{9,8... | collective-permute-start | bytes 405512 | tf_op jit(solution)/shard_map/ppermute | solution.py:82
  16.7 0.5 collective-permute-start.5
  17.3 1.9 %stage.3 = (bf16[384,4096]{1,0:T(8,128)(2,1)S(1)}, f32[8,128]{1,0:T(8,128)S(1)}) custom-call(bf16[384,4096]{1,0:T(8,128)(2,1)} %bitcast.5, f32[8,128]{1,0:T(8,128)S(1)} %get-tuple-element.84.refs_1_), custom_call_target="tpu_custom_call" | custom-call | tf_op jit(solution)/shard_map/stage/pallas_call | solution.py:117
  19.2 1.1 %collective-permute-done.3.refs_1_ = bf16[16,4224]{1,0:T(8,128)(2,1)S(1)} collective-permute-done((bf16[16,4224]{1,0:T(8,128)(2,1)S(1)}, bf16[16,4224]{1,0:T(8,128)(2,1)S(1)}, u32[]{:S(2)}, u32[]{:S(2)}) %collective-permute-start.3) | collective-permute-done | bytes 135200 | tf_op jit(solution)/shard_map/ppermute | solution.py:82
  20.2 1.5 %collective-permute-done.5.refs_5_ = bf16[16,4224]{1,0:T(8,128)(2,1)S(1)} collective-permute-done((bf16[16,4224]{1,0:T(8,128)(2,1)S(1)}, bf16[16,4224]{1,0:T(8,128)(2,1)S(1)}, u32[]{:S(2)}, u32[]{:S(2)}) %collective-permute-start.5) | collective-permute-done | bytes 135200 | tf_op jit(solution)/shard_map/ppermute | solution.py:82
  21.9 0.6 collective-permute-start.9
  22.5 1.3 %collective-permute-start.10 = (bf16[16,4224]{1,0:T(8,128)(2,1)S(1)}, bf16[16,4224]{1,0:T(8,128)(2,1)S(1)}, u32[]{:S(2)}, u32[]{:S(2)}) collective-permute-start(bf16[16,4224]{1,0:T(8,128)(2,1)S(1)} %get-tuple-element.95.refs_0_), channel_id=1, source_target_pairs={{0,16},{1,17},{2,18},{3,19},{4,20},{5,21},{6,22},{7,23},{8,9},{9,8... | collective-permute-start | bytes 405512 | tf_op jit(solution)/shard_map/ppermute | solution.py:82
  23.7 1.7 %collective-permute-start.8 = (bf16[32,4224]{1,0:T(8,128)(2,1)S(1)}, bf16[32,4224]{1,0:T(8,128)(2,1)S(1)}, u32[]{:S(2)}, u32[]{:S(2)}) collective-permute-start(bf16[32,4224]{1,0:T(8,128)(2,1)S(1)} %get-tuple-element.93.refs_0_), channel_id=1, source_target_pairs={{0,1},{1,0},{2,3},{3,2},{4,5},{5,4},{6,7},{7,6},{8,24},{9,25},{10,... | collective-permute-start | bytes 811016 | tf_op jit(solution)/shard_map/ppermute | solution.py:82
  25.4 1.9 %stage.4 = (bf16[4096,384]{1,0:T(8,128)(2,1)S(1)}, f32[8,128]{1,0:T(8,128)S(1)}) custom-call(bf16[4096,384]{1,0:T(8,128)(2,1)} %bitcast.6, f32[8,128]{1,0:T(8,128)S(1)} %get-tuple-element.88.refs_1_), custom_call_target="tpu_custom_call" | custom-call | tf_op jit(solution)/shard_map/stage/pallas_call | solution.py:117
  27.3 1.9 %stage.5 = (bf16[4096,384]{1,0:T(8,128)(2,1)S(1)}, f32[8,128]{1,0:T(8,128)S(1)}) custom-call(bf16[4096,384]{1,0:T(8,128)(2,1)} %bitcast.7, f32[8,128]{1,0:T(8,128)S(1)} %get-tuple-element.89.refs_1_), custom_call_target="tpu_custom_call" | custom-call | tf_op jit(solution)/shard_map/stage/pallas_call | solution.py:117
  29.2 0.6 collective-permute-done.9.refs_1_
  30.0 0.7 %collective-permute-start.15 = (bf16[32,4224]{1,0:T(8,128)(2,1)S(1)}, bf16[32,4224]{1,0:T(8,128)(2,1)S(1)}, u32[]{:S(2)}, u32[]{:S(2)}) collective-permute-start(bf16[32,4224]{1,0:T(8,128)(2,1)S(1)} %get-tuple-element.108.refs_4_), channel_id=1, source_target_pairs={{0,1},{1,0},{2,3},{3,2},{4,5},{5,4},{6,7},{7,6},{8,24},{9,25},{10,... | collective-permute-start | bytes 811016 | tf_op jit(solution)/shard_map/ppermute | solution.py:82
  30.7 2.0 %collective-permute-done.8.refs_1_ = bf16[32,4224]{1,0:T(8,128)(2,1)S(1)} collective-permute-done((bf16[32,4224]{1,0:T(8,128)(2,1)S(1)}, bf16[32,4224]{1,0:T(8,128)(2,1)S(1)}, u32[]{:S(2)}, u32[]{:S(2)}) %collective-permute-start.8) | collective-permute-done | bytes 270368 | tf_op jit(solution)/shard_map/ppermute | solution.py:82
  32.9 1.9 %expert.4 = (bf16[32,4096]{1,0:T(8,128)(2,1)S(1)}, bf16[32,4096]{1,0:T(8,128)(2,1)S(1)}, bf16[32,4096]{1,0:T(8,128)(2,1)S(1)}, bf16[32,4096]{1,0:T(8,128)(2,1)S(1)}, f32[8,128]{1,0:T(8,128)S(1)}) custom-call(bf16[64,4224]{1,0:T(8,128)(2,1)S(1)} %get-tuple-element.87.refs_0_, bf16[64,4224]{1,0:T(8,128)(2,1)S(1)} %collective-permute-done.7.refs_1_, ...), custom_call_target="tpu_custom_call" | custom-call | flops 3623878656 | tf_op jit(solution)/shard_map/expert/pallas_call | solution.py:117
  34.8 0.6 collective-permute-start.12
  35.4 1.9 %expert.5 = (bf16[32,4096]{1,0:T(8,128)(2,1)S(1)}, bf16[32,4096]{1,0:T(8,128)(2,1)S(1)}, bf16[32,4096]{1,0:T(8,128)(2,1)S(1)}, bf16[32,4096]{1,0:T(8,128)(2,1)S(1)}, f32[8,128]{1,0:T(8,128)S(1)}) custom-call(bf16[64,4224]{1,0:T(8,128)(2,1)S(1)} %get-tuple-element.104.refs_0_, bf16[64,4224]{1,0:T(8,128)(2,1)S(1)} %collective-permute-done.13.refs_1_, ...), custom_call_target="tpu_custom_call" | custom-call | flops 3623878656 | tf_op jit(solution)/shard_map/expert/pallas_call | solution.py:117
  37.4 1.9 %expert.6 = (bf16[32,4096]{1,0:T(8,128)(2,1)S(1)}, bf16[32,4096]{1,0:T(8,128)(2,1)S(1)}, bf16[32,4096]{1,0:T(8,128)(2,1)S(1)}, bf16[32,4096]{1,0:T(8,128)(2,1)S(1)}, f32[8,128]{1,0:T(8,128)S(1)}) custom-call(bf16[64,4224]{1,0:T(8,128)(2,1)S(1)} %get-tuple-element.109.refs_0_, bf16[64,4224]{1,0:T(8,128)(2,1)S(1)} %collective-permute-done.16.refs_1_, ...), custom_call_target="tpu_custom_call" | custom-call | flops 3623878656 | tf_op jit(solution)/shard_map/expert/pallas_call | solution.py:117
  39.5 0.5 collective-permute-start.21
  40.2 0.4 collective-permute-start.18
  40.7 0.5 collective-permute-start.20
  41.2 0.5 collective-permute-done.21.refs_1_
  41.6 1.1 %collective-permute-start.17 = (bf16[32,4096]{1,0:T(8,128)(2,1)S(1)}, bf16[32,4096]{1,0:T(8,128)(2,1)S(1)}, u32[]{:S(2)}, u32[]{:S(2)}) collective-permute-start(bf16[32,4096]{1,0:T(8,128)(2,1)S(1)} %get-tuple-element.112), channel_id=1, source_target_pairs={{0,1},{1,0},{2,3},{3,2},{4,5},{5,4},{6,7},{7,6},{8,24},{9,25},{10,... | collective-permute-start | bytes 786440 | tf_op jit(solution)/shard_map/ppermute | solution.py:82
  42.7 1.9 %expert.7 = (bf16[32,4096]{1,0:T(8,128)(2,1)S(1)}, bf16[32,4096]{1,0:T(8,128)(2,1)S(1)}, bf16[32,4096]{1,0:T(8,128)(2,1)S(1)}, bf16[32,4096]{1,0:T(8,128)(2,1)S(1)}, f32[8,128]{1,0:T(8,128)S(1)}) custom-call(bf16[64,4224]{1,0:T(8,128)(2,1)S(1)} %get-tuple-element.118.refs_0_, bf16[64,4224]{1,0:T(8,128)(2,1)S(1)} %collective-permute-done.21.refs_1_, ...), custom_call_target="tpu_custom_call" | custom-call | flops 3623878656 | tf_op jit(solution)/shard_map/expert/pallas_call | solution.py:117
  45.3 1.8 %collective-permute-done.20.refs_4_ = bf16[32,4096]{1,0:T(8,128)(2,1)S(1)} collective-permute-done((bf16[32,4096]{1,0:T(8,128)(2,1)S(1)}, bf16[32,4096]{1,0:T(8,128)(2,1)S(1)}, u32[]{:S(2)}, u32[]{:S(2)}) %collective-permute-start.20) | collective-permute-done | bytes 262176 | tf_op jit(solution)/shard_map/ppermute | solution.py:82
  47.2 0.6 collective-permute-start.28
  47.8 2.1 %collective-permute-done.17.refs_2_ = bf16[32,4096]{1,0:T(8,128)(2,1)S(1)} collective-permute-done((bf16[32,4096]{1,0:T(8,128)(2,1)S(1)}, bf16[32,4096]{1,0:T(8,128)(2,1)S(1)}, u32[]{:S(2)}, u32[]{:S(2)}) %collective-permute-start.17) | collective-permute-done | bytes 262176 | tf_op jit(solution)/shard_map/ppermute | solution.py:82
  50.0 0.6 collective-permute-start.26
  50.6 1.2 %collective-permute-start.23 = (bf16[16,4096]{1,0:T(8,128)(2,1)S(1)}, bf16[16,4096]{1,0:T(8,128)(2,1)S(1)}, u32[]{:S(2)}, u32[]{:S(2)}) collective-permute-start(bf16[16,4096]{1,0:T(8,128)(2,1)S(1)} %get-tuple-element.125), channel_id=1, source_target_pairs={{0,16},{1,17},{2,18},{3,19},{4,20},{5,21},{6,22},{7,23},{8,9},{9,8... | collective-permute-start | bytes 393224 | tf_op jit(solution)/shard_map/ppermute | solution.py:82
  51.8 0.8 %collective-permute-start.22 = (bf16[16,4096]{1,0:T(8,128)(2,1)S(1)}, bf16[16,4096]{1,0:T(8,128)(2,1)S(1)}, u32[]{:S(2)}, u32[]{:S(2)}) collective-permute-start(bf16[16,4096]{1,0:T(8,128)(2,1)S(1)} %get-tuple-element.123), channel_id=1, source_target_pairs={{0,16},{1,17},{2,18},{3,19},{4,20},{5,21},{6,22},{7,23},{8,9},{9,8... | collective-permute-start | bytes 393224 | tf_op jit(solution)/shard_map/ppermute | solution.py:82
  52.6 3.8 %collective-permute-done.23.refs_1_ = bf16[16,4096]{1,0:T(8,128)(2,1)S(1)} collective-permute-done((bf16[16,4096]{1,0:T(8,128)(2,1)S(1)}, bf16[16,4096]{1,0:T(8,128)(2,1)S(1)}, u32[]{:S(2)}, u32[]{:S(2)}) %collective-permute-start.23) | collective-permute-done | bytes 131104 | tf_op jit(solution)/shard_map/ppermute | solution.py:82
  56.5 2.9 %collective-permute-done.26.refs_4_ = bf16[32,4096]{1,0:T(8,128)(2,1)S(1)} collective-permute-done((bf16[32,4096]{1,0:T(8,128)(2,1)S(1)}, bf16[32,4096]{1,0:T(8,128)(2,1)S(1)}, u32[]{:S(2)}, u32[]{:S(2)}) %collective-permute-start.26) | collective-permute-done | bytes 262176 | tf_op jit(solution)/shard_map/ppermute | solution.py:82
  59.6 1.5 %collective-permute-start.30 = (bf16[16,4096]{1,0:T(8,128)(2,1)S(1)}, bf16[16,4096]{1,0:T(8,128)(2,1)S(1)}, u32[]{:S(2)}, u32[]{:S(2)}) collective-permute-start(bf16[16,4096]{1,0:T(8,128)(2,1)S(1)} %get-tuple-element.140), channel_id=1, source_target_pairs={{0,16},{1,17},{2,18},{3,19},{4,20},{5,21},{6,22},{7,23},{8,9},{9,8... | collective-permute-start | bytes 393224 | tf_op jit(solution)/shard_map/ppermute | solution.py:82
  61.0 0.6 collective-permute-start.31
  61.7 2.0 %collective-permute-start.29 = (bf16[16,4096]{1,0:T(8,128)(2,1)S(1)}, bf16[16,4096]{1,0:T(8,128)(2,1)S(1)}, u32[]{:S(2)}, u32[]{:S(2)}) collective-permute-start(bf16[16,4096]{1,0:T(8,128)(2,1)S(1)} %get-tuple-element.138), channel_id=1, source_target_pairs={{0,6},{1,7},{2,4},{3,5},{4,2},{5,3},{6,0},{7,1},{8,14},{9,15},{10,... | collective-permute-start | bytes 393224 | tf_op jit(solution)/shard_map/ppermute | solution.py:82
  63.7 0.9 %collective-permute-done.30.refs_1_ = bf16[16,4096]{1,0:T(8,128)(2,1)S(1)} collective-permute-done((bf16[16,4096]{1,0:T(8,128)(2,1)S(1)}, bf16[16,4096]{1,0:T(8,128)(2,1)S(1)}, u32[]{:S(2)}, u32[]{:S(2)}) %collective-permute-start.30) | collective-permute-done | bytes 131104 | tf_op jit(solution)/shard_map/ppermute | solution.py:82
  64.6 1.4 %collective-permute-done.31.refs_3_ = bf16[16,4096]{1,0:T(8,128)(2,1)S(1)} collective-permute-done((bf16[16,4096]{1,0:T(8,128)(2,1)S(1)}, bf16[16,4096]{1,0:T(8,128)(2,1)S(1)}, u32[]{:S(2)}, u32[]{:S(2)}) %collective-permute-start.31) | collective-permute-done | bytes 131104 | tf_op jit(solution)/shard_map/ppermute | solution.py:82
  66.1 0.6 collective-permute-start.32
  66.7 2.0 %collective-permute-start.33 = (bf16[16,4096]{1,0:T(8,128)(2,1)S(1)}, bf16[16,4096]{1,0:T(8,128)(2,1)S(1)}, u32[]{:S(2)}, u32[]{:S(2)}) collective-permute-start(bf16[16,4096]{1,0:T(8,128)(2,1)S(1)} %get-tuple-element.149), channel_id=1, source_target_pairs={{0,2},{1,3},{2,0},{3,1},{4,6},{5,7},{6,4},{7,5},{8,10},{9,11},{10,... | collective-permute-start | bytes 393224 | tf_op jit(solution)/shard_map/ppermute | solution.py:82
  68.7 1.2 %collective-permute-done.29.refs_1_ = bf16[16,4096]{1,0:T(8,128)(2,1)S(1)} collective-permute-done((bf16[16,4096]{1,0:T(8,128)(2,1)S(1)}, bf16[16,4096]{1,0:T(8,128)(2,1)S(1)}, u32[]{:S(2)}, u32[]{:S(2)}) %collective-permute-start.29) | collective-permute-done | bytes 131104 | tf_op jit(solution)/shard_map/ppermute | solution.py:82
  69.9 4.1 %collective-permute-done.32.refs_1_ = bf16[16,4096]{1,0:T(8,128)(2,1)S(1)} collective-permute-done((bf16[16,4096]{1,0:T(8,128)(2,1)S(1)}, bf16[16,4096]{1,0:T(8,128)(2,1)S(1)}, u32[]{:S(2)}, u32[]{:S(2)}) %collective-permute-start.32) | collective-permute-done | bytes 131104 | tf_op jit(solution)/shard_map/ppermute | solution.py:82
  74.1 0.7 copy.9
  (46 shorter events, 2.2 us)
Async XLA Ops:
  1.2 6.6 %collective-permute-start.2 = (bf16[16,4224]{1,0:T(8,128)(2,1)S(1)}, bf16[16,4224]{1,0:T(8,128)(2,1)S(1)}, u32[]{:S(2)}, u32[]{:S(2)}) collective-permute-start(bf16[16,4224]{1,0:T(8,128)(2,1)S(1)} %get-tuple-element.78.refs_0_), channel_id=1, source_target_pairs={{0,16},{1,17},{2,18},{3,19},{4,20},{5,21},{6,22},{7,23},{8,9},{9,8... | collective-permute-start | bytes 405512 | tf_op jit(solution)/shard_map/ppermute | solution.py:82
  4.2 8.3 %collective-permute-start = (bf16[16,4224]{1,0:T(8,128)(2,1)S(1)}, bf16[16,4224]{1,0:T(8,128)(2,1)S(1)}, u32[]{:S(2)}, u32[]{:S(2)}) collective-permute-start(bf16[16,4224]{1,0:T(8,128)(2,1)S(1)} %get-tuple-element.78.refs_0_), channel_id=1, source_target_pairs={{0,6},{1,7},{2,4},{3,5},{4,2},{5,3},{6,0},{7,1},{8,14},{9,15},{10,... | collective-permute-start | bytes 405512 | tf_op jit(solution)/shard_map/ppermute | solution.py:82
  7.8 7.3 %collective-permute-start.1 = (bf16[16,4224]{1,0:T(8,128)(2,1)S(1)}, bf16[16,4224]{1,0:T(8,128)(2,1)S(1)}, u32[]{:S(2)}, u32[]{:S(2)}) collective-permute-start(bf16[16,4224]{1,0:T(8,128)(2,1)S(1)} %get-tuple-element.78.refs_0_), channel_id=1, source_target_pairs={{0,2},{1,3},{2,0},{3,1},{4,6},{5,7},{6,4},{7,5},{8,10},{9,11},{10,... | collective-permute-start | bytes 405512 | tf_op jit(solution)/shard_map/ppermute | solution.py:82
  7.8 13.9 %collective-permute-start.4 = (bf16[32,4224]{1,0:T(8,128)(2,1)S(1)}, bf16[32,4224]{1,0:T(8,128)(2,1)S(1)}, u32[]{:S(2)}, u32[]{:S(2)}) collective-permute-start(bf16[32,4224]{1,0:T(8,128)(2,1)S(1)} %get-tuple-element.82.refs_2_), channel_id=1, source_target_pairs={{0,1},{1,0},{2,3},{3,2},{4,5},{5,4},{6,7},{7,6},{8,24},{9,25},{10,... | collective-permute-start | bytes 811016 | tf_op jit(solution)/shard_map/ppermute | solution.py:82
  9.4 9.7 %collective-permute-start.6 = (bf16[16,4224]{1,0:T(8,128)(2,1)S(1)}, bf16[16,4224]{1,0:T(8,128)(2,1)S(1)}, u32[]{:S(2)}, u32[]{:S(2)}) collective-permute-start(bf16[16,4224]{1,0:T(8,128)(2,1)S(1)} %get-tuple-element.78.refs_0_), channel_id=1, source_target_pairs={{0,4},{1,5},{2,6},{3,7},{4,0},{5,1},{6,2},{7,3},{8,12},{9,13},{10,... | collective-permute-start | bytes 405512 | tf_op jit(solution)/shard_map/ppermute | solution.py:82
  15.2 5.1 %collective-permute-start.3 = (bf16[16,4224]{1,0:T(8,128)(2,1)S(1)}, bf16[16,4224]{1,0:T(8,128)(2,1)S(1)}, u32[]{:S(2)}, u32[]{:S(2)}) collective-permute-start(bf16[16,4224]{1,0:T(8,128)(2,1)S(1)} %get-tuple-element.81.refs_0_), channel_id=1, source_target_pairs={{0,16},{1,17},{2,18},{3,19},{4,20},{5,21},{6,22},{7,23},{8,9},{9,8... | collective-permute-start | bytes 405512 | tf_op jit(solution)/shard_map/ppermute | solution.py:82
  16.7 5.0 %collective-permute-start.5 = (bf16[16,4224]{1,0:T(8,128)(2,1)S(1)}, bf16[16,4224]{1,0:T(8,128)(2,1)S(1)}, u32[]{:S(2)}, u32[]{:S(2)}) collective-permute-start(bf16[16,4224]{1,0:T(8,128)(2,1)S(1)} %get-tuple-element.83.refs_4_), channel_id=1, source_target_pairs={{0,16},{1,17},{2,18},{3,19},{4,20},{5,21},{6,22},{7,23},{8,9},{9,8... | collective-permute-start | bytes 405512 | tf_op jit(solution)/shard_map/ppermute | solution.py:82
  21.8 11.1 %collective-permute-start.7 = (bf16[64,4224]{1,0:T(8,128)(2,1)S(1)}, bf16[64,4224]{1,0:T(8,128)(2,1)S(1)}, u32[]{:S(2)}, u32[]{:S(2)}) collective-permute-start(bf16[64,4224]{1,0:T(8,128)(2,1)S(1)} %get-tuple-element.87.refs_0_), channel_id=1, source_target_pairs={{0,8},{1,9},{2,10},{3,11},{4,12},{5,13},{6,14},{7,15},{8,0},{9,1},... | collective-permute-start | bytes 1622024 | tf_op jit(solution)/shard_map/ppermute | solution.py:82
  21.9 8.0 %collective-permute-start.9 = (bf16[32,4224]{1,0:T(8,128)(2,1)S(1)}, bf16[32,4224]{1,0:T(8,128)(2,1)S(1)}, u32[]{:S(2)}, u32[]{:S(2)}) collective-permute-start(bf16[32,4224]{1,0:T(8,128)(2,1)S(1)} %get-tuple-element.94.refs_0_), channel_id=1, source_target_pairs={{0,1},{1,0},{2,3},{3,2},{4,5},{5,4},{6,7},{7,6},{8,24},{9,25},{10,... | collective-permute-start | bytes 811016 | tf_op jit(solution)/shard_map/ppermute | solution.py:82
  22.5 6.7 %collective-permute-start.10 = (bf16[16,4224]{1,0:T(8,128)(2,1)S(1)}, bf16[16,4224]{1,0:T(8,128)(2,1)S(1)}, u32[]{:S(2)}, u32[]{:S(2)}) collective-permute-start(bf16[16,4224]{1,0:T(8,128)(2,1)S(1)} %get-tuple-element.95.refs_0_), channel_id=1, source_target_pairs={{0,16},{1,17},{2,18},{3,19},{4,20},{5,21},{6,22},{7,23},{8,9},{9,8... | collective-permute-start | bytes 405512 | tf_op jit(solution)/shard_map/ppermute | solution.py:82
  23.7 9.0 %collective-permute-start.8 = (bf16[32,4224]{1,0:T(8,128)(2,1)S(1)}, bf16[32,4224]{1,0:T(8,128)(2,1)S(1)}, u32[]{:S(2)}, u32[]{:S(2)}) collective-permute-start(bf16[32,4224]{1,0:T(8,128)(2,1)S(1)} %get-tuple-element.93.refs_0_), channel_id=1, source_target_pairs={{0,1},{1,0},{2,3},{3,2},{4,5},{5,4},{6,7},{7,6},{8,24},{9,25},{10,... | collective-permute-start | bytes 811016 | tf_op jit(solution)/shard_map/ppermute | solution.py:82
  29.9 5.5 %collective-permute-start.13 = (bf16[64,4224]{1,0:T(8,128)(2,1)S(1)}, bf16[64,4224]{1,0:T(8,128)(2,1)S(1)}, u32[]{:S(2)}, u32[]{:S(2)}) collective-permute-start(bf16[64,4224]{1,0:T(8,128)(2,1)S(1)} %get-tuple-element.104.refs_0_), channel_id=1, source_target_pairs={{0,8},{1,9},{2,10},{3,11},{4,12},{5,13},{6,14},{7,15},{8,0},{9,1},... | collective-permute-start | bytes 1622024 | tf_op jit(solution)/shard_map/ppermute | solution.py:82
  30.0 9.4 %collective-permute-start.15 = (bf16[32,4224]{1,0:T(8,128)(2,1)S(1)}, bf16[32,4224]{1,0:T(8,128)(2,1)S(1)}, u32[]{:S(2)}, u32[]{:S(2)}) collective-permute-start(bf16[32,4224]{1,0:T(8,128)(2,1)S(1)} %get-tuple-element.108.refs_4_), channel_id=1, source_target_pairs={{0,1},{1,0},{2,3},{3,2},{4,5},{5,4},{6,7},{7,6},{8,24},{9,25},{10,... | collective-permute-start | bytes 811016 | tf_op jit(solution)/shard_map/ppermute | solution.py:82
  32.8 4.6 %collective-permute-start.16 = (bf16[64,4224]{1,0:T(8,128)(2,1)S(1)}, bf16[64,4224]{1,0:T(8,128)(2,1)S(1)}, u32[]{:S(2)}, u32[]{:S(2)}) collective-permute-start(bf16[64,4224]{1,0:T(8,128)(2,1)S(1)} %get-tuple-element.109.refs_0_), channel_id=1, source_target_pairs={{0,8},{1,9},{2,10},{3,11},{4,12},{5,13},{6,14},{7,15},{8,0},{9,1},... | collective-permute-start | bytes 1622024 | tf_op jit(solution)/shard_map/ppermute | solution.py:82
  34.8 4.5 %collective-permute-start.12 = (bf16[32,4096]{1,0:T(8,128)(2,1)S(1)}, bf16[32,4096]{1,0:T(8,128)(2,1)S(1)}, u32[]{:S(2)}, u32[]{:S(2)}) collective-permute-start(bf16[32,4096]{1,0:T(8,128)(2,1)S(1)} %get-tuple-element.103), channel_id=1, source_target_pairs={{0,8},{1,9},{2,10},{3,11},{4,12},{5,13},{6,14},{7,15},{8,0},{9,1},... | collective-permute-start | bytes 786440 | tf_op jit(solution)/shard_map/ppermute | solution.py:82
  37.3 2.1 %collective-permute-start.14 = (bf16[32,4096]{1,0:T(8,128)(2,1)S(1)}, bf16[32,4096]{1,0:T(8,128)(2,1)S(1)}, u32[]{:S(2)}, u32[]{:S(2)}) collective-permute-start(bf16[32,4096]{1,0:T(8,128)(2,1)S(1)} %get-tuple-element.107), channel_id=1, source_target_pairs={{0,8},{1,9},{2,10},{3,11},{4,12},{5,13},{6,14},{7,15},{8,0},{9,1},... | collective-permute-start | bytes 786440 | tf_op jit(solution)/shard_map/ppermute | solution.py:82
  39.5 2.1 %collective-permute-start.21 = (bf16[64,4224]{1,0:T(8,128)(2,1)S(1)}, bf16[64,4224]{1,0:T(8,128)(2,1)S(1)}, u32[]{:S(2)}, u32[]{:S(2)}) collective-permute-start(bf16[64,4224]{1,0:T(8,128)(2,1)S(1)} %get-tuple-element.118.refs_0_), channel_id=1, source_target_pairs={{0,8},{1,9},{2,10},{3,11},{4,12},{5,13},{6,14},{7,15},{8,0},{9,1},... | collective-permute-start | bytes 1622024 | tf_op jit(solution)/shard_map/ppermute | solution.py:82
  40.1 7.7 %collective-permute-start.11 = (bf16[32,4096]{1,0:T(8,128)(2,1)S(1)}, bf16[32,4096]{1,0:T(8,128)(2,1)S(1)}, u32[]{:S(2)}, u32[]{:S(2)}) collective-permute-start(bf16[32,4096]{1,0:T(8,128)(2,1)S(1)} %get-tuple-element.101), channel_id=1, source_target_pairs={{0,8},{1,9},{2,10},{3,11},{4,12},{5,13},{6,14},{7,15},{8,0},{9,1},... | collective-permute-start | bytes 786440 | tf_op jit(solution)/shard_map/ppermute | solution.py:82
  40.2 4.5 %collective-permute-start.18 = (bf16[32,4096]{1,0:T(8,128)(2,1)S(1)}, bf16[32,4096]{1,0:T(8,128)(2,1)S(1)}, u32[]{:S(2)}, u32[]{:S(2)}) collective-permute-start(bf16[32,4096]{1,0:T(8,128)(2,1)S(1)} %get-tuple-element.114), channel_id=1, source_target_pairs={{0,8},{1,9},{2,10},{3,11},{4,12},{5,13},{6,14},{7,15},{8,0},{9,1},... | collective-permute-start | bytes 786440 | tf_op jit(solution)/shard_map/ppermute | solution.py:82
  40.6 4.4 %collective-permute-start.19 = (bf16[32,4096]{1,0:T(8,128)(2,1)S(1)}, bf16[32,4096]{1,0:T(8,128)(2,1)S(1)}, u32[]{:S(2)}, u32[]{:S(2)}) collective-permute-start(bf16[32,4096]{1,0:T(8,128)(2,1)S(1)} %get-tuple-element.116), channel_id=1, source_target_pairs={{0,8},{1,9},{2,10},{3,11},{4,12},{5,13},{6,14},{7,15},{8,0},{9,1},... | collective-permute-start | bytes 786440 | tf_op jit(solution)/shard_map/ppermute | solution.py:82
  40.7 6.4 %collective-permute-start.20 = (bf16[32,4096]{1,0:T(8,128)(2,1)S(1)}, bf16[32,4096]{1,0:T(8,128)(2,1)S(1)}, u32[]{:S(2)}, u32[]{:S(2)}) collective-permute-start(bf16[32,4096]{1,0:T(8,128)(2,1)S(1)} %get-tuple-element.117), channel_id=1, source_target_pairs={{0,1},{1,0},{2,3},{3,2},{4,5},{5,4},{6,7},{7,6},{8,24},{9,25},{10,... | collective-permute-start | bytes 786440 | tf_op jit(solution)/shard_map/ppermute | solution.py:82
  41.6 8.2 %collective-permute-start.17 = (bf16[32,4096]{1,0:T(8,128)(2,1)S(1)}, bf16[32,4096]{1,0:T(8,128)(2,1)S(1)}, u32[]{:S(2)}, u32[]{:S(2)}) collective-permute-start(bf16[32,4096]{1,0:T(8,128)(2,1)S(1)} %get-tuple-element.112), channel_id=1, source_target_pairs={{0,1},{1,0},{2,3},{3,2},{4,5},{5,4},{6,7},{7,6},{8,24},{9,25},{10,... | collective-permute-start | bytes 786440 | tf_op jit(solution)/shard_map/ppermute | solution.py:82
  44.7 5.3 %collective-permute-start.25 = (bf16[32,4096]{1,0:T(8,128)(2,1)S(1)}, bf16[32,4096]{1,0:T(8,128)(2,1)S(1)}, u32[]{:S(2)}, u32[]{:S(2)}) collective-permute-start(bf16[32,4096]{1,0:T(8,128)(2,1)S(1)} %get-tuple-element.129), channel_id=1, source_target_pairs={{0,8},{1,9},{2,10},{3,11},{4,12},{5,13},{6,14},{7,15},{8,0},{9,1},... | collective-permute-start | bytes 786440 | tf_op jit(solution)/shard_map/ppermute | solution.py:82
  45.0 6.9 %collective-permute-start.27 = (bf16[32,4096]{1,0:T(8,128)(2,1)S(1)}, bf16[32,4096]{1,0:T(8,128)(2,1)S(1)}, u32[]{:S(2)}, u32[]{:S(2)}) collective-permute-start(bf16[32,4096]{1,0:T(8,128)(2,1)S(1)} %get-tuple-element.133), channel_id=1, source_target_pairs={{0,8},{1,9},{2,10},{3,11},{4,12},{5,13},{6,14},{7,15},{8,0},{9,1},... | collective-permute-start | bytes 786440 | tf_op jit(solution)/shard_map/ppermute | solution.py:82
  47.2 9.3 %collective-permute-start.28 = (bf16[32,4096]{1,0:T(8,128)(2,1)S(1)}, bf16[32,4096]{1,0:T(8,128)(2,1)S(1)}, u32[]{:S(2)}, u32[]{:S(2)}) collective-permute-start(bf16[32,4096]{1,0:T(8,128)(2,1)S(1)} %get-tuple-element.134), channel_id=1, source_target_pairs={{0,1},{1,0},{2,3},{3,2},{4,5},{5,4},{6,7},{7,6},{8,24},{9,25},{10,... | collective-permute-start | bytes 786440 | tf_op jit(solution)/shard_map/ppermute | solution.py:82
  47.8 8.7 %collective-permute-start.24 = (bf16[32,4096]{1,0:T(8,128)(2,1)S(1)}, bf16[32,4096]{1,0:T(8,128)(2,1)S(1)}, u32[]{:S(2)}, u32[]{:S(2)}) collective-permute-start(bf16[32,4096]{1,0:T(8,128)(2,1)S(1)} %get-tuple-element.127), channel_id=1, source_target_pairs={{0,8},{1,9},{2,10},{3,11},{4,12},{5,13},{6,14},{7,15},{8,0},{9,1},... | collective-permute-start | bytes 786440 | tf_op jit(solution)/shard_map/ppermute | solution.py:82
  50.0 9.3 %collective-permute-start.26 = (bf16[32,4096]{1,0:T(8,128)(2,1)S(1)}, bf16[32,4096]{1,0:T(8,128)(2,1)S(1)}, u32[]{:S(2)}, u32[]{:S(2)}) collective-permute-start(bf16[32,4096]{1,0:T(8,128)(2,1)S(1)} %get-tuple-element.131), channel_id=1, source_target_pairs={{0,1},{1,0},{2,3},{3,2},{4,5},{5,4},{6,7},{7,6},{8,24},{9,25},{10,... | collective-permute-start | bytes 786440 | tf_op jit(solution)/shard_map/ppermute | solution.py:82
  50.6 5.9 %collective-permute-start.23 = (bf16[16,4096]{1,0:T(8,128)(2,1)S(1)}, bf16[16,4096]{1,0:T(8,128)(2,1)S(1)}, u32[]{:S(2)}, u32[]{:S(2)}) collective-permute-start(bf16[16,4096]{1,0:T(8,128)(2,1)S(1)} %get-tuple-element.125), channel_id=1, source_target_pairs={{0,16},{1,17},{2,18},{3,19},{4,20},{5,21},{6,22},{7,23},{8,9},{9,8... | collective-permute-start | bytes 393224 | tf_op jit(solution)/shard_map/ppermute | solution.py:82
  51.8 11.8 %collective-permute-start.22 = (bf16[16,4096]{1,0:T(8,128)(2,1)S(1)}, bf16[16,4096]{1,0:T(8,128)(2,1)S(1)}, u32[]{:S(2)}, u32[]{:S(2)}) collective-permute-start(bf16[16,4096]{1,0:T(8,128)(2,1)S(1)} %get-tuple-element.123), channel_id=1, source_target_pairs={{0,16},{1,17},{2,18},{3,19},{4,20},{5,21},{6,22},{7,23},{8,9},{9,8... | collective-permute-start | bytes 393224 | tf_op jit(solution)/shard_map/ppermute | solution.py:82
  59.6 5.0 %collective-permute-start.30 = (bf16[16,4096]{1,0:T(8,128)(2,1)S(1)}, bf16[16,4096]{1,0:T(8,128)(2,1)S(1)}, u32[]{:S(2)}, u32[]{:S(2)}) collective-permute-start(bf16[16,4096]{1,0:T(8,128)(2,1)S(1)} %get-tuple-element.140), channel_id=1, source_target_pairs={{0,16},{1,17},{2,18},{3,19},{4,20},{5,21},{6,22},{7,23},{8,9},{9,8... | collective-permute-start | bytes 393224 | tf_op jit(solution)/shard_map/ppermute | solution.py:82
  61.0 5.0 %collective-permute-start.31 = (bf16[16,4096]{1,0:T(8,128)(2,1)S(1)}, bf16[16,4096]{1,0:T(8,128)(2,1)S(1)}, u32[]{:S(2)}, u32[]{:S(2)}) collective-permute-start(bf16[16,4096]{1,0:T(8,128)(2,1)S(1)} %get-tuple-element.142), channel_id=1, source_target_pairs={{0,16},{1,17},{2,18},{3,19},{4,20},{5,21},{6,22},{7,23},{8,9},{9,8... | collective-permute-start | bytes 393224 | tf_op jit(solution)/shard_map/ppermute | solution.py:82
  61.7 8.2 %collective-permute-start.29 = (bf16[16,4096]{1,0:T(8,128)(2,1)S(1)}, bf16[16,4096]{1,0:T(8,128)(2,1)S(1)}, u32[]{:S(2)}, u32[]{:S(2)}) collective-permute-start(bf16[16,4096]{1,0:T(8,128)(2,1)S(1)} %get-tuple-element.138), channel_id=1, source_target_pairs={{0,6},{1,7},{2,4},{3,5},{4,2},{5,3},{6,0},{7,1},{8,14},{9,15},{10,... | collective-permute-start | bytes 393224 | tf_op jit(solution)/shard_map/ppermute | solution.py:82
  66.1 8.0 %collective-permute-start.32 = (bf16[16,4096]{1,0:T(8,128)(2,1)S(1)}, bf16[16,4096]{1,0:T(8,128)(2,1)S(1)}, u32[]{:S(2)}, u32[]{:S(2)}) collective-permute-start(bf16[16,4096]{1,0:T(8,128)(2,1)S(1)} %get-tuple-element.146), channel_id=1, source_target_pairs={{0,4},{1,5},{2,6},{3,7},{4,0},{5,1},{6,2},{7,3},{8,12},{9,13},{10,... | collective-permute-start | bytes 393224 | tf_op jit(solution)/shard_map/ppermute | solution.py:82
  66.7 7.4 %collective-permute-start.33 = (bf16[16,4096]{1,0:T(8,128)(2,1)S(1)}, bf16[16,4096]{1,0:T(8,128)(2,1)S(1)}, u32[]{:S(2)}, u32[]{:S(2)}) collective-permute-start(bf16[16,4096]{1,0:T(8,128)(2,1)S(1)} %get-tuple-element.149), channel_id=1, source_target_pairs={{0,2},{1,3},{2,0},{3,1},{4,6},{5,7},{6,4},{7,5},{8,10},{9,11},{10,... | collective-permute-start | bytes 393224 | tf_op jit(solution)/shard_map/ppermute | solution.py:82

commit v4 on v3

--- a/solution.py
+++ b/solution.py
@@ -36,32 +36,35 @@
 PARTS = 3
 PIECES = 4
 SEQUENCE = (
+    "stage1",
     "pair0",
-    "block3 block1",
+    "block3",
+    "block1",
+    "stage0",
     "stage2",
-    "block2",
-    "pair3 mine0 pair1",
-    "stage1",
-    "stage0",
+    "block2 pair3 mine0 pair1",
     "pair2",
     "mine3",
+    "expert0",
     "mine1",
-    "expert0",
     "expert3",
+    "mine2 core3",
     "expert1",
-    "core0 core3 mine2",
     "expert2",
-    "core1 far3",
+    "far3",
+    "core0",
+    "core2",
+    "core1 near3",
+    "far2",
     "far0",
-    "core2",
-    "near3 far2 far1",
+    "far1",
+    "near2",
+    "near1 fold3",
+    "fold2",
     "near0",
-    "near2 near1",
-    "fold3",
-    "fold2",
     "fold1",
 )
-WEIGHT = 3
+WEIGHT = 20
 
 IN_VMEM = pl.BlockSpec(memory_space=pltpu.VMEM)
 IN_HBM = pl.BlockSpec(memory_space=pltpu.HBM)
@@ -128,23 +131,40 @@
         return results[:made]
 
 
-def together(order, parts, last):
+def rows_of(value):
+    return value if isinstance(value, tuple) else (value, 0, value.shape[0])
+
+
+def together(order, steps, last):
+    arrays, reads, outs, writes, place = [], [], [], [], {}
+    for run, _, shapes, values in steps:
+        read = []
+        for array, first, count in map(rows_of, values):
+            known = [i for i, other in enumerate(arrays) if other is array]
+            if not known:
+                arrays.append(array)
+            read.append((known[0] if known else len(arrays) - 1, first, count))
+        reads.append(read)
+        write = []
+        for which, ((count, width), dtype) in enumerate(shapes):
+            key = (run, which)
+            if key not in place:
+                place[key] = len(outs)
+                outs.append([0, width, dtype])
+            out = outs[place[key]]
+            write.append((place[key], out[0], count))
+            out[0] += count
+        writes.append(write)
+
     def body(*refs):
-        taken = 0
-        made = sum(len(arrays) for _, _, arrays in parts)
-        for part, outs, arrays in parts:
-            part(*refs[taken : taken + len(arrays)], *refs[made : made + len(outs)])
-            taken += len(arrays)
-            made += len(outs)
-
-    all_outs = [out for _, outs, _ in parts for out in outs]
-    all_arrays = [a for _, _, arrays in parts for a in arrays]
-    results = order(body, "sums", all_outs, all_arrays, last=last)
-    split = []
-    for _, outs, _ in parts:
-        split.append(results[: len(outs)])
-        results = results[len(outs) :]
-    return split
+        for (_, part, _, _), read, write in zip(steps, reads, writes):
+            views = [refs[i].at[first : first + count] for i, first, count in read]
+            views += [refs[len(arrays) + i].at[first : first + count] for i, first, count in write]
+            part(*views)
+
+    shapes = [((rows, width), dtype) for rows, width, dtype in outs]
+    results = order(body, "sums", shapes, arrays, last=last)
+    return results, writes
 
 
 def label_body(
@@ -227,9 +247,10 @@
     out[...] = received[...]
 
 
-def expert_body(features, experts, mine, others, w_gate, w_up, w_down, *refs):
+def expert_body(features, experts, places, mine, others, w_gate, w_up, w_down, *refs):
     kept, sent, partner_kept, partner_sent, joined, hidden = refs
-    count, half = mine.shape[0], kept.shape[0]
+    count, half = places[0][1], kept.shape[0]
+    mine, others = (ref.at[first : first + n] for ref, (first, n) in zip((mine, others), places))
     position = lax.axis_index("expert") * NX + lax.div(lax.axis_index("dp"), NC)
     joined[:count, :] = mine[...]
     joined[count:, :] = others[...]
@@ -254,13 +275,15 @@
 
 
 def expert_rows(order, mine, others, weights, experts):
-    count, width = mine.shape
+    arrays, *places = zip(rows_of(mine), rows_of(others))
+    places = tuple(zip(*places))
+    count, width = places[0][1], arrays[0].shape[1]
     features, hidden_units = weights[0].shape
     return order(
-        functools.partial(expert_body, features, experts),
+        functools.partial(expert_body, features, experts, places),
         "expert",
         [((n, features), BF16) for n in (count // 2,) * 4],
-        (mine, others, *weights),
+        (*arrays, *weights),
         scratch=[pltpu.VMEM((2 * count, width), BF16), pltpu.VMEM((2 * count, hidden_units), BF16)],
         vmem=6,
         flops=WEIGHT * 12 * count * features * hidden_units,
@@ -281,8 +304,12 @@
     passed[...] = total(slice(rows, 2 * rows)).astype(BF16)
 
 
-def plane_sum_body(mine, received, out):
-    out[...] = (mine[...] + received[...].astype(F32)).astype(out.dtype)
+def sum_body(*refs):
+    *parts, out = refs
+    total = parts[0][...].astype(F32)
+    for part in parts[1:]:
+        total += part[...].astype(F32)
+    out[...] = total.astype(out.dtype)
 
 
 def on_device_plane(
@@ -313,35 +340,39 @@
         if kind == "far":
             outs = [((rows, features), F32), ((rows, features), BF16)]
             return part_sum_body, outs, [kept[step], more_kept[step], sent[step]]
-        if kind == "near":
-            outs = [((rows, features), BF16 if step else F32)]
-            return plane_sum_body, outs, [kept[step], sent[step]]
-        outs = [((rows, features), BF16 if step == folds[-1] else F32)]
-        return plane_sum_body, outs, [total[0], total[step]]
-
-    def passed_on(kind, step, results):
-        if kind == "block":
-            [block[step]] = results
-            from_first[step] = over_first(block[step])
-        elif kind == "pair":
-            [pair[step]] = results
-            from_second[step] = over_second(pair[step])
-        elif kind == "mine":
-            [mine[step]] = results
-            others[step] = over_core(mine[step])
-        elif kind == "core":
-            sent[step] = over_second(results[0])
-        elif kind == "far":
-            kept[step], sent[step] = results[0], over_first(results[1])
-        elif kind == "near":
-            total[step] = along_z(results[0], step) if step else results[0]
-        else:
-            [total[0]] = results
-
-    folds = [int(name[-1]) for group in SEQUENCE for name in group.split() if name[:-1] == "fold"]
+        if kind == "near" and step:
+            return sum_body, [((rows, features), BF16)], [kept[step], sent[step]]
+        parts = [total[step]] if kind == "fold" else [kept[step], sent[step]]
+        outs = [((rows, features), BF16 if (kind, step) == final else F32)]
+        return sum_body, outs, whole + parts
+
+    def passed_on(kind, which, results, writes):
+        made = [results[i] for i, _, _ in writes[0]]
+        send = {"block": over_first, "pair": over_second, "mine": over_core, "core": over_second, "far": over_first}
+        received = send[kind](made[-1]) if kind in send else None
+        for step, write in zip(which, writes):
+            (_, first, count) = write[-1]
+            here, there = (made[-1], first, count), (received, first, count)
+            if kind == "block":
+                block[step], from_first[step] = here, there
+            elif kind == "pair":
+                pair[step], from_second[step] = here, there
+            elif kind == "mine":
+                mine[step], others[step] = here, there
+            elif kind == "core":
+                sent[step] = there
+            elif kind == "far":
+                kept[step], sent[step] = (made[0], *write[0][1:]), there
+            elif kind == "near" and step:
+                total[step] = along_z(made[0], step)
+            else:
+                whole[:] = made
+
+    final = (SEQUENCE[-1][:-1], int(SEQUENCE[-1][-1]))
+    whole = []
     for group in SEQUENCE:
-        names = [(name[:-1], int(name[-1])) for name in group.split()]
-        kind, step = names[0]
+        runs = [[(name[:-1], int(name[-1])) for name in run.split("+")] for run in group.split()]
+        kind, step = runs[0][0]
         if kind == "stage":
             weights[step] = staged(order, weights[step])
         elif kind == "expert":
@@ -350,10 +381,12 @@
             more_sent[step] = over_core(more_sent[step])
             more_kept[step] = over_core(more_kept[step])
         else:
-            results = together(order, [inputs(*name) for name in names], group is SEQUENCE[-1])
-            for name, result in zip(names, results):
-                passed_on(*name, result)
-    return total[0]
+            steps = [(i, *inputs(*name)) for i, run in enumerate(runs) for name in run]
+            results, writes = together(order, steps, group is SEQUENCE[-1])
+            for i, run in enumerate(runs):
+                at = [write for step, write in zip(steps, writes) if step[0] == i]
+                passed_on(run[0][0], [step for _, step in run], results, at)
+    return whole[0]
 
 
 def on_device_lanes(

time: 74.9 us -> 71.3 us (0.952)
  waiting for transfers between devices: 27.1 us -> 23.1 us
    ppermute x34, waiting for transfers between devices: 27.1 us -> 23.1 us  [moved(): return lax.ppermute(value, MESH_AXES, pairs)]
    pallas_call x25 -> x28, Pallas kernels: 15.6 us -> 15.7 us  [__call__(): pl.pallas_call(marked, name=name, out_shape=[pltpu.VMEM(shape, dtype) for...]
  transfers between devices with their start and end apart: 34 -> 34, of which waited for: 15 -> 12; matrix products, arithmetic and copies ran while one was open for 0% -> 0% of each run, Pallas kernels for 19% -> 20%
where the time goes in v4:
time: 71.3 us; the launch traced here: 71.1 us
  starting transfers between devices  31.4 us (44%)
  waiting for transfers between devices  23.1 us (32%)
  Pallas kernels  15.7 us (22%)
    ppermute x34, starting transfers between devices, moved(): return lax.ppermute(value, MESH_AXES, pairs)  31.4 us
    ppermute x34, waiting for transfers between devices, moved(): return lax.ppermute(value, MESH_AXES, pairs)  23.1 us
    pallas_call x28, Pallas kernels, __call__(): pl.pallas_call(marked, name=name, out_shape=[pltpu.VMEM(shape, dtype) for...  15.7 us
  transfers between devices with their start and end apart: 34, of which 12 were waited for; matrix products, arithmetic and copies ran while one was open for 0% of the time, Pallas kernels for 20%

profile of v4, /device:TPU:0, one launch (start us, length us, event | category | flops | bytes accessed | tf_op | source)
XLA Modules:
  0.0 71.1 jit_solution(16055976963130404828)
XLA Ops:
  0.0 1.2 %label.1 = (bf16[16,4224]{1,0:T(8,128)(2,1)S(1)}, f32[8,128]{1,0:T(8,128)S(1)}) custom-call(bf16[16,4096]{1,0:T(8,128)(2,1)} %refs_0_.1, s32[8,16]{1,0:T(8,128)} %bitcast.8, f32[8,16]{1,0:T(8,128)} %bitcast.9, s32[16]{0:T(128)} %refs_3_.1, s32[16]{0:T(128)} %refs_4_.1), custom_call_target="tpu_custom_call" | custom-call | tf_op jit(solution)/shard_map/label/pallas_call | solution.py:120
  1.2 3.0 %collective-permute-start.2 = (bf16[16,4224]{1,0:T(8,128)(2,1)S(1)}, bf16[16,4224]{1,0:T(8,128)(2,1)S(1)}, u32[]{:S(2)}, u32[]{:S(2)}) collective-permute-start(bf16[16,4224]{1,0:T(8,128)(2,1)S(1)} %get-tuple-element.81.refs_0_), channel_id=1, source_target_pairs={{0,16},{1,17},{2,18},{3,19},{4,20},{5,21},{6,22},{7,23},{8,9},{9,8... | collective-permute-start | bytes 405512 | tf_op jit(solution)/shard_map/ppermute | solution.py:85
  4.2 3.6 %collective-permute-start.1 = (bf16[16,4224]{1,0:T(8,128)(2,1)S(1)}, bf16[16,4224]{1,0:T(8,128)(2,1)S(1)}, u32[]{:S(2)}, u32[]{:S(2)}) collective-permute-start(bf16[16,4224]{1,0:T(8,128)(2,1)S(1)} %get-tuple-element.81.refs_0_), channel_id=1, source_target_pairs={{0,6},{1,7},{2,4},{3,5},{4,2},{5,3},{6,0},{7,1},{8,14},{9,15},{10,... | collective-permute-start | bytes 405512 | tf_op jit(solution)/shard_map/ppermute | solution.py:85
  7.8 1.9 %stage.3 = (bf16[4096,384]{1,0:T(8,128)(2,1)S(1)}, f32[8,128]{1,0:T(8,128)S(1)}) custom-call(bf16[4096,384]{1,0:T(8,128)(2,1)} %bitcast.5, f32[8,128]{1,0:T(8,128)S(1)} %get-tuple-element.82.refs_1_), custom_call_target="tpu_custom_call" | custom-call | tf_op jit(solution)/shard_map/stage/pallas_call | solution.py:120
  9.7 1.6 %collective-permute-start.4 = (bf16[32,4224]{1,0:T(8,128)(2,1)S(1)}, bf16[32,4224]{1,0:T(8,128)(2,1)S(1)}, u32[]{:S(2)}, u32[]{:S(2)}) collective-permute-start(bf16[32,4224]{1,0:T(8,128)(2,1)S(1)} %get-tuple-element.86.refs_3_), channel_id=1, source_target_pairs={{0,1},{1,0},{2,3},{3,2},{4,5},{5,4},{6,7},{7,6},{8,24},{9,25},{10,... | collective-permute-start | bytes 811016 | tf_op jit(solution)/shard_map/ppermute | solution.py:85
  11.3 0.8 %collective-permute-start = (bf16[16,4224]{1,0:T(8,128)(2,1)S(1)}, bf16[16,4224]{1,0:T(8,128)(2,1)S(1)}, u32[]{:S(2)}, u32[]{:S(2)}) collective-permute-start(bf16[16,4224]{1,0:T(8,128)(2,1)S(1)} %get-tuple-element.81.refs_0_), channel_id=1, source_target_pairs={{0,4},{1,5},{2,6},{3,7},{4,0},{5,1},{6,2},{7,3},{8,12},{9,13},{10,... | collective-permute-start | bytes 405512 | tf_op jit(solution)/shard_map/ppermute | solution.py:85
  12.1 0.4 collective-permute-done.1.refs_0_
  12.5 1.0 %collective-permute-start.3 = (bf16[16,4224]{1,0:T(8,128)(2,1)S(1)}, bf16[16,4224]{1,0:T(8,128)(2,1)S(1)}, u32[]{:S(2)}, u32[]{:S(2)}) collective-permute-start(bf16[16,4224]{1,0:T(8,128)(2,1)S(1)} %get-tuple-element.85.refs_1_), channel_id=1, source_target_pairs={{0,16},{1,17},{2,18},{3,19},{4,20},{5,21},{6,22},{7,23},{8,9},{9,8... | collective-permute-start | bytes 405512 | tf_op jit(solution)/shard_map/ppermute | solution.py:85
  13.5 1.9 %collective-permute-done.5.refs_0_ = bf16[16,4224]{1,0:T(8,128)(2,1)S(1)} collective-permute-done((bf16[16,4224]{1,0:T(8,128)(2,1)S(1)}, bf16[16,4224]{1,0:T(8,128)(2,1)S(1)}, u32[]{:S(2)}, u32[]{:S(2)}) %collective-permute-start.5) | collective-permute-done | bytes 135200 | tf_op jit(solution)/shard_map/ppermute | solution.py:85
  15.4 1.3 %collective-permute-start.6 = (bf16[16,4224]{1,0:T(8,128)(2,1)S(1)}, bf16[16,4224]{1,0:T(8,128)(2,1)S(1)}, u32[]{:S(2)}, u32[]{:S(2)}) collective-permute-start(bf16[16,4224]{1,0:T(8,128)(2,1)S(1)} %get-tuple-element.88.refs_5_), channel_id=1, source_target_pairs={{0,16},{1,17},{2,18},{3,19},{4,20},{5,21},{6,22},{7,23},{8,9},{9,8... | collective-permute-start | bytes 405512 | tf_op jit(solution)/shard_map/ppermute | solution.py:85
  16.7 1.9 %stage.4 = (bf16[4096,384]{1,0:T(8,128)(2,1)S(1)}, f32[8,128]{1,0:T(8,128)S(1)}) custom-call(bf16[4096,384]{1,0:T(8,128)(2,1)} %bitcast.6, f32[8,128]{1,0:T(8,128)S(1)} %get-tuple-element.89.refs_1_), custom_call_target="tpu_custom_call" | custom-call | tf_op jit(solution)/shard_map/stage/pallas_call | solution.py:120
  18.6 1.9 %stage.5 = (bf16[384,4096]{1,0:T(8,128)(2,1)S(1)}, f32[8,128]{1,0:T(8,128)S(1)}) custom-call(bf16[384,4096]{1,0:T(8,128)(2,1)} %bitcast.7, f32[8,128]{1,0:T(8,128)S(1)} %get-tuple-element.90.refs_1_), custom_call_target="tpu_custom_call" | custom-call | tf_op jit(solution)/shard_map/stage/pallas_call | solution.py:120
  20.7 0.6 collective-permute-start.9
  21.3 1.2 %collective-permute-start.10 = (bf16[16,4224]{1,0:T(8,128)(2,1)S(1)}, bf16[16,4224]{1,0:T(8,128)(2,1)S(1)}, u32[]{:S(2)}, u32[]{:S(2)}) collective-permute-start(bf16[16,4224]{1,0:T(8,128)(2,1)S(1)} %get-tuple-element.98.refs_0_), channel_id=1, source_target_pairs={{0,16},{1,17},{2,18},{3,19},{4,20},{5,21},{6,22},{7,23},{8,9},{9,8... | collective-permute-start | bytes 405512 | tf_op jit(solution)/shard_map/ppermute | solution.py:85
  22.5 1.5 %collective-permute-start.7 = (bf16[32,4224]{1,0:T(8,128)(2,1)S(1)}, bf16[32,4224]{1,0:T(8,128)(2,1)S(1)}, u32[]{:S(2)}, u32[]{:S(2)}) collective-permute-start(bf16[32,4224]{1,0:T(8,128)(2,1)S(1)} %get-tuple-element.92.refs_0_), channel_id=1, source_target_pairs={{0,1},{1,0},{2,3},{3,2},{4,5},{5,4},{6,7},{7,6},{8,24},{9,25},{10,... | collective-permute-start | bytes 811016 | tf_op jit(solution)/shard_map/ppermute | solution.py:85
  24.0 3.8 %collective-permute-done.10.refs_1_ = bf16[16,4224]{1,0:T(8,128)(2,1)S(1)} collective-permute-done((bf16[16,4224]{1,0:T(8,128)(2,1)S(1)}, bf16[16,4224]{1,0:T(8,128)(2,1)S(1)}, u32[]{:S(2)}, u32[]{:S(2)}) %collective-permute-start.10) | collective-permute-done | bytes 135200 | tf_op jit(solution)/shard_map/ppermute | solution.py:85
  27.8 1.6 %collective-permute-start.12 = (bf16[32,4224]{1,0:T(8,128)(2,1)S(1)}, bf16[32,4224]{1,0:T(8,128)(2,1)S(1)}, u32[]{:S(2)}, u32[]{:S(2)}) collective-permute-start(bf16[32,4224]{1,0:T(8,128)(2,1)S(1)} %get-tuple-element.104.refs_0_), channel_id=1, source_target_pairs={{0,1},{1,0},{2,3},{3,2},{4,5},{5,4},{6,7},{7,6},{8,24},{9,25},{10,... | collective-permute-start | bytes 811016 | tf_op jit(solution)/shard_map/ppermute | solution.py:85
  29.5 1.9 %expert.4 = (bf16[32,4096]{1,0:T(8,128)(2,1)S(1)}, bf16[32,4096]{1,0:T(8,128)(2,1)S(1)}, bf16[32,4096]{1,0:T(8,128)(2,1)S(1)}, bf16[32,4096]{1,0:T(8,128)(2,1)S(1)}, f32[8,128]{1,0:T(8,128)S(1)}) custom-call(bf16[64,4224]{1,0:T(8,128)(2,1)S(1)} %get-tuple-element.93.refs_0_, bf16[64,4224]{1,0:T(8,128)(2,1)S(1)} %collective-permute-done.8.refs_1_, ...), custom_call_target="tpu_custom_call" | custom-call | flops 24159191040 | tf_op jit(solution)/shard_map/expert/pallas_call | solution.py:120
  31.6 0.5 collective-permute-start.11
  32.1 1.9 %expert.5 = (bf16[32,4096]{1,0:T(8,128)(2,1)S(1)}, bf16[32,4096]{1,0:T(8,128)(2,1)S(1)}, bf16[32,4096]{1,0:T(8,128)(2,1)S(1)}, bf16[32,4096]{1,0:T(8,128)(2,1)S(1)}, f32[8,128]{1,0:T(8,128)S(1)}) custom-call(bf16[64,4224]{1,0:T(8,128)(2,1)S(1)} %get-tuple-element.105.refs_0_, bf16[64,4224]{1,0:T(8,128)(2,1)S(1)} %collective-permute-done.13.refs_1_, ...), custom_call_target="tpu_custom_call" | custom-call | flops 24159191040 | tf_op jit(solution)/shard_map/expert/pallas_call | solution.py:120
  34.0 0.2 collective-permute-start.14
  34.2 0.4 collective-permute-start.22
  34.7 0.9 %collective-permute-done.14.refs_3_ = bf16[32,4096]{1,0:T(8,128)(2,1)S(1)} collective-permute-done((bf16[32,4096]{1,0:T(8,128)(2,1)S(1)}, bf16[32,4096]{1,0:T(8,128)(2,1)S(1)}, u32[]{:S(2)}, u32[]{:S(2)}) %collective-permute-start.14) | collective-permute-done | bytes 262176 | tf_op jit(solution)/shard_map/ppermute | solution.py:85
  35.6 0.1 sums.27
  35.8 0.5 collective-permute-start.18
  36.3 0.6 collective-permute-start.19
  36.9 1.9 %expert.6 = (bf16[32,4096]{1,0:T(8,128)(2,1)S(1)}, bf16[32,4096]{1,0:T(8,128)(2,1)S(1)}, bf16[32,4096]{1,0:T(8,128)(2,1)S(1)}, bf16[32,4096]{1,0:T(8,128)(2,1)S(1)}, f32[8,128]{1,0:T(8,128)S(1)}) custom-call(bf16[64,4224]{1,0:T(8,128)(2,1)S(1)} %get-tuple-element.103.refs_0_, bf16[64,4224]{1,0:T(8,128)(2,1)S(1)} %collective-permute-done.11.refs_1_, ...), custom_call_target="tpu_custom_call" | custom-call | flops 24159191040 | tf_op jit(solution)/shard_map/expert/pallas_call | solution.py:120
  38.8 1.9 %expert.7 = (bf16[32,4096]{1,0:T(8,128)(2,1)S(1)}, bf16[32,4096]{1,0:T(8,128)(2,1)S(1)}, bf16[32,4096]{1,0:T(8,128)(2,1)S(1)}, bf16[32,4096]{1,0:T(8,128)(2,1)S(1)}, f32[8,128]{1,0:T(8,128)S(1)}) custom-call(bf16[64,4224]{1,0:T(8,128)(2,1)S(1)} %get-tuple-element.118.refs_0_, bf16[64,4224]{1,0:T(8,128)(2,1)S(1)} %collective-permute-done.19.refs_1_, ...), custom_call_target="tpu_custom_call" | custom-call | flops 24159191040 | tf_op jit(solution)/shard_map/expert/pallas_call | solution.py:120
  40.9 0.5 collective-permute-start.16
  41.4 0.8 %collective-permute-done.18.refs_2_ = bf16[32,4096]{1,0:T(8,128)(2,1)S(1)} collective-permute-done((bf16[32,4096]{1,0:T(8,128)(2,1)S(1)}, bf16[32,4096]{1,0:T(8,128)(2,1)S(1)}, u32[]{:S(2)}, u32[]{:S(2)}) %collective-permute-start.18) | collective-permute-done | bytes 262176 | tf_op jit(solution)/shard_map/ppermute | solution.py:85
  42.3 1.3 %collective-permute-start.20 = (bf16[16,4096]{1,0:T(8,128)(2,1)S(1)}, bf16[16,4096]{1,0:T(8,128)(2,1)S(1)}, u32[]{:S(2)}, u32[]{:S(2)}) collective-permute-start(bf16[16,4096]{1,0:T(8,128)(2,1)S(1)} %get-tuple-element.122), channel_id=1, source_target_pairs={{0,16},{1,17},{2,18},{3,19},{4,20},{5,21},{6,22},{7,23},{8,9},{9,8... | collective-permute-start | bytes 393224 | tf_op jit(solution)/shard_map/ppermute | solution.py:85
  43.7 0.7 %collective-permute-start.27 = (bf16[32,4096]{1,0:T(8,128)(2,1)S(1)}, bf16[32,4096]{1,0:T(8,128)(2,1)S(1)}, u32[]{:S(2)}, u32[]{:S(2)}) collective-permute-start(bf16[32,4096]{1,0:T(8,128)(2,1)S(1)} %get-tuple-element.136), channel_id=1, source_target_pairs={{0,1},{1,0},{2,3},{3,2},{4,5},{5,4},{6,7},{7,6},{8,24},{9,25},{10,... | collective-permute-start | bytes 786440 | tf_op jit(solution)/shard_map/ppermute | solution.py:85
  44.4 0.5 collective-permute-start.15
  44.9 3.8 %collective-permute-done.20.refs_3_ = bf16[16,4096]{1,0:T(8,128)(2,1)S(1)} collective-permute-done((bf16[16,4096]{1,0:T(8,128)(2,1)S(1)}, bf16[16,4096]{1,0:T(8,128)(2,1)S(1)}, u32[]{:S(2)}, u32[]{:S(2)}) %collective-permute-start.20) | collective-permute-done | bytes 131104 | tf_op jit(solution)/shard_map/ppermute | solution.py:85
  48.7 0.6 collective-permute-start.25
  49.5 1.4 %collective-permute-start.23 = (bf16[32,4096]{1,0:T(8,128)(2,1)S(1)}, bf16[32,4096]{1,0:T(8,128)(2,1)S(1)}, u32[]{:S(2)}, u32[]{:S(2)}) collective-permute-start(bf16[32,4096]{1,0:T(8,128)(2,1)S(1)} %get-tuple-element.130), channel_id=1, source_target_pairs={{0,1},{1,0},{2,3},{3,2},{4,5},{5,4},{6,7},{7,6},{8,24},{9,25},{10,... | collective-permute-start | bytes 786440 | tf_op jit(solution)/shard_map/ppermute | solution.py:85
  50.9 2.2 %collective-permute-start.29 = (bf16[16,4096]{1,0:T(8,128)(2,1)S(1)}, bf16[16,4096]{1,0:T(8,128)(2,1)S(1)}, u32[]{:S(2)}, u32[]{:S(2)}) collective-permute-start(bf16[16,4096]{1,0:T(8,128)(2,1)S(1)} %get-tuple-element.142), channel_id=1, source_target_pairs={{0,6},{1,7},{2,4},{3,5},{4,2},{5,3},{6,0},{7,1},{8,14},{9,15},{10,... | collective-permute-start | bytes 393224 | tf_op jit(solution)/shard_map/ppermute | solution.py:85
  53.2 1.2 %collective-permute-start.30 = (bf16[16,4096]{1,0:T(8,128)(2,1)S(1)}, bf16[16,4096]{1,0:T(8,128)(2,1)S(1)}, u32[]{:S(2)}, u32[]{:S(2)}) collective-permute-start(bf16[16,4096]{1,0:T(8,128)(2,1)S(1)} %get-tuple-element.144), channel_id=1, source_target_pairs={{0,16},{1,17},{2,18},{3,19},{4,20},{5,21},{6,22},{7,23},{8,9},{9,8... | collective-permute-start | bytes 393224 | tf_op jit(solution)/shard_map/ppermute | solution.py:85
  54.4 1.1 %collective-permute-done.25.refs_2_ = bf16[32,4096]{1,0:T(8,128)(2,1)S(1)} collective-permute-done((bf16[32,4096]{1,0:T(8,128)(2,1)S(1)}, bf16[32,4096]{1,0:T(8,128)(2,1)S(1)}, u32[]{:S(2)}, u32[]{:S(2)}) %collective-permute-start.25) | collective-permute-done | bytes 262176 | tf_op jit(solution)/shard_map/ppermute | solution.py:85
  55.6 4.6 %collective-permute-done.23.refs_2_ = bf16[32,4096]{1,0:T(8,128)(2,1)S(1)} collective-permute-done((bf16[32,4096]{1,0:T(8,128)(2,1)S(1)}, bf16[32,4096]{1,0:T(8,128)(2,1)S(1)}, u32[]{:S(2)}, u32[]{:S(2)}) %collective-permute-start.23) | collective-permute-done | bytes 262176 | tf_op jit(solution)/shard_map/ppermute | solution.py:85
  60.3 1.3 %collective-permute-start.28 = (bf16[16,4096]{1,0:T(8,128)(2,1)S(1)}, bf16[16,4096]{1,0:T(8,128)(2,1)S(1)}, u32[]{:S(2)}, u32[]{:S(2)}) collective-permute-start(bf16[16,4096]{1,0:T(8,128)(2,1)S(1)} %get-tuple-element.141), channel_id=1, source_target_pairs={{0,16},{1,17},{2,18},{3,19},{4,20},{5,21},{6,22},{7,23},{8,9},{9,8... | collective-permute-start | bytes 393224 | tf_op jit(solution)/shard_map/ppermute | solution.py:85
  61.6 1.5 %collective-permute-start.31 = (bf16[16,4096]{1,0:T(8,128)(2,1)S(1)}, bf16[16,4096]{1,0:T(8,128)(2,1)S(1)}, u32[]{:S(2)}, u32[]{:S(2)}) collective-permute-start(bf16[16,4096]{1,0:T(8,128)(2,1)S(1)} %get-tuple-element.148), channel_id=1, source_target_pairs={{0,4},{1,5},{2,6},{3,7},{4,0},{5,1},{6,2},{7,3},{8,12},{9,13},{10,... | collective-permute-start | bytes 393224 | tf_op jit(solution)/shard_map/ppermute | solution.py:85
  63.1 0.3 collective-permute-start.32
  63.4 1.9 %collective-permute-done.28.refs_1_ = bf16[16,4096]{1,0:T(8,128)(2,1)S(1)} collective-permute-done((bf16[16,4096]{1,0:T(8,128)(2,1)S(1)}, bf16[16,4096]{1,0:T(8,128)(2,1)S(1)}, u32[]{:S(2)}, u32[]{:S(2)}) %collective-permute-start.28) | collective-permute-done | bytes 131104 | tf_op jit(solution)/shard_map/ppermute | solution.py:85
  65.4 1.1 %collective-permute-start.33 = (bf16[16,4096]{1,0:T(8,128)(2,1)S(1)}, bf16[16,4096]{1,0:T(8,128)(2,1)S(1)}, u32[]{:S(2)}, u32[]{:S(2)}) collective-permute-start(bf16[16,4096]{1,0:T(8,128)(2,1)S(1)} %get-tuple-element.155), channel_id=1, source_target_pairs={{0,2},{1,3},{2,0},{3,1},{4,6},{5,7},{6,4},{7,5},{8,10},{9,11},{10,... | collective-permute-start | bytes 393224 | tf_op jit(solution)/shard_map/ppermute | solution.py:85
  66.6 2.4 %collective-permute-done.31.refs_1_ = bf16[16,4096]{1,0:T(8,128)(2,1)S(1)} collective-permute-done((bf16[16,4096]{1,0:T(8,128)(2,1)S(1)}, bf16[16,4096]{1,0:T(8,128)(2,1)S(1)}, u32[]{:S(2)}, u32[]{:S(2)}) %collective-permute-start.31) | collective-permute-done | bytes 131104 | tf_op jit(solution)/shard_map/ppermute | solution.py:85
  69.1 1.4 %collective-permute-done.33.refs_1_ = bf16[16,4096]{1,0:T(8,128)(2,1)S(1)} collective-permute-done((bf16[16,4096]{1,0:T(8,128)(2,1)S(1)}, bf16[16,4096]{1,0:T(8,128)(2,1)S(1)}, u32[]{:S(2)}, u32[]{:S(2)}) %collective-permute-start.33) | collective-permute-done | bytes 131104 | tf_op jit(solution)/shard_map/ppermute | solution.py:85
  70.5 0.7 copy.9
  (49 shorter events, 1.5 us)
Async XLA Ops:
  1.2 8.5 %collective-permute-start.2 = (bf16[16,4224]{1,0:T(8,128)(2,1)S(1)}, bf16[16,4224]{1,0:T(8,128)(2,1)S(1)}, u32[]{:S(2)}, u32[]{:S(2)}) collective-permute-start(bf16[16,4224]{1,0:T(8,128)(2,1)S(1)} %get-tuple-element.81.refs_0_), channel_id=1, source_target_pairs={{0,16},{1,17},{2,18},{3,19},{4,20},{5,21},{6,22},{7,23},{8,9},{9,8... | collective-permute-start | bytes 405512 | tf_op jit(solution)/shard_map/ppermute | solution.py:85
  4.2 8.3 %collective-permute-start.1 = (bf16[16,4224]{1,0:T(8,128)(2,1)S(1)}, bf16[16,4224]{1,0:T(8,128)(2,1)S(1)}, u32[]{:S(2)}, u32[]{:S(2)}) collective-permute-start(bf16[16,4224]{1,0:T(8,128)(2,1)S(1)} %get-tuple-element.81.refs_0_), channel_id=1, source_target_pairs={{0,6},{1,7},{2,4},{3,5},{4,2},{5,3},{6,0},{7,1},{8,14},{9,15},{10,... | collective-permute-start | bytes 405512 | tf_op jit(solution)/shard_map/ppermute | solution.py:85
  7.8 7.6 %collective-permute-start.5 = (bf16[16,4224]{1,0:T(8,128)(2,1)S(1)}, bf16[16,4224]{1,0:T(8,128)(2,1)S(1)}, u32[]{:S(2)}, u32[]{:S(2)}) collective-permute-start(bf16[16,4224]{1,0:T(8,128)(2,1)S(1)} %get-tuple-element.81.refs_0_), channel_id=1, source_target_pairs={{0,2},{1,3},{2,0},{3,1},{4,6},{5,7},{6,4},{7,5},{8,10},{9,11},{10,... | collective-permute-start | bytes 405512 | tf_op jit(solution)/shard_map/ppermute | solution.py:85
  9.7 10.8 %collective-permute-start.4 = (bf16[32,4224]{1,0:T(8,128)(2,1)S(1)}, bf16[32,4224]{1,0:T(8,128)(2,1)S(1)}, u32[]{:S(2)}, u32[]{:S(2)}) collective-permute-start(bf16[32,4224]{1,0:T(8,128)(2,1)S(1)} %get-tuple-element.86.refs_3_), channel_id=1, source_target_pairs={{0,1},{1,0},{2,3},{3,2},{4,5},{5,4},{6,7},{7,6},{8,24},{9,25},{10,... | collective-permute-start | bytes 811016 | tf_op jit(solution)/shard_map/ppermute | solution.py:85
  11.3 9.2 %collective-permute-start = (bf16[16,4224]{1,0:T(8,128)(2,1)S(1)}, bf16[16,4224]{1,0:T(8,128)(2,1)S(1)}, u32[]{:S(2)}, u32[]{:S(2)}) collective-permute-start(bf16[16,4224]{1,0:T(8,128)(2,1)S(1)} %get-tuple-element.81.refs_0_), channel_id=1, source_target_pairs={{0,4},{1,5},{2,6},{3,7},{4,0},{5,1},{6,2},{7,3},{8,12},{9,13},{10,... | collective-permute-start | bytes 405512 | tf_op jit(solution)/shard_map/ppermute | solution.py:85
  12.5 8.0 %collective-permute-start.3 = (bf16[16,4224]{1,0:T(8,128)(2,1)S(1)}, bf16[16,4224]{1,0:T(8,128)(2,1)S(1)}, u32[]{:S(2)}, u32[]{:S(2)}) collective-permute-start(bf16[16,4224]{1,0:T(8,128)(2,1)S(1)} %get-tuple-element.85.refs_1_), channel_id=1, source_target_pairs={{0,16},{1,17},{2,18},{3,19},{4,20},{5,21},{6,22},{7,23},{8,9},{9,8... | collective-permute-start | bytes 405512 | tf_op jit(solution)/shard_map/ppermute | solution.py:85
  15.4 5.1 %collective-permute-start.6 = (bf16[16,4224]{1,0:T(8,128)(2,1)S(1)}, bf16[16,4224]{1,0:T(8,128)(2,1)S(1)}, u32[]{:S(2)}, u32[]{:S(2)}) collective-permute-start(bf16[16,4224]{1,0:T(8,128)(2,1)S(1)} %get-tuple-element.88.refs_5_), channel_id=1, source_target_pairs={{0,16},{1,17},{2,18},{3,19},{4,20},{5,21},{6,22},{7,23},{8,9},{9,8... | collective-permute-start | bytes 405512 | tf_op jit(solution)/shard_map/ppermute | solution.py:85
  20.6 8.9 %collective-permute-start.8 = (bf16[64,4224]{1,0:T(8,128)(2,1)S(1)}, bf16[64,4224]{1,0:T(8,128)(2,1)S(1)}, u32[]{:S(2)}, u32[]{:S(2)}) collective-permute-start(bf16[64,4224]{1,0:T(8,128)(2,1)S(1)} %get-tuple-element.93.refs_0_), channel_id=1, source_target_pairs={{0,8},{1,9},{2,10},{3,11},{4,12},{5,13},{6,14},{7,15},{8,0},{9,1},... | collective-permute-start | bytes 1622024 | tf_op jit(solution)/shard_map/ppermute | solution.py:85
  20.7 8.7 %collective-permute-start.9 = (bf16[32,4224]{1,0:T(8,128)(2,1)S(1)}, bf16[32,4224]{1,0:T(8,128)(2,1)S(1)}, u32[]{:S(2)}, u32[]{:S(2)}) collective-permute-start(bf16[32,4224]{1,0:T(8,128)(2,1)S(1)} %get-tuple-element.97.refs_0_), channel_id=1, source_target_pairs={{0,1},{1,0},{2,3},{3,2},{4,5},{5,4},{6,7},{7,6},{8,24},{9,25},{10,... | collective-permute-start | bytes 811016 | tf_op jit(solution)/shard_map/ppermute | solution.py:85
  21.3 6.5 %collective-permute-start.10 = (bf16[16,4224]{1,0:T(8,128)(2,1)S(1)}, bf16[16,4224]{1,0:T(8,128)(2,1)S(1)}, u32[]{:S(2)}, u32[]{:S(2)}) collective-permute-start(bf16[16,4224]{1,0:T(8,128)(2,1)S(1)} %get-tuple-element.98.refs_0_), channel_id=1, source_target_pairs={{0,16},{1,17},{2,18},{3,19},{4,20},{5,21},{6,22},{7,23},{8,9},{9,8... | collective-permute-start | bytes 405512 | tf_op jit(solution)/shard_map/ppermute | solution.py:85
  22.5 9.1 %collective-permute-start.7 = (bf16[32,4224]{1,0:T(8,128)(2,1)S(1)}, bf16[32,4224]{1,0:T(8,128)(2,1)S(1)}, u32[]{:S(2)}, u32[]{:S(2)}) collective-permute-start(bf16[32,4224]{1,0:T(8,128)(2,1)S(1)} %get-tuple-element.92.refs_0_), channel_id=1, source_target_pairs={{0,1},{1,0},{2,3},{3,2},{4,5},{5,4},{6,7},{7,6},{8,24},{9,25},{10,... | collective-permute-start | bytes 811016 | tf_op jit(solution)/shard_map/ppermute | solution.py:85
  27.8 7.0 %collective-permute-start.12 = (bf16[32,4224]{1,0:T(8,128)(2,1)S(1)}, bf16[32,4224]{1,0:T(8,128)(2,1)S(1)}, u32[]{:S(2)}, u32[]{:S(2)}) collective-permute-start(bf16[32,4224]{1,0:T(8,128)(2,1)S(1)} %get-tuple-element.104.refs_0_), channel_id=1, source_target_pairs={{0,1},{1,0},{2,3},{3,2},{4,5},{5,4},{6,7},{7,6},{8,24},{9,25},{10,... | collective-permute-start | bytes 811016 | tf_op jit(solution)/shard_map/ppermute | solution.py:85
  29.4 2.6 %collective-permute-start.13 = (bf16[64,4224]{1,0:T(8,128)(2,1)S(1)}, bf16[64,4224]{1,0:T(8,128)(2,1)S(1)}, u32[]{:S(2)}, u32[]{:S(2)}) collective-permute-start(bf16[64,4224]{1,0:T(8,128)(2,1)S(1)} %get-tuple-element.105.refs_0_), channel_id=1, source_target_pairs={{0,8},{1,9},{2,10},{3,11},{4,12},{5,13},{6,14},{7,15},{8,0},{9,1},... | collective-permute-start | bytes 1622024 | tf_op jit(solution)/shard_map/ppermute | solution.py:85
  31.6 5.3 %collective-permute-start.11 = (bf16[64,4224]{1,0:T(8,128)(2,1)S(1)}, bf16[64,4224]{1,0:T(8,128)(2,1)S(1)}, u32[]{:S(2)}, u32[]{:S(2)}) collective-permute-start(bf16[64,4224]{1,0:T(8,128)(2,1)S(1)} %get-tuple-element.103.refs_0_), channel_id=1, source_target_pairs={{0,8},{1,9},{2,10},{3,11},{4,12},{5,13},{6,14},{7,15},{8,0},{9,1},... | collective-permute-start | bytes 1622024 | tf_op jit(solution)/shard_map/ppermute | solution.py:85
  34.0 1.6 %collective-permute-start.14 = (bf16[32,4096]{1,0:T(8,128)(2,1)S(1)}, bf16[32,4096]{1,0:T(8,128)(2,1)S(1)}, u32[]{:S(2)}, u32[]{:S(2)}) collective-permute-start(bf16[32,4096]{1,0:T(8,128)(2,1)S(1)} %get-tuple-element.108), channel_id=1, source_target_pairs={{0,8},{1,9},{2,10},{3,11},{4,12},{5,13},{6,14},{7,15},{8,0},{9,1},... | collective-permute-start | bytes 786440 | tf_op jit(solution)/shard_map/ppermute | solution.py:85
  34.2 9.4 %collective-permute-start.22 = (bf16[32,4096]{1,0:T(8,128)(2,1)S(1)}, bf16[32,4096]{1,0:T(8,128)(2,1)S(1)}, u32[]{:S(2)}, u32[]{:S(2)}) collective-permute-start(bf16[32,4096]{1,0:T(8,128)(2,1)S(1)} %get-tuple-element.126), channel_id=1, source_target_pairs={{0,8},{1,9},{2,10},{3,11},{4,12},{5,13},{6,14},{7,15},{8,0},{9,1},... | collective-permute-start | bytes 786440 | tf_op jit(solution)/shard_map/ppermute | solution.py:85
  34.6 6.8 %collective-permute-start.17 = (bf16[32,4096]{1,0:T(8,128)(2,1)S(1)}, bf16[32,4096]{1,0:T(8,128)(2,1)S(1)}, u32[]{:S(2)}, u32[]{:S(2)}) collective-permute-start(bf16[32,4096]{1,0:T(8,128)(2,1)S(1)} %get-tuple-element.116), channel_id=1, source_target_pairs={{0,8},{1,9},{2,10},{3,11},{4,12},{5,13},{6,14},{7,15},{8,0},{9,1},... | collective-permute-start | bytes 786440 | tf_op jit(solution)/shard_map/ppermute | solution.py:85
  35.8 6.4 %collective-permute-start.18 = (bf16[32,4096]{1,0:T(8,128)(2,1)S(1)}, bf16[32,4096]{1,0:T(8,128)(2,1)S(1)}, u32[]{:S(2)}, u32[]{:S(2)}) collective-permute-start(bf16[32,4096]{1,0:T(8,128)(2,1)S(1)} %get-tuple-element.117), channel_id=1, source_target_pairs={{0,1},{1,0},{2,3},{3,2},{4,5},{5,4},{6,7},{7,6},{8,24},{9,25},{10,... | collective-permute-start | bytes 786440 | tf_op jit(solution)/shard_map/ppermute | solution.py:85
  36.3 2.5 %collective-permute-start.19 = (bf16[64,4224]{1,0:T(8,128)(2,1)S(1)}, bf16[64,4224]{1,0:T(8,128)(2,1)S(1)}, u32[]{:S(2)}, u32[]{:S(2)}) collective-permute-start(bf16[64,4224]{1,0:T(8,128)(2,1)S(1)} %get-tuple-element.118.refs_0_), channel_id=1, source_target_pairs={{0,8},{1,9},{2,10},{3,11},{4,12},{5,13},{6,14},{7,15},{8,0},{9,1},... | collective-permute-start | bytes 1622024 | tf_op jit(solution)/shard_map/ppermute | solution.py:85
  40.8 2.8 %collective-permute-start.21 = (bf16[32,4096]{1,0:T(8,128)(2,1)S(1)}, bf16[32,4096]{1,0:T(8,128)(2,1)S(1)}, u32[]{:S(2)}, u32[]{:S(2)}) collective-permute-start(bf16[32,4096]{1,0:T(8,128)(2,1)S(1)} %get-tuple-element.124), channel_id=1, source_target_pairs={{0,8},{1,9},{2,10},{3,11},{4,12},{5,13},{6,14},{7,15},{8,0},{9,1},... | collective-permute-start | bytes 786440 | tf_op jit(solution)/shard_map/ppermute | solution.py:85
  40.9 3.6 %collective-permute-start.16 = (bf16[32,4096]{1,0:T(8,128)(2,1)S(1)}, bf16[32,4096]{1,0:T(8,128)(2,1)S(1)}, u32[]{:S(2)}, u32[]{:S(2)}) collective-permute-start(bf16[32,4096]{1,0:T(8,128)(2,1)S(1)} %get-tuple-element.114), channel_id=1, source_target_pairs={{0,8},{1,9},{2,10},{3,11},{4,12},{5,13},{6,14},{7,15},{8,0},{9,1},... | collective-permute-start | bytes 786440 | tf_op jit(solution)/shard_map/ppermute | solution.py:85
  41.4 8.1 %collective-permute-start.26 = (bf16[32,4096]{1,0:T(8,128)(2,1)S(1)}, bf16[32,4096]{1,0:T(8,128)(2,1)S(1)}, u32[]{:S(2)}, u32[]{:S(2)}) collective-permute-start(bf16[32,4096]{1,0:T(8,128)(2,1)S(1)} %get-tuple-element.135), channel_id=1, source_target_pairs={{0,8},{1,9},{2,10},{3,11},{4,12},{5,13},{6,14},{7,15},{8,0},{9,1},... | collective-permute-start | bytes 786440 | tf_op jit(solution)/shard_map/ppermute | solution.py:85
  42.3 6.4 %collective-permute-start.20 = (bf16[16,4096]{1,0:T(8,128)(2,1)S(1)}, bf16[16,4096]{1,0:T(8,128)(2,1)S(1)}, u32[]{:S(2)}, u32[]{:S(2)}) collective-permute-start(bf16[16,4096]{1,0:T(8,128)(2,1)S(1)} %get-tuple-element.122), channel_id=1, source_target_pairs={{0,16},{1,17},{2,18},{3,19},{4,20},{5,21},{6,22},{7,23},{8,9},{9,8... | collective-permute-start | bytes 393224 | tf_op jit(solution)/shard_map/ppermute | solution.py:85
  43.7 7.2 %collective-permute-start.27 = (bf16[32,4096]{1,0:T(8,128)(2,1)S(1)}, bf16[32,4096]{1,0:T(8,128)(2,1)S(1)}, u32[]{:S(2)}, u32[]{:S(2)}) collective-permute-start(bf16[32,4096]{1,0:T(8,128)(2,1)S(1)} %get-tuple-element.136), channel_id=1, source_target_pairs={{0,1},{1,0},{2,3},{3,2},{4,5},{5,4},{6,7},{7,6},{8,24},{9,25},{10,... | collective-permute-start | bytes 786440 | tf_op jit(solution)/shard_map/ppermute | solution.py:85
  44.4 8.8 %collective-permute-start.24 = (bf16[32,4096]{1,0:T(8,128)(2,1)S(1)}, bf16[32,4096]{1,0:T(8,128)(2,1)S(1)}, u32[]{:S(2)}, u32[]{:S(2)}) collective-permute-start(bf16[32,4096]{1,0:T(8,128)(2,1)S(1)} %get-tuple-element.132), channel_id=1, source_target_pairs={{0,8},{1,9},{2,10},{3,11},{4,12},{5,13},{6,14},{7,15},{8,0},{9,1},... | collective-permute-start | bytes 786440 | tf_op jit(solution)/shard_map/ppermute | solution.py:85
  44.4 11.2 %collective-permute-start.15 = (bf16[32,4096]{1,0:T(8,128)(2,1)S(1)}, bf16[32,4096]{1,0:T(8,128)(2,1)S(1)}, u32[]{:S(2)}, u32[]{:S(2)}) collective-permute-start(bf16[32,4096]{1,0:T(8,128)(2,1)S(1)} %get-tuple-element.112), channel_id=1, source_target_pairs={{0,8},{1,9},{2,10},{3,11},{4,12},{5,13},{6,14},{7,15},{8,0},{9,1},... | collective-permute-start | bytes 786440 | tf_op jit(solution)/shard_map/ppermute | solution.py:85
  48.7 6.8 %collective-permute-start.25 = (bf16[32,4096]{1,0:T(8,128)(2,1)S(1)}, bf16[32,4096]{1,0:T(8,128)(2,1)S(1)}, u32[]{:S(2)}, u32[]{:S(2)}) collective-permute-start(bf16[32,4096]{1,0:T(8,128)(2,1)S(1)} %get-tuple-element.133), channel_id=1, source_target_pairs={{0,1},{1,0},{2,3},{3,2},{4,5},{5,4},{6,7},{7,6},{8,24},{9,25},{10,... | collective-permute-start | bytes 786440 | tf_op jit(solution)/shard_map/ppermute | solution.py:85
  49.5 10.8 %collective-permute-start.23 = (bf16[32,4096]{1,0:T(8,128)(2,1)S(1)}, bf16[32,4096]{1,0:T(8,128)(2,1)S(1)}, u32[]{:S(2)}, u32[]{:S(2)}) collective-permute-start(bf16[32,4096]{1,0:T(8,128)(2,1)S(1)} %get-tuple-element.130), channel_id=1, source_target_pairs={{0,1},{1,0},{2,3},{3,2},{4,5},{5,4},{6,7},{7,6},{8,24},{9,25},{10,... | collective-permute-start | bytes 786440 | tf_op jit(solution)/shard_map/ppermute | solution.py:85
  50.9 12.5 %collective-permute-start.29 = (bf16[16,4096]{1,0:T(8,128)(2,1)S(1)}, bf16[16,4096]{1,0:T(8,128)(2,1)S(1)}, u32[]{:S(2)}, u32[]{:S(2)}) collective-permute-start(bf16[16,4096]{1,0:T(8,128)(2,1)S(1)} %get-tuple-element.142), channel_id=1, source_target_pairs={{0,6},{1,7},{2,4},{3,5},{4,2},{5,3},{6,0},{7,1},{8,14},{9,15},{10,... | collective-permute-start | bytes 393224 | tf_op jit(solution)/shard_map/ppermute | solution.py:85
  53.2 8.4 %collective-permute-start.30 = (bf16[16,4096]{1,0:T(8,128)(2,1)S(1)}, bf16[16,4096]{1,0:T(8,128)(2,1)S(1)}, u32[]{:S(2)}, u32[]{:S(2)}) collective-permute-start(bf16[16,4096]{1,0:T(8,128)(2,1)S(1)} %get-tuple-element.144), channel_id=1, source_target_pairs={{0,16},{1,17},{2,18},{3,19},{4,20},{5,21},{6,22},{7,23},{8,9},{9,8... | collective-permute-start | bytes 393224 | tf_op jit(solution)/shard_map/ppermute | solution.py:85
  60.3 5.0 %collective-permute-start.28 = (bf16[16,4096]{1,0:T(8,128)(2,1)S(1)}, bf16[16,4096]{1,0:T(8,128)(2,1)S(1)}, u32[]{:S(2)}, u32[]{:S(2)}) collective-permute-start(bf16[16,4096]{1,0:T(8,128)(2,1)S(1)} %get-tuple-element.141), channel_id=1, source_target_pairs={{0,16},{1,17},{2,18},{3,19},{4,20},{5,21},{6,22},{7,23},{8,9},{9,8... | collective-permute-start | bytes 393224 | tf_op jit(solution)/shard_map/ppermute | solution.py:85
  61.6 7.3 %collective-permute-start.31 = (bf16[16,4096]{1,0:T(8,128)(2,1)S(1)}, bf16[16,4096]{1,0:T(8,128)(2,1)S(1)}, u32[]{:S(2)}, u32[]{:S(2)}) collective-permute-start(bf16[16,4096]{1,0:T(8,128)(2,1)S(1)} %get-tuple-element.148), channel_id=1, source_target_pairs={{0,4},{1,5},{2,6},{3,7},{4,0},{5,1},{6,2},{7,3},{8,12},{9,13},{10,... | collective-permute-start | bytes 393224 | tf_op jit(solution)/shard_map/ppermute | solution.py:85
  63.1 5.9 %collective-permute-start.32 = (bf16[16,4096]{1,0:T(8,128)(2,1)S(1)}, bf16[16,4096]{1,0:T(8,128)(2,1)S(1)}, u32[]{:S(2)}, u32[]{:S(2)}) collective-permute-start(bf16[16,4096]{1,0:T(8,128)(2,1)S(1)} %get-tuple-element.152), channel_id=1, source_target_pairs={{0,16},{1,17},{2,18},{3,19},{4,20},{5,21},{6,22},{7,23},{8,9},{9,8... | collective-permute-start | bytes 393224 | tf_op jit(solution)/shard_map/ppermute | solution.py:85
  65.4 5.0 %collective-permute-start.33 = (bf16[16,4096]{1,0:T(8,128)(2,1)S(1)}, bf16[16,4096]{1,0:T(8,128)(2,1)S(1)}, u32[]{:S(2)}, u32[]{:S(2)}) collective-permute-start(bf16[16,4096]{1,0:T(8,128)(2,1)S(1)} %get-tuple-element.155), channel_id=1, source_target_pairs={{0,2},{1,3},{2,0},{3,1},{4,6},{5,7},{6,4},{7,5},{8,10},{9,11},{10,... | collective-permute-start | bytes 393224 | tf_op jit(solution)/shard_map/ppermute | solution.py:85

commit v5 on v4

--- a/solution.py
+++ b/solution.py
@@ -36,35 +36,35 @@
 PARTS = 3
 PIECES = 4
 SEQUENCE = (
-    "stage1",
+    "stage1*",
     "pair0",
     "block3",
     "block1",
+    "stage2",
     "stage0",
-    "stage2",
     "block2 pair3 mine0 pair1",
     "pair2",
     "mine3",
     "expert0",
+    "expert3",
     "mine1",
-    "expert3",
-    "mine2 core3",
+    "mine2 core3*",
     "expert1",
     "expert2",
-    "far3",
-    "core0",
-    "core2",
-    "core1 near3",
-    "far2",
-    "far0",
-    "far1",
+    "core0 far3*",
+    "core2*",
+    "core1 near3*",
+    "far2*",
+    "far1*",
     "near2",
-    "near1 fold3",
+    "near1 fold3*",
+    "far0*",
     "fold2",
+    "fold1*",
     "near0",
-    "fold1",
 )
 WEIGHT = 20
+LONG = 10**10
 
 IN_VMEM = pl.BlockSpec(memory_space=pltpu.VMEM)
 IN_HBM = pl.BlockSpec(memory_space=pltpu.HBM)
@@ -135,7 +135,7 @@
     return value if isinstance(value, tuple) else (value, 0, value.shape[0])
 
 
-def together(order, steps, last):
+def together(order, steps, last, flops):
     arrays, reads, outs, writes, place = [], [], [], [], {}
     for run, _, shapes, values in steps:
         read = []
@@ -163,7 +163,7 @@
             part(*views)
 
     shapes = [((rows, width), dtype) for rows, width, dtype in outs]
-    results = order(body, "sums", shapes, arrays, last=last)
+    results = order(body, "sums", shapes, arrays, flops=flops, last=last)
     return results, writes
 
 
@@ -217,24 +217,25 @@
     return out
 
 
-def stage_body(source, out, sems):
-    size = source.shape[0] // PIECES
-    pieces = [pl.ds(i * size, size) for i in range(PIECES)]
-    copies = [
-        pltpu.make_async_copy(source.at[piece], out.at[piece], sems.at[i])
-        for i, piece in enumerate(pieces)
-    ]
+def stage_body(*refs):
+    *pairs, sems = refs
+    count = len(pairs) // 2
+    copies = []
+    for i, (source, out) in enumerate(zip(pairs[:count], pairs[count:])):
+        size = source.shape[0] // PIECES
+        for j in range(PIECES):
+            piece = pl.ds(j * size, size)
+            copies.append(pltpu.make_async_copy(source.at[piece], out.at[piece], sems.at[i, j]))
     for copy in copies:
         copy.start()
     for copy in copies:
         copy.wait()
 
 
-def staged(order, weight):
-    outs = [(weight.shape, weight.dtype)]
-    scratch = [pltpu.SemaphoreType.DMA((PIECES,))]
-    [result] = order(stage_body, "stage", outs, (weight,), scratch, far=1)
-    return result
+def staged(order, weights, flops):
+    outs = [(w.shape, w.dtype) for w in weights]
+    scratch = [pltpu.SemaphoreType.DMA((len(weights), PIECES))]
+    return order(stage_body, "stage", outs, weights, scratch, far=len(weights), flops=flops)
 
 
 def pack_body(block, received, out):
@@ -371,10 +372,13 @@
     final = (SEQUENCE[-1][:-1], int(SEQUENCE[-1][-1]))
     whole = []
     for group in SEQUENCE:
+        group, flops = group.rstrip("*"), LONG if group.endswith("*") else 0
         runs = [[(name[:-1], int(name[-1])) for name in run.split("+")] for run in group.split()]
         kind, step = runs[0][0]
         if kind == "stage":
-            weights[step] = staged(order, weights[step])
+            which = [step for _, step in runs[0]]
+            for step, weight in zip(which, staged(order, [weights[i] for i in which], flops)):
+                weights[step] = weight
         elif kind == "expert":
             results = expert_rows(order, mine[step], others[step], weights, experts)
             kept[step], sent[step], more_kept[step], more_sent[step] = results
@@ -382,7 +386,7 @@
             more_kept[step] = over_core(more_kept[step])
         else:
             steps = [(i, *inputs(*name)) for i, run in enumerate(runs) for name in run]
-            results, writes = together(order, steps, group is SEQUENCE[-1])
+            results, writes = together(order, steps, group == SEQUENCE[-1], flops)
             for i, run in enumerate(runs):
                 at = [write for step, write in zip(steps, writes) if step[0] == i]
                 passed_on(run[0][0], [step for _, step in run], results, at)

time: 71.3 us -> 69.7 us (0.978)
  starting transfers between devices: 31.4 us -> 29.2 us
  waiting for transfers between devices: 23.1 us -> 23.9 us
    ppermute x34, starting transfers between devices: 31.4 us -> 29.2 us  [moved(): return lax.ppermute(value, MESH_AXES, pairs)]
    ppermute x34, waiting for transfers between devices: 23.1 us -> 23.9 us  [moved(): return lax.ppermute(value, MESH_AXES, pairs)]
    pallas_call x28 -> x27, Pallas kernels: 15.7 us -> 15.6 us  [__call__(): pl.pallas_call(marked, name=name, out_shape=[pltpu.VMEM(shape, dtype) for...]
  transfers between devices with their start and end apart: 34 -> 34, of which waited for: 12 -> 11; matrix products, arithmetic and copies ran while one was open for 0% -> 0% of each run, Pallas kernels for 20% -> 21%
where the time goes in v5:
time: 69.7 us; the launch traced here: 69.6 us
  starting transfers between devices  29.2 us (42%)
  waiting for transfers between devices  23.9 us (34%)
  Pallas kernels  15.6 us (22%)
    ppermute x34, starting transfers between devices, moved(): return lax.ppermute(value, MESH_AXES, pairs)  29.2 us
    ppermute x34, waiting for transfers between devices, moved(): return lax.ppermute(value, MESH_AXES, pairs)  23.9 us
    pallas_call x27, Pallas kernels, __call__(): pl.pallas_call(marked, name=name, out_shape=[pltpu.VMEM(shape, dtype) for...  15.6 us
  transfers between devices with their start and end apart: 34, of which 11 were waited for; matrix products, arithmetic and copies ran while one was open for 0% of the time, Pallas kernels for 21%

profile of v5, /device:TPU:0, one launch (start us, length us, event | category | flops | bytes accessed | tf_op | source)
XLA Modules:
  0.0 69.6 jit_solution(14162159188455042167)
XLA Ops:
  0.0 1.2 %label.1 = (bf16[16,4224]{1,0:T(8,128)(2,1)S(1)}, f32[8,128]{1,0:T(8,128)S(1)}) custom-call(bf16[16,4096]{1,0:T(8,128)(2,1)} %refs_0_.1, s32[8,16]{1,0:T(8,128)} %bitcast.7, f32[8,16]{1,0:T(8,128)} %bitcast.8, s32[16]{0:T(128)} %refs_3_.1, s32[16]{0:T(128)} %refs_4_.1), custom_call_target="tpu_custom_call" | custom-call | tf_op jit(solution)/shard_map/label/pallas_call | solution.py:120
  1.2 5.1 %collective-permute-start.1 = (bf16[16,4224]{1,0:T(8,128)(2,1)S(1)}, bf16[16,4224]{1,0:T(8,128)(2,1)S(1)}, u32[]{:S(2)}, u32[]{:S(2)}) collective-permute-start(bf16[16,4224]{1,0:T(8,128)(2,1)S(1)} %get-tuple-element.80.refs_0_), channel_id=1, source_target_pairs={{0,6},{1,7},{2,4},{3,5},{4,2},{5,3},{6,0},{7,1},{8,14},{9,15},{10,... | collective-permute-start | bytes 405512 | tf_op jit(solution)/shard_map/ppermute | solution.py:85
  6.3 1.5 %collective-permute-start.2 = (bf16[16,4224]{1,0:T(8,128)(2,1)S(1)}, bf16[16,4224]{1,0:T(8,128)(2,1)S(1)}, u32[]{:S(2)}, u32[]{:S(2)}) collective-permute-start(bf16[16,4224]{1,0:T(8,128)(2,1)S(1)} %get-tuple-element.80.refs_0_), channel_id=1, source_target_pairs={{0,16},{1,17},{2,18},{3,19},{4,20},{5,21},{6,22},{7,23},{8,9},{9,8... | collective-permute-start | bytes 405512 | tf_op jit(solution)/shard_map/ppermute | solution.py:85
  7.8 1.9 %stage.3 = (bf16[4096,384]{1,0:T(8,128)(2,1)S(1)}, f32[8,128]{1,0:T(8,128)S(1)}) custom-call(bf16[4096,384]{1,0:T(8,128)(2,1)} %bitcast.9, f32[8,128]{1,0:T(8,128)S(1)} %get-tuple-element.81.refs_1_), custom_call_target="tpu_custom_call" | custom-call | flops 10000000000 | tf_op jit(solution)/shard_map/stage/pallas_call | solution.py:120
  9.7 1.6 %collective-permute-done.2.refs_1_ = bf16[16,4224]{1,0:T(8,128)(2,1)S(1)} collective-permute-done((bf16[16,4224]{1,0:T(8,128)(2,1)S(1)}, bf16[16,4224]{1,0:T(8,128)(2,1)S(1)}, u32[]{:S(2)}, u32[]{:S(2)}) %collective-permute-start.2) | collective-permute-done | bytes 135200 | tf_op jit(solution)/shard_map/ppermute | solution.py:85
  11.4 1.6 %collective-permute-start.4 = (bf16[32,4224]{1,0:T(8,128)(2,1)S(1)}, bf16[32,4224]{1,0:T(8,128)(2,1)S(1)}, u32[]{:S(2)}, u32[]{:S(2)}) collective-permute-start(bf16[32,4224]{1,0:T(8,128)(2,1)S(1)} %get-tuple-element.85.refs_3_), channel_id=1, source_target_pairs={{0,1},{1,0},{2,3},{3,2},{4,5},{5,4},{6,7},{7,6},{8,24},{9,25},{10,... | collective-permute-start | bytes 811016 | tf_op jit(solution)/shard_map/ppermute | solution.py:85
  13.0 1.6 %collective-permute-start.3 = (bf16[16,4224]{1,0:T(8,128)(2,1)S(1)}, bf16[16,4224]{1,0:T(8,128)(2,1)S(1)}, u32[]{:S(2)}, u32[]{:S(2)}) collective-permute-start(bf16[16,4224]{1,0:T(8,128)(2,1)S(1)} %get-tuple-element.84.refs_1_), channel_id=1, source_target_pairs={{0,16},{1,17},{2,18},{3,19},{4,20},{5,21},{6,22},{7,23},{8,9},{9,8... | collective-permute-start | bytes 405512 | tf_op jit(solution)/shard_map/ppermute | solution.py:85
  14.5 0.6 collective-permute-start.6
  15.1 1.9 %stage.4 = (bf16[384,4096]{1,0:T(8,128)(2,1)S(1)}, f32[8,128]{1,0:T(8,128)S(1)}) custom-call(bf16[384,4096]{1,0:T(8,128)(2,1)} %bitcast.5, f32[8,128]{1,0:T(8,128)S(1)} %get-tuple-element.88.refs_1_), custom_call_target="tpu_custom_call" | custom-call | tf_op jit(solution)/shard_map/stage/pallas_call | solution.py:120
  17.0 1.9 %stage.5 = (bf16[4096,384]{1,0:T(8,128)(2,1)S(1)}, f32[8,128]{1,0:T(8,128)S(1)}) custom-call(bf16[4096,384]{1,0:T(8,128)(2,1)} %bitcast.6, f32[8,128]{1,0:T(8,128)S(1)} %get-tuple-element.89.refs_1_), custom_call_target="tpu_custom_call" | custom-call | tf_op jit(solution)/shard_map/stage/pallas_call | solution.py:120
  18.9 1.7 %collective-permute-done.refs_0_ = bf16[16,4224]{1,0:T(8,128)(2,1)S(1)} collective-permute-done((bf16[16,4224]{1,0:T(8,128)(2,1)S(1)}, bf16[16,4224]{1,0:T(8,128)(2,1)S(1)}, u32[]{:S(2)}, u32[]{:S(2)}) %collective-permute-start) | collective-permute-done | bytes 135200 | tf_op jit(solution)/shard_map/ppermute | solution.py:85
  20.8 0.8 %collective-permute-start.8 = (bf16[32,4224]{1,0:T(8,128)(2,1)S(1)}, bf16[32,4224]{1,0:T(8,128)(2,1)S(1)}, u32[]{:S(2)}, u32[]{:S(2)}) collective-permute-start(bf16[32,4224]{1,0:T(8,128)(2,1)S(1)} %get-tuple-element.92.refs_0_), channel_id=1, source_target_pairs={{0,1},{1,0},{2,3},{3,2},{4,5},{5,4},{6,7},{7,6},{8,24},{9,25},{10,... | collective-permute-start | bytes 811016 | tf_op jit(solution)/shard_map/ppermute | solution.py:85
  21.6 1.0 %collective-permute-start.9 = (bf16[16,4224]{1,0:T(8,128)(2,1)S(1)}, bf16[16,4224]{1,0:T(8,128)(2,1)S(1)}, u32[]{:S(2)}, u32[]{:S(2)}) collective-permute-start(bf16[16,4224]{1,0:T(8,128)(2,1)S(1)} %get-tuple-element.93.refs_0_), channel_id=1, source_target_pairs={{0,16},{1,17},{2,18},{3,19},{4,20},{5,21},{6,22},{7,23},{8,9},{9,8... | collective-permute-start | bytes 405512 | tf_op jit(solution)/shard_map/ppermute | solution.py:85
  22.5 0.9 %collective-permute-start.7 = (bf16[32,4224]{1,0:T(8,128)(2,1)S(1)}, bf16[32,4224]{1,0:T(8,128)(2,1)S(1)}, u32[]{:S(2)}, u32[]{:S(2)}) collective-permute-start(bf16[32,4224]{1,0:T(8,128)(2,1)S(1)} %get-tuple-element.91.refs_0_), channel_id=1, source_target_pairs={{0,1},{1,0},{2,3},{3,2},{4,5},{5,4},{6,7},{7,6},{8,24},{9,25},{10,... | collective-permute-start | bytes 811016 | tf_op jit(solution)/shard_map/ppermute | solution.py:85
  23.4 4.6 %collective-permute-done.9.refs_1_ = bf16[16,4224]{1,0:T(8,128)(2,1)S(1)} collective-permute-done((bf16[16,4224]{1,0:T(8,128)(2,1)S(1)}, bf16[16,4224]{1,0:T(8,128)(2,1)S(1)}, u32[]{:S(2)}, u32[]{:S(2)}) %collective-permute-start.9) | collective-permute-done | bytes 135200 | tf_op jit(solution)/shard_map/ppermute | solution.py:85
  28.1 1.4 %collective-permute-start.13 = (bf16[32,4224]{1,0:T(8,128)(2,1)S(1)}, bf16[32,4224]{1,0:T(8,128)(2,1)S(1)}, u32[]{:S(2)}, u32[]{:S(2)}) collective-permute-start(bf16[32,4224]{1,0:T(8,128)(2,1)S(1)} %get-tuple-element.105.refs_0_), channel_id=1, source_target_pairs={{0,1},{1,0},{2,3},{3,2},{4,5},{5,4},{6,7},{7,6},{8,24},{9,25},{10,... | collective-permute-start | bytes 811016 | tf_op jit(solution)/shard_map/ppermute | solution.py:85
  29.6 1.9 %expert.4 = (bf16[32,4096]{1,0:T(8,128)(2,1)S(1)}, bf16[32,4096]{1,0:T(8,128)(2,1)S(1)}, bf16[32,4096]{1,0:T(8,128)(2,1)S(1)}, bf16[32,4096]{1,0:T(8,128)(2,1)S(1)}, f32[8,128]{1,0:T(8,128)S(1)}) custom-call(bf16[64,4224]{1,0:T(8,128)(2,1)S(1)} %get-tuple-element.100.refs_0_, bf16[64,4224]{1,0:T(8,128)(2,1)S(1)} %collective-permute-done.11.refs_1_, ...), custom_call_target="tpu_custom_call" | custom-call | flops 24159191040 | tf_op jit(solution)/shard_map/expert/pallas_call | solution.py:120
  31.6 1.9 %expert.5 = (bf16[32,4096]{1,0:T(8,128)(2,1)S(1)}, bf16[32,4096]{1,0:T(8,128)(2,1)S(1)}, bf16[32,4096]{1,0:T(8,128)(2,1)S(1)}, bf16[32,4096]{1,0:T(8,128)(2,1)S(1)}, f32[8,128]{1,0:T(8,128)S(1)}) custom-call(bf16[64,4224]{1,0:T(8,128)(2,1)S(1)} %get-tuple-element.96.refs_0_, bf16[64,4224]{1,0:T(8,128)(2,1)S(1)} %collective-permute-done.10.refs_1_, ...), custom_call_target="tpu_custom_call" | custom-call | flops 24159191040 | tf_op jit(solution)/shard_map/expert/pallas_call | solution.py:120
  33.5 0.6 collective-permute-start.14
  34.2 0.5 collective-permute-start.12
  34.8 0.5 collective-permute-done.14.refs_3_
  35.2 0.1 sums.26
  35.4 0.8 %collective-permute-start.19 = (bf16[32,4096]{1,0:T(8,128)(2,1)S(1)}, bf16[32,4096]{1,0:T(8,128)(2,1)S(1)}, u32[]{:S(2)}, u32[]{:S(2)}) collective-permute-start(bf16[32,4096]{1,0:T(8,128)(2,1)S(1)} %get-tuple-element.118), channel_id=1, source_target_pairs={{0,1},{1,0},{2,3},{3,2},{4,5},{5,4},{6,7},{7,6},{8,24},{9,25},{10,... | collective-permute-start | bytes 786440 | tf_op jit(solution)/shard_map/ppermute | solution.py:85
  36.2 0.2 collective-permute-done.12.refs_1_
  36.4 1.9 %expert.6 = (bf16[32,4096]{1,0:T(8,128)(2,1)S(1)}, bf16[32,4096]{1,0:T(8,128)(2,1)S(1)}, bf16[32,4096]{1,0:T(8,128)(2,1)S(1)}, bf16[32,4096]{1,0:T(8,128)(2,1)S(1)}, f32[8,128]{1,0:T(8,128)S(1)}) custom-call(bf16[64,4224]{1,0:T(8,128)(2,1)S(1)} %get-tuple-element.104.refs_0_, bf16[64,4224]{1,0:T(8,128)(2,1)S(1)} %collective-permute-done.12.refs_1_, ...), custom_call_target="tpu_custom_call" | custom-call | flops 24159191040 | tf_op jit(solution)/shard_map/expert/pallas_call | solution.py:120
  38.3 0.4 collective-permute-start.15
  38.7 0.1 collective-permute-start.16
  38.9 1.9 %expert.7 = (bf16[32,4096]{1,0:T(8,128)(2,1)S(1)}, bf16[32,4096]{1,0:T(8,128)(2,1)S(1)}, bf16[32,4096]{1,0:T(8,128)(2,1)S(1)}, bf16[32,4096]{1,0:T(8,128)(2,1)S(1)}, f32[8,128]{1,0:T(8,128)S(1)}) custom-call(bf16[64,4224]{1,0:T(8,128)(2,1)S(1)} %get-tuple-element.119.refs_0_, bf16[64,4224]{1,0:T(8,128)(2,1)S(1)} %collective-permute-done.20.refs_1_, ...), custom_call_target="tpu_custom_call" | custom-call | flops 24159191040 | tf_op jit(solution)/shard_map/expert/pallas_call | solution.py:120
  40.8 0.4 collective-permute-start.22
  41.3 0.5 collective-permute-done.19.refs_4_
  41.8 0.2 sums.27
  41.9 0.6 collective-permute-start.21
  42.6 1.2 %collective-permute-start.25 = (bf16[32,4096]{1,0:T(8,128)(2,1)S(1)}, bf16[32,4096]{1,0:T(8,128)(2,1)S(1)}, u32[]{:S(2)}, u32[]{:S(2)}) collective-permute-start(bf16[32,4096]{1,0:T(8,128)(2,1)S(1)} %get-tuple-element.131), channel_id=1, source_target_pairs={{0,1},{1,0},{2,3},{3,2},{4,5},{5,4},{6,7},{7,6},{8,24},{9,25},{10,... | collective-permute-start | bytes 786440 | tf_op jit(solution)/shard_map/ppermute | solution.py:85
  43.8 4.4 %collective-permute-done.21.refs_3_ = bf16[16,4096]{1,0:T(8,128)(2,1)S(1)} collective-permute-done((bf16[16,4096]{1,0:T(8,128)(2,1)S(1)}, bf16[16,4096]{1,0:T(8,128)(2,1)S(1)}, u32[]{:S(2)}, u32[]{:S(2)}) %collective-permute-start.21) | collective-permute-done | bytes 131104 | tf_op jit(solution)/shard_map/ppermute | solution.py:85
  48.2 0.1 sums.29
  48.3 0.5 collective-permute-start.23
  48.8 1.7 %collective-permute-start.27 = (bf16[16,4096]{1,0:T(8,128)(2,1)S(1)}, bf16[16,4096]{1,0:T(8,128)(2,1)S(1)}, u32[]{:S(2)}, u32[]{:S(2)}) collective-permute-start(bf16[16,4096]{1,0:T(8,128)(2,1)S(1)} %get-tuple-element.136), channel_id=1, source_target_pairs={{0,6},{1,7},{2,4},{3,5},{4,2},{5,3},{6,0},{7,1},{8,14},{9,15},{10,... | collective-permute-start | bytes 393224 | tf_op jit(solution)/shard_map/ppermute | solution.py:85
  50.5 0.1 sums.30
  50.6 1.7 %collective-permute-start.28 = (bf16[16,4096]{1,0:T(8,128)(2,1)S(1)}, bf16[16,4096]{1,0:T(8,128)(2,1)S(1)}, u32[]{:S(2)}, u32[]{:S(2)}) collective-permute-start(bf16[16,4096]{1,0:T(8,128)(2,1)S(1)} %get-tuple-element.138), channel_id=1, source_target_pairs={{0,16},{1,17},{2,18},{3,19},{4,20},{5,21},{6,22},{7,23},{8,9},{9,8... | collective-permute-start | bytes 393224 | tf_op jit(solution)/shard_map/ppermute | solution.py:85
  52.3 4.4 %collective-permute-done.23.refs_2_ = bf16[32,4096]{1,0:T(8,128)(2,1)S(1)} collective-permute-done((bf16[32,4096]{1,0:T(8,128)(2,1)S(1)}, bf16[32,4096]{1,0:T(8,128)(2,1)S(1)}, u32[]{:S(2)}, u32[]{:S(2)}) %collective-permute-start.23) | collective-permute-done | bytes 262176 | tf_op jit(solution)/shard_map/ppermute | solution.py:85
  56.7 0.1 sums.31
  56.9 0.4 collective-permute-start.31
  57.4 3.3 %collective-permute-start.29 = (bf16[16,4096]{1,0:T(8,128)(2,1)S(1)}, bf16[16,4096]{1,0:T(8,128)(2,1)S(1)}, u32[]{:S(2)}, u32[]{:S(2)}) collective-permute-start(bf16[16,4096]{1,0:T(8,128)(2,1)S(1)} %get-tuple-element.142), channel_id=1, source_target_pairs={{0,4},{1,5},{2,6},{3,7},{4,0},{5,1},{6,2},{7,3},{8,12},{9,13},{10,... | collective-permute-start | bytes 393224 | tf_op jit(solution)/shard_map/ppermute | solution.py:85
  60.7 2.5 %collective-permute-done.26.refs_1_ = bf16[16,4096]{1,0:T(8,128)(2,1)S(1)} collective-permute-done((bf16[16,4096]{1,0:T(8,128)(2,1)S(1)}, bf16[16,4096]{1,0:T(8,128)(2,1)S(1)}, u32[]{:S(2)}, u32[]{:S(2)}) %collective-permute-start.26) | collective-permute-done | bytes 131104 | tf_op jit(solution)/shard_map/ppermute | solution.py:85
  63.5 1.9 %collective-permute-start.33 = (bf16[16,4096]{1,0:T(8,128)(2,1)S(1)}, bf16[16,4096]{1,0:T(8,128)(2,1)S(1)}, u32[]{:S(2)}, u32[]{:S(2)}) collective-permute-start(bf16[16,4096]{1,0:T(8,128)(2,1)S(1)} %get-tuple-element.153), channel_id=1, source_target_pairs={{0,16},{1,17},{2,18},{3,19},{4,20},{5,21},{6,22},{7,23},{8,9},{9,8... | collective-permute-start | bytes 393224 | tf_op jit(solution)/shard_map/ppermute | solution.py:85
  65.4 2.0 %collective-permute-done.29.refs_1_ = bf16[16,4096]{1,0:T(8,128)(2,1)S(1)} collective-permute-done((bf16[16,4096]{1,0:T(8,128)(2,1)S(1)}, bf16[16,4096]{1,0:T(8,128)(2,1)S(1)}, u32[]{:S(2)}, u32[]{:S(2)}) %collective-permute-start.29) | collective-permute-done | bytes 131104 | tf_op jit(solution)/shard_map/ppermute | solution.py:85
  67.5 1.4 %collective-permute-done.32.refs_1_ = bf16[16,4096]{1,0:T(8,128)(2,1)S(1)} collective-permute-done((bf16[16,4096]{1,0:T(8,128)(2,1)S(1)}, bf16[16,4096]{1,0:T(8,128)(2,1)S(1)}, u32[]{:S(2)}, u32[]{:S(2)}) %collective-permute-start.32) | collective-permute-done | bytes 131104 | tf_op jit(solution)/shard_map/ppermute | solution.py:85
  68.9 0.7 copy.9
  (48 shorter events, 1.1 us)
Async XLA Ops:
  1.2 11.7 %collective-permute-start.1 = (bf16[16,4224]{1,0:T(8,128)(2,1)S(1)}, bf16[16,4224]{1,0:T(8,128)(2,1)S(1)}, u32[]{:S(2)}, u32[]{:S(2)}) collective-permute-start(bf16[16,4224]{1,0:T(8,128)(2,1)S(1)} %get-tuple-element.80.refs_0_), channel_id=1, source_target_pairs={{0,6},{1,7},{2,4},{3,5},{4,2},{5,3},{6,0},{7,1},{8,14},{9,15},{10,... | collective-permute-start | bytes 405512 | tf_op jit(solution)/shard_map/ppermute | solution.py:85
  6.3 5.0 %collective-permute-start.2 = (bf16[16,4224]{1,0:T(8,128)(2,1)S(1)}, bf16[16,4224]{1,0:T(8,128)(2,1)S(1)}, u32[]{:S(2)}, u32[]{:S(2)}) collective-permute-start(bf16[16,4224]{1,0:T(8,128)(2,1)S(1)} %get-tuple-element.80.refs_0_), channel_id=1, source_target_pairs={{0,16},{1,17},{2,18},{3,19},{4,20},{5,21},{6,22},{7,23},{8,9},{9,8... | collective-permute-start | bytes 405512 | tf_op jit(solution)/shard_map/ppermute | solution.py:85
  7.8 6.7 %collective-permute-start.5 = (bf16[16,4224]{1,0:T(8,128)(2,1)S(1)}, bf16[16,4224]{1,0:T(8,128)(2,1)S(1)}, u32[]{:S(2)}, u32[]{:S(2)}) collective-permute-start(bf16[16,4224]{1,0:T(8,128)(2,1)S(1)} %get-tuple-element.80.refs_0_), channel_id=1, source_target_pairs={{0,2},{1,3},{2,0},{3,1},{4,6},{5,7},{6,4},{7,5},{8,10},{9,11},{10,... | collective-permute-start | bytes 405512 | tf_op jit(solution)/shard_map/ppermute | solution.py:85
  11.4 9.3 %collective-permute-start.4 = (bf16[32,4224]{1,0:T(8,128)(2,1)S(1)}, bf16[32,4224]{1,0:T(8,128)(2,1)S(1)}, u32[]{:S(2)}, u32[]{:S(2)}) collective-permute-start(bf16[32,4224]{1,0:T(8,128)(2,1)S(1)} %get-tuple-element.85.refs_3_), channel_id=1, source_target_pairs={{0,1},{1,0},{2,3},{3,2},{4,5},{5,4},{6,7},{7,6},{8,24},{9,25},{10,... | collective-permute-start | bytes 811016 | tf_op jit(solution)/shard_map/ppermute | solution.py:85
  12.9 7.7 %collective-permute-start = (bf16[16,4224]{1,0:T(8,128)(2,1)S(1)}, bf16[16,4224]{1,0:T(8,128)(2,1)S(1)}, u32[]{:S(2)}, u32[]{:S(2)}) collective-permute-start(bf16[16,4224]{1,0:T(8,128)(2,1)S(1)} %get-tuple-element.80.refs_0_), channel_id=1, source_target_pairs={{0,4},{1,5},{2,6},{3,7},{4,0},{5,1},{6,2},{7,3},{8,12},{9,13},{10,... | collective-permute-start | bytes 405512 | tf_op jit(solution)/shard_map/ppermute | solution.py:85
  13.0 7.7 %collective-permute-start.3 = (bf16[16,4224]{1,0:T(8,128)(2,1)S(1)}, bf16[16,4224]{1,0:T(8,128)(2,1)S(1)}, u32[]{:S(2)}, u32[]{:S(2)}) collective-permute-start(bf16[16,4224]{1,0:T(8,128)(2,1)S(1)} %get-tuple-element.84.refs_1_), channel_id=1, source_target_pairs={{0,16},{1,17},{2,18},{3,19},{4,20},{5,21},{6,22},{7,23},{8,9},{9,8... | collective-permute-start | bytes 405512 | tf_op jit(solution)/shard_map/ppermute | solution.py:85
  14.5 6.1 %collective-permute-start.6 = (bf16[16,4224]{1,0:T(8,128)(2,1)S(1)}, bf16[16,4224]{1,0:T(8,128)(2,1)S(1)}, u32[]{:S(2)}, u32[]{:S(2)}) collective-permute-start(bf16[16,4224]{1,0:T(8,128)(2,1)S(1)} %get-tuple-element.87.refs_5_), channel_id=1, source_target_pairs={{0,16},{1,17},{2,18},{3,19},{4,20},{5,21},{6,22},{7,23},{8,9},{9,8... | collective-permute-start | bytes 405512 | tf_op jit(solution)/shard_map/ppermute | solution.py:85
  20.7 8.9 %collective-permute-start.11 = (bf16[64,4224]{1,0:T(8,128)(2,1)S(1)}, bf16[64,4224]{1,0:T(8,128)(2,1)S(1)}, u32[]{:S(2)}, u32[]{:S(2)}) collective-permute-start(bf16[64,4224]{1,0:T(8,128)(2,1)S(1)} %get-tuple-element.100.refs_0_), channel_id=1, source_target_pairs={{0,8},{1,9},{2,10},{3,11},{4,12},{5,13},{6,14},{7,15},{8,0},{9,1},... | collective-permute-start | bytes 1622024 | tf_op jit(solution)/shard_map/ppermute | solution.py:85
  20.8 8.7 %collective-permute-start.8 = (bf16[32,4224]{1,0:T(8,128)(2,1)S(1)}, bf16[32,4224]{1,0:T(8,128)(2,1)S(1)}, u32[]{:S(2)}, u32[]{:S(2)}) collective-permute-start(bf16[32,4224]{1,0:T(8,128)(2,1)S(1)} %get-tuple-element.92.refs_0_), channel_id=1, source_target_pairs={{0,1},{1,0},{2,3},{3,2},{4,5},{5,4},{6,7},{7,6},{8,24},{9,25},{10,... | collective-permute-start | bytes 811016 | tf_op jit(solution)/shard_map/ppermute | solution.py:85
  21.6 6.5 %collective-permute-start.9 = (bf16[16,4224]{1,0:T(8,128)(2,1)S(1)}, bf16[16,4224]{1,0:T(8,128)(2,1)S(1)}, u32[]{:S(2)}, u32[]{:S(2)}) collective-permute-start(bf16[16,4224]{1,0:T(8,128)(2,1)S(1)} %get-tuple-element.93.refs_0_), channel_id=1, source_target_pairs={{0,16},{1,17},{2,18},{3,19},{4,20},{5,21},{6,22},{7,23},{8,9},{9,8... | collective-permute-start | bytes 405512 | tf_op jit(solution)/shard_map/ppermute | solution.py:85
  22.5 11.6 %collective-permute-start.7 = (bf16[32,4224]{1,0:T(8,128)(2,1)S(1)}, bf16[32,4224]{1,0:T(8,128)(2,1)S(1)}, u32[]{:S(2)}, u32[]{:S(2)}) collective-permute-start(bf16[32,4224]{1,0:T(8,128)(2,1)S(1)} %get-tuple-element.91.refs_0_), channel_id=1, source_target_pairs={{0,1},{1,0},{2,3},{3,2},{4,5},{5,4},{6,7},{7,6},{8,24},{9,25},{10,... | collective-permute-start | bytes 811016 | tf_op jit(solution)/shard_map/ppermute | solution.py:85
  28.1 6.7 %collective-permute-start.13 = (bf16[32,4224]{1,0:T(8,128)(2,1)S(1)}, bf16[32,4224]{1,0:T(8,128)(2,1)S(1)}, u32[]{:S(2)}, u32[]{:S(2)}) collective-permute-start(bf16[32,4224]{1,0:T(8,128)(2,1)S(1)} %get-tuple-element.105.refs_0_), channel_id=1, source_target_pairs={{0,1},{1,0},{2,3},{3,2},{4,5},{5,4},{6,7},{7,6},{8,24},{9,25},{10,... | collective-permute-start | bytes 811016 | tf_op jit(solution)/shard_map/ppermute | solution.py:85
  29.6 2.0 %collective-permute-start.10 = (bf16[64,4224]{1,0:T(8,128)(2,1)S(1)}, bf16[64,4224]{1,0:T(8,128)(2,1)S(1)}, u32[]{:S(2)}, u32[]{:S(2)}) collective-permute-start(bf16[64,4224]{1,0:T(8,128)(2,1)S(1)} %get-tuple-element.96.refs_0_), channel_id=1, source_target_pairs={{0,8},{1,9},{2,10},{3,11},{4,12},{5,13},{6,14},{7,15},{8,0},{9,1},... | collective-permute-start | bytes 1622024 | tf_op jit(solution)/shard_map/ppermute | solution.py:85
  33.5 1.7 %collective-permute-start.14 = (bf16[32,4096]{1,0:T(8,128)(2,1)S(1)}, bf16[32,4096]{1,0:T(8,128)(2,1)S(1)}, u32[]{:S(2)}, u32[]{:S(2)}) collective-permute-start(bf16[32,4096]{1,0:T(8,128)(2,1)S(1)} %get-tuple-element.107), channel_id=1, source_target_pairs={{0,8},{1,9},{2,10},{3,11},{4,12},{5,13},{6,14},{7,15},{8,0},{9,1},... | collective-permute-start | bytes 786440 | tf_op jit(solution)/shard_map/ppermute | solution.py:85
  34.1 6.8 %collective-permute-start.17 = (bf16[32,4096]{1,0:T(8,128)(2,1)S(1)}, bf16[32,4096]{1,0:T(8,128)(2,1)S(1)}, u32[]{:S(2)}, u32[]{:S(2)}) collective-permute-start(bf16[32,4096]{1,0:T(8,128)(2,1)S(1)} %get-tuple-element.115), channel_id=1, source_target_pairs={{0,8},{1,9},{2,10},{3,11},{4,12},{5,13},{6,14},{7,15},{8,0},{9,1},... | collective-permute-start | bytes 786440 | tf_op jit(solution)/shard_map/ppermute | solution.py:85
  34.2 2.2 %collective-permute-start.12 = (bf16[64,4224]{1,0:T(8,128)(2,1)S(1)}, bf16[64,4224]{1,0:T(8,128)(2,1)S(1)}, u32[]{:S(2)}, u32[]{:S(2)}) collective-permute-start(bf16[64,4224]{1,0:T(8,128)(2,1)S(1)} %get-tuple-element.104.refs_0_), channel_id=1, source_target_pairs={{0,8},{1,9},{2,10},{3,11},{4,12},{5,13},{6,14},{7,15},{8,0},{9,1},... | collective-permute-start | bytes 1622024 | tf_op jit(solution)/shard_map/ppermute | solution.py:85
  34.7 6.6 %collective-permute-start.18 = (bf16[32,4096]{1,0:T(8,128)(2,1)S(1)}, bf16[32,4096]{1,0:T(8,128)(2,1)S(1)}, u32[]{:S(2)}, u32[]{:S(2)}) collective-permute-start(bf16[32,4096]{1,0:T(8,128)(2,1)S(1)} %get-tuple-element.117), channel_id=1, source_target_pairs={{0,8},{1,9},{2,10},{3,11},{4,12},{5,13},{6,14},{7,15},{8,0},{9,1},... | collective-permute-start | bytes 786440 | tf_op jit(solution)/shard_map/ppermute | solution.py:85
  35.4 6.4 %collective-permute-start.19 = (bf16[32,4096]{1,0:T(8,128)(2,1)S(1)}, bf16[32,4096]{1,0:T(8,128)(2,1)S(1)}, u32[]{:S(2)}, u32[]{:S(2)}) collective-permute-start(bf16[32,4096]{1,0:T(8,128)(2,1)S(1)} %get-tuple-element.118), channel_id=1, source_target_pairs={{0,1},{1,0},{2,3},{3,2},{4,5},{5,4},{6,7},{7,6},{8,24},{9,25},{10,... | collective-permute-start | bytes 786440 | tf_op jit(solution)/shard_map/ppermute | solution.py:85
  36.2 2.6 %collective-permute-start.20 = (bf16[64,4224]{1,0:T(8,128)(2,1)S(1)}, bf16[64,4224]{1,0:T(8,128)(2,1)S(1)}, u32[]{:S(2)}, u32[]{:S(2)}) collective-permute-start(bf16[64,4224]{1,0:T(8,128)(2,1)S(1)} %get-tuple-element.119.refs_0_), channel_id=1, source_target_pairs={{0,8},{1,9},{2,10},{3,11},{4,12},{5,13},{6,14},{7,15},{8,0},{9,1},... | collective-permute-start | bytes 1622024 | tf_op jit(solution)/shard_map/ppermute | solution.py:85
  38.3 14.0 %collective-permute-start.15 = (bf16[32,4096]{1,0:T(8,128)(2,1)S(1)}, bf16[32,4096]{1,0:T(8,128)(2,1)S(1)}, u32[]{:S(2)}, u32[]{:S(2)}) collective-permute-start(bf16[32,4096]{1,0:T(8,128)(2,1)S(1)} %get-tuple-element.111), channel_id=1, source_target_pairs={{0,8},{1,9},{2,10},{3,11},{4,12},{5,13},{6,14},{7,15},{8,0},{9,1},... | collective-permute-start | bytes 786440 | tf_op jit(solution)/shard_map/ppermute | solution.py:85
  38.7 5.0 %collective-permute-start.16 = (bf16[32,4096]{1,0:T(8,128)(2,1)S(1)}, bf16[32,4096]{1,0:T(8,128)(2,1)S(1)}, u32[]{:S(2)}, u32[]{:S(2)}) collective-permute-start(bf16[32,4096]{1,0:T(8,128)(2,1)S(1)} %get-tuple-element.113), channel_id=1, source_target_pairs={{0,8},{1,9},{2,10},{3,11},{4,12},{5,13},{6,14},{7,15},{8,0},{9,1},... | collective-permute-start | bytes 786440 | tf_op jit(solution)/shard_map/ppermute | solution.py:85
  40.8 1.7 %collective-permute-start.22 = (bf16[32,4096]{1,0:T(8,128)(2,1)S(1)}, bf16[32,4096]{1,0:T(8,128)(2,1)S(1)}, u32[]{:S(2)}, u32[]{:S(2)}) collective-permute-start(bf16[32,4096]{1,0:T(8,128)(2,1)S(1)} %get-tuple-element.125), channel_id=1, source_target_pairs={{0,8},{1,9},{2,10},{3,11},{4,12},{5,13},{6,14},{7,15},{8,0},{9,1},... | collective-permute-start | bytes 786440 | tf_op jit(solution)/shard_map/ppermute | solution.py:85
  41.9 6.2 %collective-permute-start.21 = (bf16[16,4096]{1,0:T(8,128)(2,1)S(1)}, bf16[16,4096]{1,0:T(8,128)(2,1)S(1)}, u32[]{:S(2)}, u32[]{:S(2)}) collective-permute-start(bf16[16,4096]{1,0:T(8,128)(2,1)S(1)} %get-tuple-element.123), channel_id=1, source_target_pairs={{0,16},{1,17},{2,18},{3,19},{4,20},{5,21},{6,22},{7,23},{8,9},{9,8... | collective-permute-start | bytes 393224 | tf_op jit(solution)/shard_map/ppermute | solution.py:85
  42.5 8.0 %collective-permute-start.24 = (bf16[32,4096]{1,0:T(8,128)(2,1)S(1)}, bf16[32,4096]{1,0:T(8,128)(2,1)S(1)}, u32[]{:S(2)}, u32[]{:S(2)}) collective-permute-start(bf16[32,4096]{1,0:T(8,128)(2,1)S(1)} %get-tuple-element.130), channel_id=1, source_target_pairs={{0,8},{1,9},{2,10},{3,11},{4,12},{5,13},{6,14},{7,15},{8,0},{9,1},... | collective-permute-start | bytes 786440 | tf_op jit(solution)/shard_map/ppermute | solution.py:85
  42.6 7.9 %collective-permute-start.25 = (bf16[32,4096]{1,0:T(8,128)(2,1)S(1)}, bf16[32,4096]{1,0:T(8,128)(2,1)S(1)}, u32[]{:S(2)}, u32[]{:S(2)}) collective-permute-start(bf16[32,4096]{1,0:T(8,128)(2,1)S(1)} %get-tuple-element.131), channel_id=1, source_target_pairs={{0,1},{1,0},{2,3},{3,2},{4,5},{5,4},{6,7},{7,6},{8,24},{9,25},{10,... | collective-permute-start | bytes 786440 | tf_op jit(solution)/shard_map/ppermute | solution.py:85
  48.3 8.4 %collective-permute-start.23 = (bf16[32,4096]{1,0:T(8,128)(2,1)S(1)}, bf16[32,4096]{1,0:T(8,128)(2,1)S(1)}, u32[]{:S(2)}, u32[]{:S(2)}) collective-permute-start(bf16[32,4096]{1,0:T(8,128)(2,1)S(1)} %get-tuple-element.128), channel_id=1, source_target_pairs={{0,1},{1,0},{2,3},{3,2},{4,5},{5,4},{6,7},{7,6},{8,24},{9,25},{10,... | collective-permute-start | bytes 786440 | tf_op jit(solution)/shard_map/ppermute | solution.py:85
  48.8 12.0 %collective-permute-start.27 = (bf16[16,4096]{1,0:T(8,128)(2,1)S(1)}, bf16[16,4096]{1,0:T(8,128)(2,1)S(1)}, u32[]{:S(2)}, u32[]{:S(2)}) collective-permute-start(bf16[16,4096]{1,0:T(8,128)(2,1)S(1)} %get-tuple-element.136), channel_id=1, source_target_pairs={{0,6},{1,7},{2,4},{3,5},{4,2},{5,3},{6,0},{7,1},{8,14},{9,15},{10,... | collective-permute-start | bytes 393224 | tf_op jit(solution)/shard_map/ppermute | solution.py:85
  50.6 6.8 %collective-permute-start.28 = (bf16[16,4096]{1,0:T(8,128)(2,1)S(1)}, bf16[16,4096]{1,0:T(8,128)(2,1)S(1)}, u32[]{:S(2)}, u32[]{:S(2)}) collective-permute-start(bf16[16,4096]{1,0:T(8,128)(2,1)S(1)} %get-tuple-element.138), channel_id=1, source_target_pairs={{0,16},{1,17},{2,18},{3,19},{4,20},{5,21},{6,22},{7,23},{8,9},{9,8... | collective-permute-start | bytes 393224 | tf_op jit(solution)/shard_map/ppermute | solution.py:85
  56.8 6.4 %collective-permute-start.26 = (bf16[16,4096]{1,0:T(8,128)(2,1)S(1)}, bf16[16,4096]{1,0:T(8,128)(2,1)S(1)}, u32[]{:S(2)}, u32[]{:S(2)}) collective-permute-start(bf16[16,4096]{1,0:T(8,128)(2,1)S(1)} %get-tuple-element.135), channel_id=1, source_target_pairs={{0,16},{1,17},{2,18},{3,19},{4,20},{5,21},{6,22},{7,23},{8,9},{9,8... | collective-permute-start | bytes 393224 | tf_op jit(solution)/shard_map/ppermute | solution.py:85
  56.9 6.5 %collective-permute-start.30 = (bf16[32,4096]{1,0:T(8,128)(2,1)S(1)}, bf16[32,4096]{1,0:T(8,128)(2,1)S(1)}, u32[]{:S(2)}, u32[]{:S(2)}) collective-permute-start(bf16[32,4096]{1,0:T(8,128)(2,1)S(1)} %get-tuple-element.144), channel_id=1, source_target_pairs={{0,8},{1,9},{2,10},{3,11},{4,12},{5,13},{6,14},{7,15},{8,0},{9,1},... | collective-permute-start | bytes 786440 | tf_op jit(solution)/shard_map/ppermute | solution.py:85
  56.9 6.4 %collective-permute-start.31 = (bf16[32,4096]{1,0:T(8,128)(2,1)S(1)}, bf16[32,4096]{1,0:T(8,128)(2,1)S(1)}, u32[]{:S(2)}, u32[]{:S(2)}) collective-permute-start(bf16[32,4096]{1,0:T(8,128)(2,1)S(1)} %get-tuple-element.145), channel_id=1, source_target_pairs={{0,1},{1,0},{2,3},{3,2},{4,5},{5,4},{6,7},{7,6},{8,24},{9,25},{10,... | collective-permute-start | bytes 786440 | tf_op jit(solution)/shard_map/ppermute | solution.py:85
  57.4 10.0 %collective-permute-start.29 = (bf16[16,4096]{1,0:T(8,128)(2,1)S(1)}, bf16[16,4096]{1,0:T(8,128)(2,1)S(1)}, u32[]{:S(2)}, u32[]{:S(2)}) collective-permute-start(bf16[16,4096]{1,0:T(8,128)(2,1)S(1)} %get-tuple-element.142), channel_id=1, source_target_pairs={{0,4},{1,5},{2,6},{3,7},{4,0},{5,1},{6,2},{7,3},{8,12},{9,13},{10,... | collective-permute-start | bytes 393224 | tf_op jit(solution)/shard_map/ppermute | solution.py:85
  63.3 5.6 %collective-permute-start.32 = (bf16[16,4096]{1,0:T(8,128)(2,1)S(1)}, bf16[16,4096]{1,0:T(8,128)(2,1)S(1)}, u32[]{:S(2)}, u32[]{:S(2)}) collective-permute-start(bf16[16,4096]{1,0:T(8,128)(2,1)S(1)} %get-tuple-element.149), channel_id=1, source_target_pairs={{0,2},{1,3},{2,0},{3,1},{4,6},{5,7},{6,4},{7,5},{8,10},{9,11},{10,... | collective-permute-start | bytes 393224 | tf_op jit(solution)/shard_map/ppermute | solution.py:85
  63.5 5.4 %collective-permute-start.33 = (bf16[16,4096]{1,0:T(8,128)(2,1)S(1)}, bf16[16,4096]{1,0:T(8,128)(2,1)S(1)}, u32[]{:S(2)}, u32[]{:S(2)}) collective-permute-start(bf16[16,4096]{1,0:T(8,128)(2,1)S(1)} %get-tuple-element.153), channel_id=1, source_target_pairs={{0,16},{1,17},{2,18},{3,19},{4,20},{5,21},{6,22},{7,23},{8,9},{9,8... | collective-permute-start | bytes 393224 | tf_op jit(solution)/shard_map/ppermute | solution.py:85

commit v6 on v5

--- a/solution.py
+++ b/solution.py
@@ -51,8 +51,9 @@
     "mine2 core3*",
     "expert1",
     "expert2",
-    "core0 far3*",
+    "far3*",
     "core2*",
+    "core0*",
     "core1 near3*",
     "far2*",
     "far1*",

time: 69.7 us -> 69.4 us (level)
    pallas_call x27 -> x28, Pallas kernels: 15.6 us -> 15.6 us  [__call__(): pl.pallas_call(marked, name=name, out_shape=[pltpu.VMEM(shape, dtype) for...]
where the time goes in v6:
time: 69.4 us; the launch traced here: 69.2 us
  starting transfers between devices  29 us (42%)
  waiting for transfers between devices  23.7 us (34%)
  Pallas kernels  15.6 us (22%)
    ppermute x34, starting transfers between devices, moved(): return lax.ppermute(value, MESH_AXES, pairs)  29 us
    ppermute x34, waiting for transfers between devices, moved(): return lax.ppermute(value, MESH_AXES, pairs)  23.7 us
    pallas_call x28, Pallas kernels, __call__(): pl.pallas_call(marked, name=name, out_shape=[pltpu.VMEM(shape, dtype) for...  15.6 us
  transfers between devices with their start and end apart: 34, of which 11 were waited for; matrix products, arithmetic and copies ran while one was open for 0% of the time, Pallas kernels for 21%

profile of v6, /device:TPU:0, one launch (start us, length us, event | category | flops | bytes accessed | tf_op | source)
XLA Modules:
  0.0 69.2 jit_solution(2892165666142098435)
XLA Ops:
  0.0 1.2 %label.1 = (bf16[16,4224]{1,0:T(8,128)(2,1)S(1)}, f32[8,128]{1,0:T(8,128)S(1)}) custom-call(bf16[16,4096]{1,0:T(8,128)(2,1)} %refs_0_.1, s32[8,16]{1,0:T(8,128)} %bitcast.7, f32[8,16]{1,0:T(8,128)} %bitcast.8, s32[16]{0:T(128)} %refs_3_.1, s32[16]{0:T(128)} %refs_4_.1), custom_call_target="tpu_custom_call" | custom-call | tf_op jit(solution)/shard_map/label/pallas_call | solution.py:121
  1.2 5.1 %collective-permute-start.1 = (bf16[16,4224]{1,0:T(8,128)(2,1)S(1)}, bf16[16,4224]{1,0:T(8,128)(2,1)S(1)}, u32[]{:S(2)}, u32[]{:S(2)}) collective-permute-start(bf16[16,4224]{1,0:T(8,128)(2,1)S(1)} %get-tuple-element.81.refs_0_), channel_id=1, source_target_pairs={{0,6},{1,7},{2,4},{3,5},{4,2},{5,3},{6,0},{7,1},{8,14},{9,15},{10,... | collective-permute-start | bytes 405512 | tf_op jit(solution)/shard_map/ppermute | solution.py:86
  6.3 1.5 %collective-permute-start.2 = (bf16[16,4224]{1,0:T(8,128)(2,1)S(1)}, bf16[16,4224]{1,0:T(8,128)(2,1)S(1)}, u32[]{:S(2)}, u32[]{:S(2)}) collective-permute-start(bf16[16,4224]{1,0:T(8,128)(2,1)S(1)} %get-tuple-element.81.refs_0_), channel_id=1, source_target_pairs={{0,16},{1,17},{2,18},{3,19},{4,20},{5,21},{6,22},{7,23},{8,9},{9,8... | collective-permute-start | bytes 405512 | tf_op jit(solution)/shard_map/ppermute | solution.py:86
  7.8 1.9 %stage.3 = (bf16[4096,384]{1,0:T(8,128)(2,1)S(1)}, f32[8,128]{1,0:T(8,128)S(1)}) custom-call(bf16[4096,384]{1,0:T(8,128)(2,1)} %bitcast.9, f32[8,128]{1,0:T(8,128)S(1)} %get-tuple-element.82.refs_1_), custom_call_target="tpu_custom_call" | custom-call | flops 10000000000 | tf_op jit(solution)/shard_map/stage/pallas_call | solution.py:121
  9.7 1.6 %collective-permute-done.2.refs_1_ = bf16[16,4224]{1,0:T(8,128)(2,1)S(1)} collective-permute-done((bf16[16,4224]{1,0:T(8,128)(2,1)S(1)}, bf16[16,4224]{1,0:T(8,128)(2,1)S(1)}, u32[]{:S(2)}, u32[]{:S(2)}) %collective-permute-start.2) | collective-permute-done | bytes 135200 | tf_op jit(solution)/shard_map/ppermute | solution.py:86
  11.4 1.6 %collective-permute-start.4 = (bf16[32,4224]{1,0:T(8,128)(2,1)S(1)}, bf16[32,4224]{1,0:T(8,128)(2,1)S(1)}, u32[]{:S(2)}, u32[]{:S(2)}) collective-permute-start(bf16[32,4224]{1,0:T(8,128)(2,1)S(1)} %get-tuple-element.86.refs_3_), channel_id=1, source_target_pairs={{0,1},{1,0},{2,3},{3,2},{4,5},{5,4},{6,7},{7,6},{8,24},{9,25},{10,... | collective-permute-start | bytes 811016 | tf_op jit(solution)/shard_map/ppermute | solution.py:86
  13.0 1.6 %collective-permute-start.3 = (bf16[16,4224]{1,0:T(8,128)(2,1)S(1)}, bf16[16,4224]{1,0:T(8,128)(2,1)S(1)}, u32[]{:S(2)}, u32[]{:S(2)}) collective-permute-start(bf16[16,4224]{1,0:T(8,128)(2,1)S(1)} %get-tuple-element.85.refs_1_), channel_id=1, source_target_pairs={{0,16},{1,17},{2,18},{3,19},{4,20},{5,21},{6,22},{7,23},{8,9},{9,8... | collective-permute-start | bytes 405512 | tf_op jit(solution)/shard_map/ppermute | solution.py:86
  14.5 0.6 collective-permute-start.6
  15.1 1.9 %stage.4 = (bf16[384,4096]{1,0:T(8,128)(2,1)S(1)}, f32[8,128]{1,0:T(8,128)S(1)}) custom-call(bf16[384,4096]{1,0:T(8,128)(2,1)} %bitcast.5, f32[8,128]{1,0:T(8,128)S(1)} %get-tuple-element.89.refs_1_), custom_call_target="tpu_custom_call" | custom-call | tf_op jit(solution)/shard_map/stage/pallas_call | solution.py:121
  17.0 1.9 %stage.5 = (bf16[4096,384]{1,0:T(8,128)(2,1)S(1)}, f32[8,128]{1,0:T(8,128)S(1)}) custom-call(bf16[4096,384]{1,0:T(8,128)(2,1)} %bitcast.6, f32[8,128]{1,0:T(8,128)S(1)} %get-tuple-element.90.refs_1_), custom_call_target="tpu_custom_call" | custom-call | tf_op jit(solution)/shard_map/stage/pallas_call | solution.py:121
  18.9 1.7 %collective-permute-done.refs_0_ = bf16[16,4224]{1,0:T(8,128)(2,1)S(1)} collective-permute-done((bf16[16,4224]{1,0:T(8,128)(2,1)S(1)}, bf16[16,4224]{1,0:T(8,128)(2,1)S(1)}, u32[]{:S(2)}, u32[]{:S(2)}) %collective-permute-start) | collective-permute-done | bytes 135200 | tf_op jit(solution)/shard_map/ppermute | solution.py:86
  20.8 0.8 %collective-permute-start.8 = (bf16[32,4224]{1,0:T(8,128)(2,1)S(1)}, bf16[32,4224]{1,0:T(8,128)(2,1)S(1)}, u32[]{:S(2)}, u32[]{:S(2)}) collective-permute-start(bf16[32,4224]{1,0:T(8,128)(2,1)S(1)} %get-tuple-element.93.refs_0_), channel_id=1, source_target_pairs={{0,1},{1,0},{2,3},{3,2},{4,5},{5,4},{6,7},{7,6},{8,24},{9,25},{10,... | collective-permute-start | bytes 811016 | tf_op jit(solution)/shard_map/ppermute | solution.py:86
  21.6 1.0 %collective-permute-start.9 = (bf16[16,4224]{1,0:T(8,128)(2,1)S(1)}, bf16[16,4224]{1,0:T(8,128)(2,1)S(1)}, u32[]{:S(2)}, u32[]{:S(2)}) collective-permute-start(bf16[16,4224]{1,0:T(8,128)(2,1)S(1)} %get-tuple-element.94.refs_0_), channel_id=1, source_target_pairs={{0,16},{1,17},{2,18},{3,19},{4,20},{5,21},{6,22},{7,23},{8,9},{9,8... | collective-permute-start | bytes 405512 | tf_op jit(solution)/shard_map/ppermute | solution.py:86
  22.5 0.9 %collective-permute-start.7 = (bf16[32,4224]{1,0:T(8,128)(2,1)S(1)}, bf16[32,4224]{1,0:T(8,128)(2,1)S(1)}, u32[]{:S(2)}, u32[]{:S(2)}) collective-permute-start(bf16[32,4224]{1,0:T(8,128)(2,1)S(1)} %get-tuple-element.92.refs_0_), channel_id=1, source_target_pairs={{0,1},{1,0},{2,3},{3,2},{4,5},{5,4},{6,7},{7,6},{8,24},{9,25},{10,... | collective-permute-start | bytes 811016 | tf_op jit(solution)/shard_map/ppermute | solution.py:86
  23.4 4.6 %collective-permute-done.9.refs_1_ = bf16[16,4224]{1,0:T(8,128)(2,1)S(1)} collective-permute-done((bf16[16,4224]{1,0:T(8,128)(2,1)S(1)}, bf16[16,4224]{1,0:T(8,128)(2,1)S(1)}, u32[]{:S(2)}, u32[]{:S(2)}) %collective-permute-start.9) | collective-permute-done | bytes 135200 | tf_op jit(solution)/shard_map/ppermute | solution.py:86
  28.1 1.4 %collective-permute-start.13 = (bf16[32,4224]{1,0:T(8,128)(2,1)S(1)}, bf16[32,4224]{1,0:T(8,128)(2,1)S(1)}, u32[]{:S(2)}, u32[]{:S(2)}) collective-permute-start(bf16[32,4224]{1,0:T(8,128)(2,1)S(1)} %get-tuple-element.106.refs_0_), channel_id=1, source_target_pairs={{0,1},{1,0},{2,3},{3,2},{4,5},{5,4},{6,7},{7,6},{8,24},{9,25},{10,... | collective-permute-start | bytes 811016 | tf_op jit(solution)/shard_map/ppermute | solution.py:86
  29.6 1.9 %expert.4 = (bf16[32,4096]{1,0:T(8,128)(2,1)S(1)}, bf16[32,4096]{1,0:T(8,128)(2,1)S(1)}, bf16[32,4096]{1,0:T(8,128)(2,1)S(1)}, bf16[32,4096]{1,0:T(8,128)(2,1)S(1)}, f32[8,128]{1,0:T(8,128)S(1)}) custom-call(bf16[64,4224]{1,0:T(8,128)(2,1)S(1)} %get-tuple-element.101.refs_0_, bf16[64,4224]{1,0:T(8,128)(2,1)S(1)} %collective-permute-done.11.refs_1_, ...), custom_call_target="tpu_custom_call" | custom-call | flops 24159191040 | tf_op jit(solution)/shard_map/expert/pallas_call | solution.py:121
  31.6 1.9 %expert.5 = (bf16[32,4096]{1,0:T(8,128)(2,1)S(1)}, bf16[32,4096]{1,0:T(8,128)(2,1)S(1)}, bf16[32,4096]{1,0:T(8,128)(2,1)S(1)}, bf16[32,4096]{1,0:T(8,128)(2,1)S(1)}, f32[8,128]{1,0:T(8,128)S(1)}) custom-call(bf16[64,4224]{1,0:T(8,128)(2,1)S(1)} %get-tuple-element.97.refs_0_, bf16[64,4224]{1,0:T(8,128)(2,1)S(1)} %collective-permute-done.10.refs_1_, ...), custom_call_target="tpu_custom_call" | custom-call | flops 24159191040 | tf_op jit(solution)/shard_map/expert/pallas_call | solution.py:121
  33.5 0.6 collective-permute-start.14
  34.2 0.5 collective-permute-start.12
  34.8 0.5 collective-permute-done.14.refs_3_
  35.2 0.1 sums.27
  35.3 0.8 %collective-permute-start.18 = (bf16[32,4096]{1,0:T(8,128)(2,1)S(1)}, bf16[32,4096]{1,0:T(8,128)(2,1)S(1)}, u32[]{:S(2)}, u32[]{:S(2)}) collective-permute-start(bf16[32,4096]{1,0:T(8,128)(2,1)S(1)} %get-tuple-element.117), channel_id=1, source_target_pairs={{0,1},{1,0},{2,3},{3,2},{4,5},{5,4},{6,7},{7,6},{8,24},{9,25},{10,... | collective-permute-start | bytes 786440 | tf_op jit(solution)/shard_map/ppermute | solution.py:86
  36.1 0.2 collective-permute-done.12.refs_1_
  36.4 1.9 %expert.6 = (bf16[32,4096]{1,0:T(8,128)(2,1)S(1)}, bf16[32,4096]{1,0:T(8,128)(2,1)S(1)}, bf16[32,4096]{1,0:T(8,128)(2,1)S(1)}, bf16[32,4096]{1,0:T(8,128)(2,1)S(1)}, f32[8,128]{1,0:T(8,128)S(1)}) custom-call(bf16[64,4224]{1,0:T(8,128)(2,1)S(1)} %get-tuple-element.105.refs_0_, bf16[64,4224]{1,0:T(8,128)(2,1)S(1)} %collective-permute-done.12.refs_1_, ...), custom_call_target="tpu_custom_call" | custom-call | flops 24159191040 | tf_op jit(solution)/shard_map/expert/pallas_call | solution.py:121
  38.3 0.4 collective-permute-start.15
  38.7 0.1 collective-permute-start.16
  38.9 1.9 %expert.7 = (bf16[32,4096]{1,0:T(8,128)(2,1)S(1)}, bf16[32,4096]{1,0:T(8,128)(2,1)S(1)}, bf16[32,4096]{1,0:T(8,128)(2,1)S(1)}, bf16[32,4096]{1,0:T(8,128)(2,1)S(1)}, f32[8,128]{1,0:T(8,128)S(1)}) custom-call(bf16[64,4224]{1,0:T(8,128)(2,1)S(1)} %get-tuple-element.118.refs_0_, bf16[64,4224]{1,0:T(8,128)(2,1)S(1)} %collective-permute-done.19.refs_1_, ...), custom_call_target="tpu_custom_call" | custom-call | flops 24159191040 | tf_op jit(solution)/shard_map/expert/pallas_call | solution.py:121
  40.8 0.4 collective-permute-start.22
  41.3 0.5 collective-permute-done.18.refs_2_
  41.9 0.6 collective-permute-start.20
  42.5 0.3 collective-permute-start.24
  42.9 1.3 %collective-permute-start.25 = (bf16[32,4096]{1,0:T(8,128)(2,1)S(1)}, bf16[32,4096]{1,0:T(8,128)(2,1)S(1)}, u32[]{:S(2)}, u32[]{:S(2)}) collective-permute-start(bf16[32,4096]{1,0:T(8,128)(2,1)S(1)} %get-tuple-element.133), channel_id=1, source_target_pairs={{0,1},{1,0},{2,3},{3,2},{4,5},{5,4},{6,7},{7,6},{8,24},{9,25},{10,... | collective-permute-start | bytes 786440 | tf_op jit(solution)/shard_map/ppermute | solution.py:86
  44.2 3.9 %collective-permute-done.20.refs_3_ = bf16[16,4096]{1,0:T(8,128)(2,1)S(1)} collective-permute-done((bf16[16,4096]{1,0:T(8,128)(2,1)S(1)}, bf16[16,4096]{1,0:T(8,128)(2,1)S(1)}, u32[]{:S(2)}, u32[]{:S(2)}) %collective-permute-start.20) | collective-permute-done | bytes 131104 | tf_op jit(solution)/shard_map/ppermute | solution.py:86
  48.2 0.5 collective-permute-start.23
  48.6 1.8 %collective-permute-start.27 = (bf16[16,4096]{1,0:T(8,128)(2,1)S(1)}, bf16[16,4096]{1,0:T(8,128)(2,1)S(1)}, u32[]{:S(2)}, u32[]{:S(2)}) collective-permute-start(bf16[16,4096]{1,0:T(8,128)(2,1)S(1)} %get-tuple-element.138), channel_id=1, source_target_pairs={{0,6},{1,7},{2,4},{3,5},{4,2},{5,3},{6,0},{7,1},{8,14},{9,15},{10,... | collective-permute-start | bytes 393224 | tf_op jit(solution)/shard_map/ppermute | solution.py:86
  50.4 0.1 sums.32
  50.5 1.6 %collective-permute-start.28 = (bf16[16,4096]{1,0:T(8,128)(2,1)S(1)}, bf16[16,4096]{1,0:T(8,128)(2,1)S(1)}, u32[]{:S(2)}, u32[]{:S(2)}) collective-permute-start(bf16[16,4096]{1,0:T(8,128)(2,1)S(1)} %get-tuple-element.140), channel_id=1, source_target_pairs={{0,16},{1,17},{2,18},{3,19},{4,20},{5,21},{6,22},{7,23},{8,9},{9,8... | collective-permute-start | bytes 393224 | tf_op jit(solution)/shard_map/ppermute | solution.py:86
  52.1 4.5 %collective-permute-done.23.refs_2_ = bf16[32,4096]{1,0:T(8,128)(2,1)S(1)} collective-permute-done((bf16[32,4096]{1,0:T(8,128)(2,1)S(1)}, bf16[32,4096]{1,0:T(8,128)(2,1)S(1)}, u32[]{:S(2)}, u32[]{:S(2)}) %collective-permute-start.23) | collective-permute-done | bytes 262176 | tf_op jit(solution)/shard_map/ppermute | solution.py:86
  56.6 0.1 sums.33
  56.8 0.4 collective-permute-start.31
  57.3 2.9 %collective-permute-start.29 = (bf16[16,4096]{1,0:T(8,128)(2,1)S(1)}, bf16[16,4096]{1,0:T(8,128)(2,1)S(1)}, u32[]{:S(2)}, u32[]{:S(2)}) collective-permute-start(bf16[16,4096]{1,0:T(8,128)(2,1)S(1)} %get-tuple-element.144), channel_id=1, source_target_pairs={{0,4},{1,5},{2,6},{3,7},{4,0},{5,1},{6,2},{7,3},{8,12},{9,13},{10,... | collective-permute-start | bytes 393224 | tf_op jit(solution)/shard_map/ppermute | solution.py:86
  60.2 2.9 %collective-permute-done.26.refs_1_ = bf16[16,4096]{1,0:T(8,128)(2,1)S(1)} collective-permute-done((bf16[16,4096]{1,0:T(8,128)(2,1)S(1)}, bf16[16,4096]{1,0:T(8,128)(2,1)S(1)}, u32[]{:S(2)}, u32[]{:S(2)}) %collective-permute-start.26) | collective-permute-done | bytes 131104 | tf_op jit(solution)/shard_map/ppermute | solution.py:86
  63.3 0.1 sums.36
  63.4 1.9 %collective-permute-start.33 = (bf16[16,4096]{1,0:T(8,128)(2,1)S(1)}, bf16[16,4096]{1,0:T(8,128)(2,1)S(1)}, u32[]{:S(2)}, u32[]{:S(2)}) collective-permute-start(bf16[16,4096]{1,0:T(8,128)(2,1)S(1)} %get-tuple-element.155), channel_id=1, source_target_pairs={{0,16},{1,17},{2,18},{3,19},{4,20},{5,21},{6,22},{7,23},{8,9},{9,8... | collective-permute-start | bytes 393224 | tf_op jit(solution)/shard_map/ppermute | solution.py:86
  65.3 1.7 %collective-permute-done.29.refs_1_ = bf16[16,4096]{1,0:T(8,128)(2,1)S(1)} collective-permute-done((bf16[16,4096]{1,0:T(8,128)(2,1)S(1)}, bf16[16,4096]{1,0:T(8,128)(2,1)S(1)}, u32[]{:S(2)}, u32[]{:S(2)}) %collective-permute-start.29) | collective-permute-done | bytes 131104 | tf_op jit(solution)/shard_map/ppermute | solution.py:86
  67.1 1.4 %collective-permute-done.32.refs_1_ = bf16[16,4096]{1,0:T(8,128)(2,1)S(1)} collective-permute-done((bf16[16,4096]{1,0:T(8,128)(2,1)S(1)}, bf16[16,4096]{1,0:T(8,128)(2,1)S(1)}, u32[]{:S(2)}, u32[]{:S(2)}) %collective-permute-start.32) | collective-permute-done | bytes 131104 | tf_op jit(solution)/shard_map/ppermute | solution.py:86
  68.6 0.7 copy.9
  (49 shorter events, 1.3 us)
Async XLA Ops:
  1.2 11.7 %collective-permute-start.1 = (bf16[16,4224]{1,0:T(8,128)(2,1)S(1)}, bf16[16,4224]{1,0:T(8,128)(2,1)S(1)}, u32[]{:S(2)}, u32[]{:S(2)}) collective-permute-start(bf16[16,4224]{1,0:T(8,128)(2,1)S(1)} %get-tuple-element.81.refs_0_), channel_id=1, source_target_pairs={{0,6},{1,7},{2,4},{3,5},{4,2},{5,3},{6,0},{7,1},{8,14},{9,15},{10,... | collective-permute-start | bytes 405512 | tf_op jit(solution)/shard_map/ppermute | solution.py:86
  6.3 5.0 %collective-permute-start.2 = (bf16[16,4224]{1,0:T(8,128)(2,1)S(1)}, bf16[16,4224]{1,0:T(8,128)(2,1)S(1)}, u32[]{:S(2)}, u32[]{:S(2)}) collective-permute-start(bf16[16,4224]{1,0:T(8,128)(2,1)S(1)} %get-tuple-element.81.refs_0_), channel_id=1, source_target_pairs={{0,16},{1,17},{2,18},{3,19},{4,20},{5,21},{6,22},{7,23},{8,9},{9,8... | collective-permute-start | bytes 405512 | tf_op jit(solution)/shard_map/ppermute | solution.py:86
  7.8 6.7 %collective-permute-start.5 = (bf16[16,4224]{1,0:T(8,128)(2,1)S(1)}, bf16[16,4224]{1,0:T(8,128)(2,1)S(1)}, u32[]{:S(2)}, u32[]{:S(2)}) collective-permute-start(bf16[16,4224]{1,0:T(8,128)(2,1)S(1)} %get-tuple-element.81.refs_0_), channel_id=1, source_target_pairs={{0,2},{1,3},{2,0},{3,1},{4,6},{5,7},{6,4},{7,5},{8,10},{9,11},{10,... | collective-permute-start | bytes 405512 | tf_op jit(solution)/shard_map/ppermute | solution.py:86
  11.4 9.3 %collective-permute-start.4 = (bf16[32,4224]{1,0:T(8,128)(2,1)S(1)}, bf16[32,4224]{1,0:T(8,128)(2,1)S(1)}, u32[]{:S(2)}, u32[]{:S(2)}) collective-permute-start(bf16[32,4224]{1,0:T(8,128)(2,1)S(1)} %get-tuple-element.86.refs_3_), channel_id=1, source_target_pairs={{0,1},{1,0},{2,3},{3,2},{4,5},{5,4},{6,7},{7,6},{8,24},{9,25},{10,... | collective-permute-start | bytes 811016 | tf_op jit(solution)/shard_map/ppermute | solution.py:86
  12.9 7.7 %collective-permute-start = (bf16[16,4224]{1,0:T(8,128)(2,1)S(1)}, bf16[16,4224]{1,0:T(8,128)(2,1)S(1)}, u32[]{:S(2)}, u32[]{:S(2)}) collective-permute-start(bf16[16,4224]{1,0:T(8,128)(2,1)S(1)} %get-tuple-element.81.refs_0_), channel_id=1, source_target_pairs={{0,4},{1,5},{2,6},{3,7},{4,0},{5,1},{6,2},{7,3},{8,12},{9,13},{10,... | collective-permute-start | bytes 405512 | tf_op jit(solution)/shard_map/ppermute | solution.py:86
  13.0 7.7 %collective-permute-start.3 = (bf16[16,4224]{1,0:T(8,128)(2,1)S(1)}, bf16[16,4224]{1,0:T(8,128)(2,1)S(1)}, u32[]{:S(2)}, u32[]{:S(2)}) collective-permute-start(bf16[16,4224]{1,0:T(8,128)(2,1)S(1)} %get-tuple-element.85.refs_1_), channel_id=1, source_target_pairs={{0,16},{1,17},{2,18},{3,19},{4,20},{5,21},{6,22},{7,23},{8,9},{9,8... | collective-permute-start | bytes 405512 | tf_op jit(solution)/shard_map/ppermute | solution.py:86
  14.5 6.1 %collective-permute-start.6 = (bf16[16,4224]{1,0:T(8,128)(2,1)S(1)}, bf16[16,4224]{1,0:T(8,128)(2,1)S(1)}, u32[]{:S(2)}, u32[]{:S(2)}) collective-permute-start(bf16[16,4224]{1,0:T(8,128)(2,1)S(1)} %get-tuple-element.88.refs_5_), channel_id=1, source_target_pairs={{0,16},{1,17},{2,18},{3,19},{4,20},{5,21},{6,22},{7,23},{8,9},{9,8... | collective-permute-start | bytes 405512 | tf_op jit(solution)/shard_map/ppermute | solution.py:86
  20.7 8.9 %collective-permute-start.11 = (bf16[64,4224]{1,0:T(8,128)(2,1)S(1)}, bf16[64,4224]{1,0:T(8,128)(2,1)S(1)}, u32[]{:S(2)}, u32[]{:S(2)}) collective-permute-start(bf16[64,4224]{1,0:T(8,128)(2,1)S(1)} %get-tuple-element.101.refs_0_), channel_id=1, source_target_pairs={{0,8},{1,9},{2,10},{3,11},{4,12},{5,13},{6,14},{7,15},{8,0},{9,1},... | collective-permute-start | bytes 1622024 | tf_op jit(solution)/shard_map/ppermute | solution.py:86
  20.8 8.7 %collective-permute-start.8 = (bf16[32,4224]{1,0:T(8,128)(2,1)S(1)}, bf16[32,4224]{1,0:T(8,128)(2,1)S(1)}, u32[]{:S(2)}, u32[]{:S(2)}) collective-permute-start(bf16[32,4224]{1,0:T(8,128)(2,1)S(1)} %get-tuple-element.93.refs_0_), channel_id=1, source_target_pairs={{0,1},{1,0},{2,3},{3,2},{4,5},{5,4},{6,7},{7,6},{8,24},{9,25},{10,... | collective-permute-start | bytes 811016 | tf_op jit(solution)/shard_map/ppermute | solution.py:86
  21.6 6.5 %collective-permute-start.9 = (bf16[16,4224]{1,0:T(8,128)(2,1)S(1)}, bf16[16,4224]{1,0:T(8,128)(2,1)S(1)}, u32[]{:S(2)}, u32[]{:S(2)}) collective-permute-start(bf16[16,4224]{1,0:T(8,128)(2,1)S(1)} %get-tuple-element.94.refs_0_), channel_id=1, source_target_pairs={{0,16},{1,17},{2,18},{3,19},{4,20},{5,21},{6,22},{7,23},{8,9},{9,8... | collective-permute-start | bytes 405512 | tf_op jit(solution)/shard_map/ppermute | solution.py:86
  22.5 11.6 %collective-permute-start.7 = (bf16[32,4224]{1,0:T(8,128)(2,1)S(1)}, bf16[32,4224]{1,0:T(8,128)(2,1)S(1)}, u32[]{:S(2)}, u32[]{:S(2)}) collective-permute-start(bf16[32,4224]{1,0:T(8,128)(2,1)S(1)} %get-tuple-element.92.refs_0_), channel_id=1, source_target_pairs={{0,1},{1,0},{2,3},{3,2},{4,5},{5,4},{6,7},{7,6},{8,24},{9,25},{10,... | collective-permute-start | bytes 811016 | tf_op jit(solution)/shard_map/ppermute | solution.py:86
  28.1 6.7 %collective-permute-start.13 = (bf16[32,4224]{1,0:T(8,128)(2,1)S(1)}, bf16[32,4224]{1,0:T(8,128)(2,1)S(1)}, u32[]{:S(2)}, u32[]{:S(2)}) collective-permute-start(bf16[32,4224]{1,0:T(8,128)(2,1)S(1)} %get-tuple-element.106.refs_0_), channel_id=1, source_target_pairs={{0,1},{1,0},{2,3},{3,2},{4,5},{5,4},{6,7},{7,6},{8,24},{9,25},{10,... | collective-permute-start | bytes 811016 | tf_op jit(solution)/shard_map/ppermute | solution.py:86
  29.6 2.0 %collective-permute-start.10 = (bf16[64,4224]{1,0:T(8,128)(2,1)S(1)}, bf16[64,4224]{1,0:T(8,128)(2,1)S(1)}, u32[]{:S(2)}, u32[]{:S(2)}) collective-permute-start(bf16[64,4224]{1,0:T(8,128)(2,1)S(1)} %get-tuple-element.97.refs_0_), channel_id=1, source_target_pairs={{0,8},{1,9},{2,10},{3,11},{4,12},{5,13},{6,14},{7,15},{8,0},{9,1},... | collective-permute-start | bytes 1622024 | tf_op jit(solution)/shard_map/ppermute | solution.py:86
  33.5 1.7 %collective-permute-start.14 = (bf16[32,4096]{1,0:T(8,128)(2,1)S(1)}, bf16[32,4096]{1,0:T(8,128)(2,1)S(1)}, u32[]{:S(2)}, u32[]{:S(2)}) collective-permute-start(bf16[32,4096]{1,0:T(8,128)(2,1)S(1)} %get-tuple-element.108), channel_id=1, source_target_pairs={{0,8},{1,9},{2,10},{3,11},{4,12},{5,13},{6,14},{7,15},{8,0},{9,1},... | collective-permute-start | bytes 786440 | tf_op jit(solution)/shard_map/ppermute | solution.py:86
  34.1 8.8 %collective-permute-start.21 = (bf16[32,4096]{1,0:T(8,128)(2,1)S(1)}, bf16[32,4096]{1,0:T(8,128)(2,1)S(1)}, u32[]{:S(2)}, u32[]{:S(2)}) collective-permute-start(bf16[32,4096]{1,0:T(8,128)(2,1)S(1)} %get-tuple-element.124), channel_id=1, source_target_pairs={{0,8},{1,9},{2,10},{3,11},{4,12},{5,13},{6,14},{7,15},{8,0},{9,1},... | collective-permute-start | bytes 786440 | tf_op jit(solution)/shard_map/ppermute | solution.py:86
  34.2 2.2 %collective-permute-start.12 = (bf16[64,4224]{1,0:T(8,128)(2,1)S(1)}, bf16[64,4224]{1,0:T(8,128)(2,1)S(1)}, u32[]{:S(2)}, u32[]{:S(2)}) collective-permute-start(bf16[64,4224]{1,0:T(8,128)(2,1)S(1)} %get-tuple-element.105.refs_0_), channel_id=1, source_target_pairs={{0,8},{1,9},{2,10},{3,11},{4,12},{5,13},{6,14},{7,15},{8,0},{9,1},... | collective-permute-start | bytes 1622024 | tf_op jit(solution)/shard_map/ppermute | solution.py:86
  34.7 6.1 %collective-permute-start.17 = (bf16[32,4096]{1,0:T(8,128)(2,1)S(1)}, bf16[32,4096]{1,0:T(8,128)(2,1)S(1)}, u32[]{:S(2)}, u32[]{:S(2)}) collective-permute-start(bf16[32,4096]{1,0:T(8,128)(2,1)S(1)} %get-tuple-element.116), channel_id=1, source_target_pairs={{0,8},{1,9},{2,10},{3,11},{4,12},{5,13},{6,14},{7,15},{8,0},{9,1},... | collective-permute-start | bytes 786440 | tf_op jit(solution)/shard_map/ppermute | solution.py:86
  35.3 6.4 %collective-permute-start.18 = (bf16[32,4096]{1,0:T(8,128)(2,1)S(1)}, bf16[32,4096]{1,0:T(8,128)(2,1)S(1)}, u32[]{:S(2)}, u32[]{:S(2)}) collective-permute-start(bf16[32,4096]{1,0:T(8,128)(2,1)S(1)} %get-tuple-element.117), channel_id=1, source_target_pairs={{0,1},{1,0},{2,3},{3,2},{4,5},{5,4},{6,7},{7,6},{8,24},{9,25},{10,... | collective-permute-start | bytes 786440 | tf_op jit(solution)/shard_map/ppermute | solution.py:86
  36.1 2.6 %collective-permute-start.19 = (bf16[64,4224]{1,0:T(8,128)(2,1)S(1)}, bf16[64,4224]{1,0:T(8,128)(2,1)S(1)}, u32[]{:S(2)}, u32[]{:S(2)}) collective-permute-start(bf16[64,4224]{1,0:T(8,128)(2,1)S(1)} %get-tuple-element.118.refs_0_), channel_id=1, source_target_pairs={{0,8},{1,9},{2,10},{3,11},{4,12},{5,13},{6,14},{7,15},{8,0},{9,1},... | collective-permute-start | bytes 1622024 | tf_op jit(solution)/shard_map/ppermute | solution.py:86
  38.3 13.8 %collective-permute-start.15 = (bf16[32,4096]{1,0:T(8,128)(2,1)S(1)}, bf16[32,4096]{1,0:T(8,128)(2,1)S(1)}, u32[]{:S(2)}, u32[]{:S(2)}) collective-permute-start(bf16[32,4096]{1,0:T(8,128)(2,1)S(1)} %get-tuple-element.112), channel_id=1, source_target_pairs={{0,8},{1,9},{2,10},{3,11},{4,12},{5,13},{6,14},{7,15},{8,0},{9,1},... | collective-permute-start | bytes 786440 | tf_op jit(solution)/shard_map/ppermute | solution.py:86
  38.7 5.5 %collective-permute-start.16 = (bf16[32,4096]{1,0:T(8,128)(2,1)S(1)}, bf16[32,4096]{1,0:T(8,128)(2,1)S(1)}, u32[]{:S(2)}, u32[]{:S(2)}) collective-permute-start(bf16[32,4096]{1,0:T(8,128)(2,1)S(1)} %get-tuple-element.114), channel_id=1, source_target_pairs={{0,8},{1,9},{2,10},{3,11},{4,12},{5,13},{6,14},{7,15},{8,0},{9,1},... | collective-permute-start | bytes 786440 | tf_op jit(solution)/shard_map/ppermute | solution.py:86
  40.8 1.6 %collective-permute-start.22 = (bf16[32,4096]{1,0:T(8,128)(2,1)S(1)}, bf16[32,4096]{1,0:T(8,128)(2,1)S(1)}, u32[]{:S(2)}, u32[]{:S(2)}) collective-permute-start(bf16[32,4096]{1,0:T(8,128)(2,1)S(1)} %get-tuple-element.126), channel_id=1, source_target_pairs={{0,8},{1,9},{2,10},{3,11},{4,12},{5,13},{6,14},{7,15},{8,0},{9,1},... | collective-permute-start | bytes 786440 | tf_op jit(solution)/shard_map/ppermute | solution.py:86
  41.9 6.2 %collective-permute-start.20 = (bf16[16,4096]{1,0:T(8,128)(2,1)S(1)}, bf16[16,4096]{1,0:T(8,128)(2,1)S(1)}, u32[]{:S(2)}, u32[]{:S(2)}) collective-permute-start(bf16[16,4096]{1,0:T(8,128)(2,1)S(1)} %get-tuple-element.122), channel_id=1, source_target_pairs={{0,16},{1,17},{2,18},{3,19},{4,20},{5,21},{6,22},{7,23},{8,9},{9,8... | collective-permute-start | bytes 393224 | tf_op jit(solution)/shard_map/ppermute | solution.py:86
  42.5 7.9 %collective-permute-start.24 = (bf16[32,4096]{1,0:T(8,128)(2,1)S(1)}, bf16[32,4096]{1,0:T(8,128)(2,1)S(1)}, u32[]{:S(2)}, u32[]{:S(2)}) collective-permute-start(bf16[32,4096]{1,0:T(8,128)(2,1)S(1)} %get-tuple-element.132), channel_id=1, source_target_pairs={{0,8},{1,9},{2,10},{3,11},{4,12},{5,13},{6,14},{7,15},{8,0},{9,1},... | collective-permute-start | bytes 786440 | tf_op jit(solution)/shard_map/ppermute | solution.py:86
  42.9 7.5 %collective-permute-start.25 = (bf16[32,4096]{1,0:T(8,128)(2,1)S(1)}, bf16[32,4096]{1,0:T(8,128)(2,1)S(1)}, u32[]{:S(2)}, u32[]{:S(2)}) collective-permute-start(bf16[32,4096]{1,0:T(8,128)(2,1)S(1)} %get-tuple-element.133), channel_id=1, source_target_pairs={{0,1},{1,0},{2,3},{3,2},{4,5},{5,4},{6,7},{7,6},{8,24},{9,25},{10,... | collective-permute-start | bytes 786440 | tf_op jit(solution)/shard_map/ppermute | solution.py:86
  48.2 8.4 %collective-permute-start.23 = (bf16[32,4096]{1,0:T(8,128)(2,1)S(1)}, bf16[32,4096]{1,0:T(8,128)(2,1)S(1)}, u32[]{:S(2)}, u32[]{:S(2)}) collective-permute-start(bf16[32,4096]{1,0:T(8,128)(2,1)S(1)} %get-tuple-element.130), channel_id=1, source_target_pairs={{0,1},{1,0},{2,3},{3,2},{4,5},{5,4},{6,7},{7,6},{8,24},{9,25},{10,... | collective-permute-start | bytes 786440 | tf_op jit(solution)/shard_map/ppermute | solution.py:86
  48.6 11.5 %collective-permute-start.27 = (bf16[16,4096]{1,0:T(8,128)(2,1)S(1)}, bf16[16,4096]{1,0:T(8,128)(2,1)S(1)}, u32[]{:S(2)}, u32[]{:S(2)}) collective-permute-start(bf16[16,4096]{1,0:T(8,128)(2,1)S(1)} %get-tuple-element.138), channel_id=1, source_target_pairs={{0,6},{1,7},{2,4},{3,5},{4,2},{5,3},{6,0},{7,1},{8,14},{9,15},{10,... | collective-permute-start | bytes 393224 | tf_op jit(solution)/shard_map/ppermute | solution.py:86
  50.5 6.8 %collective-permute-start.28 = (bf16[16,4096]{1,0:T(8,128)(2,1)S(1)}, bf16[16,4096]{1,0:T(8,128)(2,1)S(1)}, u32[]{:S(2)}, u32[]{:S(2)}) collective-permute-start(bf16[16,4096]{1,0:T(8,128)(2,1)S(1)} %get-tuple-element.140), channel_id=1, source_target_pairs={{0,16},{1,17},{2,18},{3,19},{4,20},{5,21},{6,22},{7,23},{8,9},{9,8... | collective-permute-start | bytes 393224 | tf_op jit(solution)/shard_map/ppermute | solution.py:86
  56.7 6.4 %collective-permute-start.26 = (bf16[16,4096]{1,0:T(8,128)(2,1)S(1)}, bf16[16,4096]{1,0:T(8,128)(2,1)S(1)}, u32[]{:S(2)}, u32[]{:S(2)}) collective-permute-start(bf16[16,4096]{1,0:T(8,128)(2,1)S(1)} %get-tuple-element.137), channel_id=1, source_target_pairs={{0,16},{1,17},{2,18},{3,19},{4,20},{5,21},{6,22},{7,23},{8,9},{9,8... | collective-permute-start | bytes 393224 | tf_op jit(solution)/shard_map/ppermute | solution.py:86
  56.8 6.5 %collective-permute-start.30 = (bf16[32,4096]{1,0:T(8,128)(2,1)S(1)}, bf16[32,4096]{1,0:T(8,128)(2,1)S(1)}, u32[]{:S(2)}, u32[]{:S(2)}) collective-permute-start(bf16[32,4096]{1,0:T(8,128)(2,1)S(1)} %get-tuple-element.146), channel_id=1, source_target_pairs={{0,8},{1,9},{2,10},{3,11},{4,12},{5,13},{6,14},{7,15},{8,0},{9,1},... | collective-permute-start | bytes 786440 | tf_op jit(solution)/shard_map/ppermute | solution.py:86
  56.8 6.4 %collective-permute-start.31 = (bf16[32,4096]{1,0:T(8,128)(2,1)S(1)}, bf16[32,4096]{1,0:T(8,128)(2,1)S(1)}, u32[]{:S(2)}, u32[]{:S(2)}) collective-permute-start(bf16[32,4096]{1,0:T(8,128)(2,1)S(1)} %get-tuple-element.147), channel_id=1, source_target_pairs={{0,1},{1,0},{2,3},{3,2},{4,5},{5,4},{6,7},{7,6},{8,24},{9,25},{10,... | collective-permute-start | bytes 786440 | tf_op jit(solution)/shard_map/ppermute | solution.py:86
  57.3 9.7 %collective-permute-start.29 = (bf16[16,4096]{1,0:T(8,128)(2,1)S(1)}, bf16[16,4096]{1,0:T(8,128)(2,1)S(1)}, u32[]{:S(2)}, u32[]{:S(2)}) collective-permute-start(bf16[16,4096]{1,0:T(8,128)(2,1)S(1)} %get-tuple-element.144), channel_id=1, source_target_pairs={{0,4},{1,5},{2,6},{3,7},{4,0},{5,1},{6,2},{7,3},{8,12},{9,13},{10,... | collective-permute-start | bytes 393224 | tf_op jit(solution)/shard_map/ppermute | solution.py:86
  63.2 5.3 %collective-permute-start.32 = (bf16[16,4096]{1,0:T(8,128)(2,1)S(1)}, bf16[16,4096]{1,0:T(8,128)(2,1)S(1)}, u32[]{:S(2)}, u32[]{:S(2)}) collective-permute-start(bf16[16,4096]{1,0:T(8,128)(2,1)S(1)} %get-tuple-element.151), channel_id=1, source_target_pairs={{0,2},{1,3},{2,0},{3,1},{4,6},{5,7},{6,4},{7,5},{8,10},{9,11},{10,... | collective-permute-start | bytes 393224 | tf_op jit(solution)/shard_map/ppermute | solution.py:86
  63.4 5.2 %collective-permute-start.33 = (bf16[16,4096]{1,0:T(8,128)(2,1)S(1)}, bf16[16,4096]{1,0:T(8,128)(2,1)S(1)}, u32[]{:S(2)}, u32[]{:S(2)}) collective-permute-start(bf16[16,4096]{1,0:T(8,128)(2,1)S(1)} %get-tuple-element.155), channel_id=1, source_target_pairs={{0,16},{1,17},{2,18},{3,19},{4,20},{5,21},{6,22},{7,23},{8,9},{9,8... | collective-permute-start | bytes 393224 | tf_op jit(solution)/shard_map/ppermute | solution.py:86
